TPU v7x, 512 devices: a whole 4x4x16 slice. The times are simulated.
512 devices in a mesh: attn: 8 (over y, core), expert: 16 (over z), tp: 4 (over x).
Axes of the slice: x: 4, y: 4, z: 16, core: 2. Of those that a mesh axis runs over, the one named last changes fastest.
Arguments:
- query: bfloat16 [2048, 8192], P(('attn', 'expert'), 'tp'), may hold values from -9 to 9
- cached_key_store: bfloat16 [2048, 128, 512], P(('attn', 'expert'), None, 'tp'), may hold values from -5 to 5
- cached_value_store: bfloat16 [2048, 128, 512], P(('attn', 'expert'), None, 'tp'), may hold values from -5 to 5
- token_keys: bfloat16 [2048, 512], P(('attn', 'expert'), 'tp'), may hold values from -5 to 5
- token_values: bfloat16 [2048, 512], P(('attn', 'expert'), 'tp'), may hold values from -5 to 5
- lengths: int32 [2048], P(('attn', 'expert')), may hold values from 2 to 128, as said below
- out_weight: bfloat16 [8192, 2048], P('tp', 'expert'), may hold values from -0.25 to 0.25
- resid: bfloat16 [2048, 2048], P(('attn', 'expert', 'tp')), may hold values from -300 to 300
- norm_gain: float32 [2048], replicated, may hold values from 0.1 to 1.9
- routes: int32 [2048, 8], P(('attn', 'expert')), may hold values from 0 to 127, all different within a row; in each aligned block of 16 rows (0 to 15, 16 to 31, ...) at most 2 rows name the same one
- route_weight: float32 [2048, 8], P(('attn', 'expert')), may hold values from 0.02 to 0.3
- w_gate: bfloat16 [128, 2048, 768], P(('attn', 'expert'), None, 'tp'), may hold values from -0.125 to 0.125
- w_up: bfloat16 [128, 2048, 768], P(('attn', 'expert'), None, 'tp'), may hold values from -0.125 to 0.125
- w_down: bfloat16 [128, 768, 2048], P(('attn', 'expert'), 'tp'), may hold values from -0.4375 to 0.4375
Outputs:
- mixed: bfloat16 [2048, 2048], P(('attn', 'expert', 'tp'))
Inputs may be any that keep to these rules, and one draw needn't show every extreme that they name: `routes`: in each aligned block of 16 rows no expert is named by more than 2 rows, a bound that some block reaches. `lengths`: every aligned block of 16 rows holds a row with exactly 128.
All inputs are finite; a program needn't handle non-finite values.
Results may differ from a plain program's by a relative error of at most 0.012.
Values may be sent and summed in bfloat16 or wider, within the bound.
No kernel may reach another device: no remote copies, remote signals or barrier semaphores. Data moves between devices by JAX's collectives and lax.ppermute only.
A program may use at most 64 MiB of HBM per device.

v0:
```python
import math

import jax
import jax.numpy as jnp
from jax import lax
from jax.sharding import PartitionSpec as P

QUERY_HEADS = 64
KEY_VALUE_HEADS = 4
HEAD_SIZE = 128
CACHE_POSITIONS = 128


def normalize(hidden_state, norm_gain):
    square_mean = jnp.mean(hidden_state * hidden_state, axis=-1, keepdims=True)
    return (hidden_state * lax.rsqrt(square_mean + 1e-06) * norm_gain).astype(jnp.bfloat16)


def shards(
    query,
    cached_key_store,
    cached_value_store,
    token_keys,
    token_values,
    lengths,
    out_weight,
    resid,
    norm_gain,
    routes,
    route_weight,
    w_gate,
    w_up,
    w_down,
):
    row_count = query.shape[0]
    kv_local = cached_key_store.shape[2] // HEAD_SIZE
    query_group_size = QUERY_HEADS // KEY_VALUE_HEADS
    score_scale = 1.0 / math.sqrt(HEAD_SIZE)
    query_rows = query.reshape(row_count, kv_local, query_group_size, HEAD_SIZE)
    key_row_list = cached_key_store.reshape(row_count, CACHE_POSITIONS, kv_local, HEAD_SIZE)
    value_row_list = cached_value_store.reshape(row_count, CACHE_POSITIONS, kv_local, HEAD_SIZE)
    incoming_key = token_keys.reshape(row_count, kv_local, HEAD_SIZE)
    incoming_value = token_values.reshape(row_count, kv_local, HEAD_SIZE)
    scores = (
        jnp.einsum("rkgd,rjkd->rkgj", query_rows, key_row_list, preferred_element_type=jnp.float32)
        * score_scale
    )
    fresh_score = (
        jnp.einsum("rkgd,rkd->rkg", query_rows, incoming_key, preferred_element_type=jnp.float32)
        * score_scale
    )
    valid = (jnp.arange(CACHE_POSITIONS, dtype=jnp.int32)[None, :] < lengths[:, None])[
        :, None, None, :
    ]
    masked = jnp.where(valid, scores, -jnp.inf)
    row_max = jnp.maximum(jnp.max(masked, axis=-1), fresh_score)
    expo = jnp.where(valid, jnp.exp(masked - row_max[..., None]), 0.0)
    fresh_expo = jnp.exp(fresh_score - row_max)
    denominator = jnp.sum(expo, axis=-1) + fresh_expo
    weights_cache = (expo / denominator[..., None]).astype(jnp.bfloat16)
    weights_fresh = (fresh_expo / denominator).astype(jnp.bfloat16)
    attn_mixed = jnp.einsum(
        "rkgj,rjkd->rkgd", weights_cache, value_row_list, preferred_element_type=jnp.float32
    )
    attn_mixed = (
        attn_mixed
        + weights_fresh.astype(jnp.float32)[..., None]
        * incoming_value.astype(jnp.float32)[:, :, None, :]
    )
    attended = attn_mixed.reshape(row_count, -1).astype(jnp.bfloat16)
    partial_value = jnp.dot(
        lax.all_gather(attended, "expert", axis=0, tiled=True),
        out_weight,
        preferred_element_type=jnp.float32,
    )
    expert_count = lax.axis_size("expert")
    partial_value = lax.all_to_all(
        partial_value.reshape(expert_count, row_count, -1),
        "expert",
        split_axis=0,
        concat_axis=2,
        tiled=True,
    ).reshape(row_count, -1)
    share_rows = row_count // lax.axis_size("tp")
    offset = lax.axis_index("tp") * share_rows
    placed = lax.dynamic_update_slice_in_dim(
        jnp.zeros_like(partial_value), resid.astype(jnp.float32), offset, 0
    )
    partial_value = partial_value + placed
    hidden_all = lax.psum(partial_value, "tp")
    normed_all = normalize(hidden_all, norm_gain)
    hidden_own = lax.dynamic_slice_in_dim(hidden_all, offset, share_rows, 0)
    attn_count = lax.axis_size("attn")
    expert_total = attn_count * expert_count
    top_count = routes.shape[1]
    capacity = min(row_count, max(2, 2 * top_count * row_count // expert_total))
    pick_ids = routes.reshape(-1)
    hot_table = (pick_ids[:, None] == jnp.arange(expert_total, dtype=jnp.int32)[None, :]).astype(
        jnp.int32
    )
    before = jnp.cumsum(hot_table, axis=0) - hot_table
    slot_rank = jnp.sum(before * hot_table, axis=1)
    slot_index = pick_ids * capacity + slot_rank
    slot_ids = jnp.arange(expert_total * capacity, dtype=jnp.int32)
    selected = slot_ids[:, None, None] == slot_index.reshape(row_count, top_count)[None, :, :]
    dispatch_matrix = jnp.any(selected, axis=-1).astype(jnp.bfloat16)
    outgoing = jnp.dot(dispatch_matrix, normed_all, preferred_element_type=jnp.float32).astype(
        jnp.bfloat16
    )
    outgoing = outgoing.reshape(expert_total, capacity, -1)
    incoming = lax.all_to_all(outgoing, ("attn", "expert"), split_axis=0, concat_axis=0, tiled=True)
    tokens_in = incoming.reshape(expert_total * capacity, -1)
    gate_value = jnp.dot(tokens_in, w_gate[0], preferred_element_type=jnp.float32)
    up_value = jnp.dot(tokens_in, w_up[0], preferred_element_type=jnp.float32)
    activated = (jax.nn.silu(gate_value) * up_value).astype(jnp.bfloat16)
    down_value = jnp.dot(activated, w_down[0], preferred_element_type=jnp.float32)
    produced = down_value.astype(jnp.bfloat16)
    returned_rows = lax.all_to_all(
        produced.reshape(expert_total, capacity, -1),
        ("attn", "expert"),
        split_axis=0,
        concat_axis=0,
        tiled=True,
    )
    returned_flat = returned_rows.reshape(expert_total * capacity, -1)
    picked = (
        jnp.take(returned_flat, slot_index, axis=0)
        .astype(jnp.float32)
        .reshape(row_count, top_count, -1)
    )
    weighted = jnp.sum(picked * route_weight[:, :, None], axis=1)
    expert_sum = lax.psum_scatter(
        weighted.astype(jnp.bfloat16), "tp", scatter_dimension=0, tiled=True
    ).astype(jnp.float32)
    return (hidden_own + expert_sum).astype(jnp.bfloat16)


def solution(mesh):
    in_specs = (
        P(("attn", "expert"), "tp"),
        P(("attn", "expert"), None, "tp"),
        P(("attn", "expert"), None, "tp"),
        P(("attn", "expert"), "tp"),
        P(("attn", "expert"), "tp"),
        P(("attn", "expert")),
        P("tp", "expert"),
        P(("attn", "expert", "tp"), None),
        P(),
        P(("attn", "expert"), None),
        P(("attn", "expert"), None),
        P(("attn", "expert"), None, "tp"),
        P(("attn", "expert"), None, "tp"),
        P(("attn", "expert"), "tp", None),
    )
    out_specs = P(("attn", "expert", "tp"), None)
    return jax.shard_map(shards, mesh=mesh, in_specs=in_specs, out_specs=out_specs, check_vma=False)
```

profile of v0, /device:TPU:24, one launch (start us, length us, event | category | flops | bytes accessed | tf_op | source)
XLA Modules:
  0.0 363.3 jit_solution(1592609433649051584)
XLA Ops:
  6.5 0.8 iota_compare_fusion.2
  7.4 0.9 copy.33
  8.2 0.8 fusion.23
  9.1 1.6 fusion.32
  10.6 0.2 fusion.14
  10.9 0.3 fusion.2
  11.2 0.6 copy.41
  11.9 75.4 %all-gather.2.cloned.1.call-done = bf16[256,2048]{1,0:T(8,128)(2,1)} async-done(((bf16[16,2048]{1,0:T(8,128)(2,1)}), bf16[256,2048]{1,0:T(8,128)(2,1)}) %all-gather.2.cloned.1.call-update) | async-done | bytes 1048592 | tf_op jit(solution)/shard_map/all_gather | solution.py:72
  87.3 2.3 fusion.33
  89.6 8.1 %all-to-all-start = ((f32[16,16,128]{2,1,0:T(8,128)}), f32[16,16,128]{2,1,0:T(8,128)S(1)}, u32[]{:S(2)}, u32[]{:S(2)}) async-start(f32[16,16,128]{2,1,0:T(8,128)} %bitcast.3), calls=%async_computation | async-start | bytes 262144 | tf_op jit(solution)/shard_map/all_to_all | solution.py:77
  98.0 0.2 reduce_window_sum.11
  98.1 0.2 select_reduce_fusion
  98.4 12.4 %all-to-all-done = f32[16,16,128]{2,1,0:T(8,128)S(1)} async-done(((f32[16,16,128]{2,1,0:T(8,128)}), f32[16,16,128]{2,1,0:T(8,128)S(1)}, u32[]{:S(2)}, u32[]{:S(2)}) %all-to-all-start) | async-done | bytes 131104 | tf_op jit(solution)/shard_map/all_to_all | solution.py:77
  110.9 0.6 copy-done.2
  111.6 0.1 fusion.13
  111.7 49.6 %all-reduce.4.cloned.1.call-done = f32[16,2048]{1,0:T(8,128)} async-done(((f32[16,2048]{1,0:T(8,128)}), f32[16,2048]{1,0:T(8,128)}) %all-reduce.4.cloned.1.call-update) | async-done | bytes 131088 | tf_op jit(solution)/shard_map/psum | solution.py:90
  161.3 1.0 multiply_reduce_fusion.1
  162.3 1.4 convolution_convert_fusion
  163.7 0.7 reshape.172
  164.4 68.5 %all_to_all.25 = bf16[128,2,2048]{2,1,0:T(2,128)(2,1)} all-to-all(bf16[128,2,2048]{2,1,0:T(2,128)(2,1)S(1)} %reshape.172), channel_id=1, replica_groups=mesh['attn'=8,'expert'=16,'tp'=4] {'attn','expert'}, dimensions={0} | all-to-all | bytes 2097152 | tf_op jit(solution)/shard_map/all_to_all | solution.py:111
  232.9 1.5 reshape.173
  234.5 0.5 fusion.6
  235.0 2.6 convolution_convert_fusion.1
  237.6 1.5 reshape.174
  239.1 11.0 %all-to-all-start.2 = ((bf16[128,2,2048]{2,1,0:T(2,128)(2,1)}), bf16[128,2,2048]{2,1,0:T(2,128)(2,1)S(1)}, u32[]{:S(2)}, u32[]{:S(2)}) async-start(bf16[128,2,2048]{2,1,0:T(2,128)(2,1)} %reshape.174), calls=%async_computation.2 | async-start | bytes 2097152 | tf_op jit(solution)/shard_map/all_to_all | solution.py:118
  250.3 51.3 %all-to-all-done.2 = bf16[128,2,2048]{2,1,0:T(2,128)(2,1)S(1)} async-done(((bf16[128,2,2048]{2,1,0:T(2,128)(2,1)}), bf16[128,2,2048]{2,1,0:T(2,128)(2,1)S(1)}, u32[]{:S(2)}, u32[]{:S(2)}) %all-to-all-start.2) | async-done | bytes 1048608 | tf_op jit(solution)/shard_map/all_to_all | solution.py:118
  301.6 0.4 reshape.175
  302.1 0.9 gather_fusion
  303.0 1.6 multiply_reduce_fusion
  304.6 1.3 dynamic-slice.1
  306.5 48.8 %all-reduce.6.cloned.1.call-done = bf16[16,2048]{1,0:T(8,128)(2,1)} async-done(((bf16[16,2048]{1,0:T(8,128)(2,1)}), bf16[16,2048]{1,0:T(8,128)(2,1)}) %all-reduce.6.cloned.1.call-update) | async-done | bytes 65552
  355.3 1.5 add_convert_fusion
  (42 shorter events, 0.8 us)
Async XLA Ops:
  6.5 228.4 %copy-start = (bf16[1,192,2048]{2,1,0:T(8,128)(2,1)S(1)}, bf16[1,192,2048]{2,1,0:T(8,128)(2,1)}, u32[]{:S(2)}) copy-start(bf16[1,192,2048]{2,1,0:T(8,128)(2,1)} %param.27) | copy-start | bytes 2359300
  6.5 4.3 %copy-start.6 = (bf16[16,128]{1,0:T(8,128)(2,1)S(1)}, bf16[16,128]{1,0:T(8,128)(2,1)}, u32[]{:S(2)}) copy-start(bf16[16,128]{1,0:T(8,128)(2,1)} %param.18) | copy-start | bytes 12292
  6.5 4.4 %copy-start.9 = (bf16[16,128,128]{2,1,0:T(8,128)(2,1)S(1)}, bf16[16,128,128]{2,1,0:T(8,128)(2,1)}, u32[]{:S(2)}) copy-start(bf16[16,128,128]{2,1,0:T(8,128)(2,1)} %param.16) | copy-start | bytes 1572868
  6.5 80.7 %all-gather.2.cloned.1.call-start = ((), (), s32[]{:S(2)}) async-start(), calls=%async_computation.3 | async-start | bytes 1114112 | tf_op jit(solution)/shard_map/all_gather | solution.py:72
  9.1 78.2 %copy-start.3 = (bf16[2048,128]{1,0:T(8,128)(2,1)S(1)}, bf16[2048,128]{1,0:T(8,128)(2,1)}, u32[]{:S(2)}) copy-start(bf16[2048,128]{1,0:T(8,128)(2,1)} %param.20) | copy-start | bytes 1572868
  11.9 85.8 %copy-start.7 = (s32[16,8]{0,1:T(8,128)S(1)}, s32[16,8]{0,1:T(8,128)}, u32[]{:S(2)}) copy-start(s32[16,8]{0,1:T(8,128)} %param.23) | copy-start | bytes 1540
  11.9 98.9 %copy-start.4 = (bf16[4,2048]{1,0:T(4,128)(2,1)S(1)}, bf16[4,2048]{1,0:T(4,128)(2,1)}, u32[]{:S(2)}) copy-start(bf16[4,2048]{1,0:T(4,128)(2,1)} %param.21) | copy-start | bytes 49156
  89.6 72.7 %copy-start.5 = (f32[2048]{0:T(1024)S(1)}, f32[2048]{0:T(1024)}, u32[]{:S(2)}) copy-start(f32[2048]{0:T(1024)} %param.22) | copy-start | bytes 24580
  89.6 21.2 %all-to-all-start = ((f32[16,16,128]{2,1,0:T(8,128)}), f32[16,16,128]{2,1,0:T(8,128)S(1)}, u32[]{:S(2)}, u32[]{:S(2)}) async-start(f32[16,16,128]{2,1,0:T(8,128)} %bitcast.3), calls=%async_computation | async-start | bytes 262144 | tf_op jit(solution)/shard_map/all_to_all | solution.py:77
  97.6 63.6 %all-reduce.4.cloned.1.call-start = ((), (), s32[]{:S(2)}) async-start(), calls=%async_computation.4 | async-start | bytes 262144 | tf_op jit(solution)/shard_map/psum | solution.py:90
  110.9 0.6 copy-start.2
  232.9 1.5 copy-start.1
  239.1 11.1 %copy-start.8 = (f32[16,8]{0,1:T(8,128)S(1)}, f32[16,8]{0,1:T(8,128)}, u32[]{:S(2)}) copy-start(f32[16,8]{0,1:T(8,128)} %param.24) | copy-start | bytes 1540
  239.1 62.5 %all-to-all-start.2 = ((bf16[128,2,2048]{2,1,0:T(2,128)(2,1)}), bf16[128,2,2048]{2,1,0:T(2,128)(2,1)S(1)}, u32[]{:S(2)}, u32[]{:S(2)}) async-start(bf16[128,2,2048]{2,1,0:T(2,128)(2,1)} %reshape.174), calls=%async_computation.2 | async-start | bytes 2097152 | tf_op jit(solution)/shard_map/all_to_all | solution.py:118
  250.1 105.2 %all-reduce.6.cloned.1.call-start = ((), (), s32[]{:S(2)}) async-start(), calls=%async_computation.5 | async-start | bytes 131072
Sparse Core Ops, SparseCore 0:
  12.0 75.2 all-gather.1
  111.7 49.5 all-reduce.3
  304.7 50.5 all-reduce.5
where the time goes:
time: 364 us; the launch traced here: 363 us
  waiting for transfers between devices  237 us (65%)
  blocking collectives  68.5 us (19%)
  starting transfers between devices  19.1 us (5%)
  between operations  14 us (4%)
  matrix products  9.46 us (3%)
  local copies, waits for them, and re-layouts  9.04 us (2%)
  other arithmetic  5.74 us (2%)
    all_gather x1, waiting for transfers between devices, shards(): lax.all_gather(attended, 'expert', axis=0, tiled=True)  75.4 us
    all_to_all x1, blocking collectives, shards(): lax.all_to_all(outgoing, ('attn', 'expert'), split_axis=0, concat_axis=0,...  68.5 us
    all_to_all x1, waiting for transfers between devices, shards(): lax.all_to_all(produced.reshape(expert_total, capacity, -1), ('attn', 'ex...  51.3 us
    psum x1, waiting for transfers between devices, shards(): hidden_all = lax.psum(partial_value, 'tp')  49.6 us
    unnamed x4, waiting for transfers between devices  48.8 us
    all_to_all x1, waiting for transfers between devices, shards(): lax.all_to_all(partial_value.reshape(expert_count, row_count, -1), 'exper...  12.4 us
    all_to_all x1, starting transfers between devices, shards(): lax.all_to_all(produced.reshape(expert_total, capacity, -1), ('attn', 'ex...  11 us
    all_to_all x1, starting transfers between devices, shards(): lax.all_to_all(partial_value.reshape(expert_count, row_count, -1), 'exper...  8.06 us
  transfers between devices with their start and end apart: 5, of which 5 were waited for; matrix products, arithmetic and copies ran while one was open for 1% of the time, Pallas kernels for 0%

commit v1 on v0

v1 whole, which is shorter than its diff:
```python
import math

import jax
import jax.numpy as jnp
from jax import lax
from jax.experimental import pallas as pl
from jax.experimental.pallas import tpu as pltpu
from jax.sharding import Mesh
from jax.sharding import PartitionSpec as P

HEADS = 16
HEAD_SIZE = 128
POSITIONS = 128
ROWS = 16
ATTN = 8
Z_HI = 4
Z_LO = 4
EXPERT = Z_HI * Z_LO
TP = 4
D = 2048
LANES = 128
QUARTER = D // TP
SLOTS = 32
FF = 192
TOPK = 8
BF16 = jnp.bfloat16
F32 = jnp.float32

VMEM = pl.BlockSpec(memory_space=pltpu.VMEM)
SMEM = pl.BlockSpec(memory_space=pltpu.SMEM)
PARAMS = pltpu.CompilerParams(vmem_limit_bytes=40 * 1024 * 1024)


def call(kernel, outs, in_specs, scratch=()):
    shapes = [jax.ShapeDtypeStruct(s, d) for s, d in outs]
    single = len(shapes) == 1
    return pl.pallas_call(
        kernel,
        out_shape=shapes[0] if single else shapes,
        in_specs=in_specs,
        out_specs=VMEM if single else [VMEM] * len(shapes),
        scratch_shapes=list(scratch),
        compiler_params=PARAMS,
    )


def attention_kernel(place, lengths, query, keys, values, new_keys, new_values, resid, meta, out, q_rows, a_rows, extra):
    for h in range(HEADS):
        q_rows[:, h, :] = query[:, h * HEAD_SIZE : (h + 1) * HEAD_SIZE].astype(F32)
    scale = 1.0 / math.sqrt(HEAD_SIZE)
    position = lax.broadcasted_iota(jnp.int32, (HEADS, POSITIONS), 1)
    new_k = new_keys[...].astype(F32)
    new_v = new_values[...].astype(F32)
    for r in range(ROWS):
        q = q_rows[r]
        scores = lax.dot_general(
            q.astype(BF16), keys[r], (((1,), (1,)), ((), ())), preferred_element_type=F32
        ) * scale
        fresh = jnp.sum(q * new_k[r : r + 1, :], axis=1, keepdims=True) * scale
        valid = position < lengths[r]
        top = jnp.maximum(jnp.max(jnp.where(valid, scores, -jnp.inf), axis=1, keepdims=True), fresh)
        expo = jnp.where(valid, jnp.exp(scores - top), 0.0)
        fresh_expo = jnp.exp(fresh - top)
        total = jnp.sum(expo, axis=1, keepdims=True) + fresh_expo
        weights = (expo / total).astype(BF16)
        fresh_weight = (fresh_expo / total).astype(BF16).astype(F32)
        mixed = jnp.dot(weights, values[r], preferred_element_type=F32)
        a_rows[:, r, :] = mixed + fresh_weight * new_v[r : r + 1, :]
    tp = place[2]
    extra[...] = jnp.zeros_like(extra)
    for e in range(EXPERT):
        extra[e, pl.ds(tp * 4, 4), :] = resid[:, e * LANES : (e + 1) * LANES].astype(F32)
        extra[e, pl.ds(lax.rem(tp + 1, 4) * 4, 4), :] = meta[...]
    for lo in range(Z_LO):
        heads = a_rows[4 * lo : 4 * lo + 4].astype(BF16).reshape(4 * ROWS, HEAD_SIZE)
        for hi in range(Z_HI):
            out[hi * Z_LO + lo, 0 : 4 * ROWS, :] = heads
    out[:, 4 * ROWS : 5 * ROWS, :] = extra[...].astype(BF16)


def project_kernel(place, gathered, weight, out):
    heads = [gathered[:, h * ROWS : (h + 1) * ROWS, :].reshape(EXPERT * ROWS, HEAD_SIZE) for h in range(4)]
    rows = jnp.concatenate(heads, axis=1)
    lo, tp = place[1], place[2]
    extra = gathered[:, 4 * ROWS : 5 * ROWS, :].astype(F32)
    line = lax.broadcasted_iota(jnp.int32, extra.shape, 1)
    resid = jnp.where((line >= tp * 4) & (line < tp * 4 + 4), extra, 0.0).reshape(EXPERT * ROWS, LANES)
    for j in range(TP):
        part = jnp.dot(rows, weight[j], preferred_element_type=F32)
        part = part + jnp.where(lo == j, resid, 0.0)
        part = part.astype(BF16)
        for i in range(Z_LO):
            out[i * TP + j] = part[i * 64 : (i + 1) * 64, :]


def reduce_kernel(parts, out):
    total = parts[0].astype(F32)
    for i in range(1, Z_LO * TP):
        total = total + parts[i].astype(F32)
    total = total.astype(BF16)
    for i in range(EXPERT):
        out[i] = total


def select_kernel(place, gathered, hidden, out, combine):
    tp = place[2]
    mine = place[0] * Z_LO + place[1]
    extra = gathered[:, 4 * ROWS : 5 * ROWS, :].astype(F32)
    line = lax.broadcasted_iota(jnp.int32, extra.shape, 1)
    base = lax.rem(tp + 1, 4) * 4
    route = jnp.sum(jnp.where(line == base, extra, 0.0), axis=1)
    high = jnp.sum(jnp.where(line == base + 1, extra, 0.0), axis=1)
    low = jnp.sum(jnp.where(line == base + 2, extra, 0.0), axis=1)
    pick_row = lax.broadcasted_iota(jnp.int32, (LANES, EXPERT * ROWS), 0) // TOPK
    row = lax.rem(lax.broadcasted_iota(jnp.int32, (LANES, EXPERT * ROWS), 1), ROWS)
    here = jnp.where(pick_row == row, 1.0, 0.0).astype(BF16)
    earlier = jnp.where(pick_row < row, 1.0, 0.0).astype(BF16)
    hits = [jnp.where(route == (a * EXPERT + mine).astype(F32), 1.0, 0.0) for a in range(ATTN)]
    hit = jnp.concatenate(hits, axis=0)
    hit_high = jnp.concatenate([m * high for m in hits], axis=0)
    hit_low = jnp.concatenate([m * low for m in hits], axis=0)
    shape = (ATTN * EXPERT, EXPERT * ROWS)
    own = lax.rem(lax.broadcasted_iota(jnp.int32, shape, 0), EXPERT) == (
        lax.broadcasted_iota(jnp.int32, shape, 1) // ROWS
    )
    dot = lambda a, b: jnp.dot(a.astype(BF16), b, preferred_element_type=F32)
    named = jnp.where(own, dot(hit, here), 0.0)
    rank = dot(hit, earlier)
    weight_high = dot(hit_high, here)
    weight_low = dot(hit_low, here)
    chosen = [jnp.where(rank == s, named, 0.0) for s in (0.0, 1.0)]

    def laid(pair):
        return jnp.concatenate(
            [pair[s][a * EXPERT : (a + 1) * EXPERT, :] for a in range(ATTN) for s in range(2)], axis=0
        )

    choice = laid(chosen).astype(BF16)
    combine[0] = jnp.transpose(laid([c * weight_high for c in chosen])).astype(BF16)
    combine[1] = jnp.transpose(laid([c * weight_low for c in chosen])).astype(BF16)
    for hi in range(Z_HI):
        block = hidden[hi * Z_LO : (hi + 1) * Z_LO].reshape(EXPERT * ROWS, LANES)
        sent = jnp.dot(choice, block, preferred_element_type=F32).astype(BF16)
        sent = sent.reshape(ATTN, SLOTS, LANES)
        for t in range(TP):
            out[:, t, :, hi * LANES : (hi + 1) * LANES] = sent


def expert_kernel(tokens, gain, w_gate, w_up, w_down, out, x, normed):
    slots = ATTN * SLOTS
    square = jnp.zeros((slots, LANES), F32)
    for hi in range(Z_HI):
        for t in range(TP):
            c = hi * TP + t
            block = tokens[:, t, :, hi * LANES : (hi + 1) * LANES].reshape(slots, LANES).astype(F32)
            x[:, c * LANES : (c + 1) * LANES] = block
            square = square + block * block
    factor = lax.rsqrt(jnp.sum(square, axis=1, keepdims=True) * (1.0 / D) + 1e-06)
    normed[...] = (x[...] * factor * gain[...]).astype(BF16)
    gate = jnp.dot(normed[...], w_gate[...], preferred_element_type=F32)
    up = jnp.dot(normed[...], w_up[...], preferred_element_type=F32)
    activated = (gate / (1.0 + jnp.exp(-gate)) * up).astype(BF16)
    for hi in range(Z_HI):
        for t in range(TP):
            c = hi * TP + t
            part = jnp.dot(activated, w_down[:, c * LANES : (c + 1) * LANES], preferred_element_type=F32)
            out[:, t, :, hi * LANES : (hi + 1) * LANES] = part.astype(BF16).reshape(ATTN, SLOTS, LANES)


def combine_kernel(parts, combine, out):
    total = jnp.zeros((EXPERT * ROWS, QUARTER), F32)
    for t in range(TP):
        block = parts[:, t].reshape(ATTN * SLOTS, QUARTER)
        total = total + jnp.dot(combine[0], block, preferred_element_type=F32)
        total = total + jnp.dot(combine[1], block, preferred_element_type=F32)
    out[...] = total.astype(BF16).reshape(EXPERT, ROWS, QUARTER)


def exchange(x, axes):
    return lax.all_to_all(x, axes, split_axis=0, concat_axis=0, tiled=True)


def shards(
    query,
    cached_key_store,
    cached_value_store,
    token_keys,
    token_values,
    lengths,
    out_weight,
    resid,
    norm_gain,
    routes,
    route_weight,
    w_gate,
    w_up,
    w_down,
):
    z = ("zhi", "zlo")
    z_hi, z_lo, tp = (lax.axis_index(n) for n in ("zhi", "zlo", "tp"))
    place = jnp.stack([z_hi, z_lo, tp]).astype(jnp.int32)
    high = route_weight.astype(BF16).astype(F32)
    meta = jnp.stack(
        [v.reshape(LANES) for v in (routes.astype(F32), high, route_weight - high, jnp.zeros_like(high))]
    )
    weight = exchange(out_weight.reshape(Z_LO, D // Z_LO, LANES), "zlo")
    sent = call(
        attention_kernel,
        [((EXPERT, 5 * ROWS, LANES), BF16)],
        [SMEM, SMEM] + [VMEM] * 7,
        [
            pltpu.VMEM((ROWS, HEADS, HEAD_SIZE), F32),
            pltpu.VMEM((HEADS, ROWS, HEAD_SIZE), F32),
            pltpu.VMEM((EXPERT, ROWS, LANES), F32),
        ],
    )(place, lengths, query, cached_key_store, cached_value_store, token_keys, token_values, resid, meta)
    gathered = exchange(sent, z)
    parts = call(project_kernel, [((Z_LO * TP, 64, LANES), BF16)], [SMEM, VMEM, VMEM])(place, gathered, weight)
    parts = exchange(parts, ("zlo", "tp"))
    own = call(reduce_kernel, [((EXPERT, 64, LANES), BF16)], [VMEM])(parts)
    hidden = exchange(own, z)
    outgoing, combine = call(
        select_kernel,
        [((ATTN, TP, SLOTS, QUARTER), BF16), ((2, EXPERT * ROWS, ATTN * SLOTS), BF16)],
        [SMEM, VMEM, VMEM],
    )(place, gathered, hidden)
    incoming = exchange(outgoing.reshape(ATTN * TP, SLOTS, QUARTER), ("attn", "tp"))
    produced = call(
        expert_kernel,
        [((ATTN, TP, SLOTS, QUARTER), BF16)],
        [VMEM] * 5,
        [pltpu.VMEM((ATTN * SLOTS, D), F32), pltpu.VMEM((ATTN * SLOTS, D), BF16)],
    )(incoming.reshape(ATTN, TP, SLOTS, QUARTER), norm_gain.reshape(1, D), w_gate[0], w_up[0], w_down[0])
    returned = exchange(produced.reshape(ATTN * TP, SLOTS, QUARTER), ("attn", "tp"))
    weighted = call(combine_kernel, [((EXPERT, ROWS, QUARTER), BF16)], [VMEM, VMEM])(
        returned.reshape(ATTN, TP, SLOTS, QUARTER), combine
    )
    back = exchange(weighted, z)
    own_hidden = lax.dynamic_slice_in_dim(
        hidden.reshape(Z_HI, EXPERT, ROWS, LANES), z_hi * Z_LO + z_lo, 1, axis=1
    )[:, 0]
    own_hidden = own_hidden.transpose(1, 0, 2).reshape(ROWS, QUARTER).astype(F32)
    mixed = (jnp.sum(back.astype(F32), axis=0) + own_hidden).astype(BF16)
    mine = exchange(mixed.reshape(TP, ROWS // TP, QUARTER), "tp")
    return mine.reshape(TP, ROWS // TP, Z_HI, LANES).transpose(1, 2, 0, 3).reshape(ROWS // TP, D)


def solution(mesh):
    fine = Mesh(mesh.devices.reshape(ATTN, Z_HI, Z_LO, TP), ("attn", "zhi", "zlo", "tp"))
    rows = ("attn", "zhi", "zlo")
    in_specs = (
        P(rows, "tp"),
        P(rows, None, "tp"),
        P(rows, None, "tp"),
        P(rows, "tp"),
        P(rows, "tp"),
        P(rows),
        P("tp", ("zhi", "zlo")),
        P((*rows, "tp"), None),
        P(),
        P(rows, None),
        P(rows, None),
        P(rows, None, "tp"),
        P(rows, None, "tp"),
        P(rows, "tp", None),
    )
    out_specs = P((*rows, "tp"), None)
    return jax.shard_map(shards, mesh=fine, in_specs=in_specs, out_specs=out_specs, check_vma=False)
```

time: 364 us -> 188 us (0.52)
  waiting for transfers between devices: 237 us -> 31.7 us
  blocking collectives: 68.5 us -> 121 us
  between operations: 14 us -> 0.17 us
  Pallas kernels: 0 us -> 11.8 us
  matrix products: 9.46 us -> 0 us
  starting transfers between devices: 19.1 us -> 11.3 us
  other arithmetic: 5.74 us -> 1.7 us
    all_gather x1 -> x0, waiting for transfers between devices: 75.4 us -> none  [shards(): lax.all_gather(attended, 'expert', axis=0, tiled=True)]
    all_to_all x1 -> x6, blocking collectives: 68.5 us -> 121 us  [exchange(): return lax.all_to_all(x, axes, split_axis=0, concat_axis=0, tiled=True)]
    psum x1 -> x0, waiting for transfers between devices: 49.6 us -> none  [shards(): hidden_all = lax.psum(partial_value, 'tp')]
    unnamed x4 -> x0, waiting for transfers between devices: 48.8 us -> none
    all_to_all x2, waiting for transfers between devices: 63.7 us -> 31.7 us  [exchange(): return lax.all_to_all(x, axes, split_axis=0, concat_axis=0, tiled=True)]
    pallas_call x0 -> x6, Pallas kernels: none -> 11.8 us  [the longest x1 5.78 us: shards(): call(attention_kernel, [((EXPERT, 5 * ROWS, LANES), BF16)], [SMEM, SMEM]...]
    dot_general x7 -> x0, matrix products: 9.46 us -> none  [the longest x1 2.57 us: shards(): jnp.dot(activated, w_down[0], preferred_element_type=jnp.float32)]
    all_to_all x2, starting transfers between devices: 19 us -> 11.3 us  [exchange(): return lax.all_to_all(x, axes, split_axis=0, concat_axis=0, tiled=True)]
  transfers between devices with their start and end apart: 5 -> 2, of which waited for: 5 -> 2; matrix products, arithmetic and copies ran while one was open for 1% -> 1% of each run, Pallas kernels for 0% -> 0%
where the time goes in v1:
time: 188 us; the launch traced here: 185 us
  blocking collectives  121 us (64%)
  waiting for transfers between devices  31.7 us (17%)
  Pallas kernels  11.8 us (6%)
  starting transfers between devices  11.3 us (6%)
  local copies, waits for them, and re-layouts  7.75 us (4%)
    all_to_all x6, blocking collectives, exchange(): return lax.all_to_all(x, axes, split_axis=0, concat_axis=0, tiled=True)  121 us
    all_to_all x2, waiting for transfers between devices, exchange(): return lax.all_to_all(x, axes, split_axis=0, concat_axis=0, tiled=True)  31.7 us
    all_to_all x2, starting transfers between devices, exchange(): return lax.all_to_all(x, axes, split_axis=0, concat_axis=0, tiled=True)  11.3 us
    unnamed x29, local copies, waits for them, and re-layouts  6.52 us
    pallas_call x1, Pallas kernels, shards(): call(attention_kernel, [((EXPERT, 5 * ROWS, LANES), BF16)], [SMEM, SMEM]...  5.78 us
  transfers between devices with their start and end apart: 2, of which 2 were waited for; matrix products, arithmetic and copies ran while one was open for 1% of the time, Pallas kernels for 0%

profile of v1, /device:TPU:24, one launch (start us, length us, event | category | flops | bytes accessed | tf_op | source)
XLA Modules:
  0.0 185.5 jit_solution(9246865083384417320)
XLA Ops:
  0.0 0.7 convert_element_type.29
  0.7 0.1 copy.26
  0.8 0.1 stack_reshape.12
  0.9 0.8 convert_convert_fusion
  1.7 0.1 stack_reshape.13
  1.9 0.1 stack_reshape.14
  2.0 0.1 pad.3.clone
  2.1 0.1 pad_add_fusion.place
  2.2 0.3 copy-done.6
  2.5 0.2 copy-done.9
  2.8 1.0 copy-done.1
  3.9 1.0 copy-done.2
  4.9 5.8 %shard_map.136 = bf16[16,80,128]{2,1,0:T(8,128)(2,1)S(1)} custom-call(s32[3]{0:T(128)S(1)} %pad_add_fusion.place, s32[16]{0:T(128)S(1)} %copy-done.10, bf16[16,2048]{1,0:T(8,128)(2,1)S(1)} %copy-done.5, bf16[16,128,128]{2,1,0:T(8,128)(2,1)S(1)} %copy-done.1, bf16[16,128,128]{2,1,0:T(8,128)(2,1)S(1)} %copy-done.2, bf16[16,128]{1,0:T(8,128)(2,1)S(1)} %copy-done.8, ...), custom_call_target="tpu_custom_call" | custom-call | tf_op jit(solution)/shard_map/pallas_call | solution.py:207
  10.7 35.9 %all_to_all.40.gathered = bf16[16,80,128]{2,1,0:T(8,128)(2,1)S(1)} all-to-all(bf16[16,80,128]{2,1,0:T(8,128)(2,1)S(1)} %shard_map.136), channel_id=1, replica_groups=mesh['attn'=8,'zhi'=4,'zlo'=4,'tp'=4] {'zhi','zlo'}, dimensions={0} | all-to-all | bytes 655360 | tf_op jit(solution)/shard_map/all_to_all | solution.py:180
  46.6 17.2 %all_to_all.41.weight = bf16[4,512,128]{2,1,0:T(8,128)(2,1)S(1)} all-to-all(bf16[4,512,128]{2,1,0:T(8,128)(2,1)S(1)} %bitcast.31), channel_id=1, replica_groups=mesh['attn'=8,'zhi'=4,'zlo'=4,'tp'=4] {'zlo'}, dimensions={0} | all-to-all | bytes 1048576 | tf_op jit(solution)/shard_map/all_to_all | solution.py:180
  63.8 1.0 shard_map.137
  64.8 15.1 %all_to_all.42.parts = bf16[16,64,128]{2,1,0:T(8,128)(2,1)S(1)} all-to-all(bf16[16,64,128]{2,1,0:T(8,128)(2,1)S(1)} %shard_map.137), channel_id=1, replica_groups=mesh['attn'=8,'zhi'=4,'zlo'=4,'tp'=4] {'zlo','tp'}, dimensions={0} | all-to-all | bytes 524288 | tf_op jit(solution)/shard_map/all_to_all | solution.py:180
  79.9 23.9 %all_to_all.43.hidden = bf16[16,64,128]{2,1,0:T(8,128)(2,1)S(1)} all-to-all(bf16[16,64,128]{2,1,0:T(8,128)(2,1)S(1)} %shard_map.138), channel_id=1, replica_groups=mesh['attn'=8,'zhi'=4,'zlo'=4,'tp'=4] {'zhi','zlo'}, dimensions={0} | all-to-all | bytes 524288 | tf_op jit(solution)/shard_map/all_to_all | solution.py:180
  103.8 2.1 %shard_map.139 = (bf16[8,4,32,512]{3,2,1,0:T(8,128)(2,1)}, bf16[2,256,256]{2,1,0:T(8,128)(2,1)S(1)}) custom-call(s32[3]{0:T(128)S(1)} %pad_add_fusion.place, bf16[16,80,128]{2,1,0:T(8,128)(2,1)S(1)} %all_to_all.40.gathered, bf16[16,64,128]{2,1,0:T(8,128)(2,1)S(1)} %all_to_all.43.hidden), custom_call_target="tpu_custom_call" | custom-call | tf_op jit(solution)/shard_map/pallas_call | solution.py:222
  105.8 0.7 copy-done.3
  106.6 5.9 %all-to-all-start.4 = ((bf16[32,32,512]{2,1,0:T(8,128)(2,1)}), bf16[32,32,512]{2,1,0:T(8,128)(2,1)S(1)}, u32[]{:S(2)}, u32[]{:S(2)}) async-start(bf16[32,32,512]{2,1,0:T(8,128)(2,1)} %bitcast.4), calls=%async_computation.4 | async-start | bytes 2097152 | tf_op jit(solution)/shard_map/all_to_all | solution.py:180
  112.5 0.5 copy.29
  113.0 1.4 copy.30
  114.5 13.4 %all-to-all-done.4 = bf16[32,32,512]{2,1,0:T(8,128)(2,1)S(1)} async-done(((bf16[32,32,512]{2,1,0:T(8,128)(2,1)}), bf16[32,32,512]{2,1,0:T(8,128)(2,1)S(1)}, u32[]{:S(2)}, u32[]{:S(2)}) %all-to-all-start.4) | async-done | bytes 1048608 | tf_op jit(solution)/shard_map/all_to_all | solution.py:180
  127.9 1.1 copy-done
  129.0 1.6 shard_map.140
  130.6 21.2 %all_to_all.44 = bf16[32,32,512]{2,1,0:T(8,128)(2,1)S(1)} all-to-all(bf16[32,32,512]{2,1,0:T(8,128)(2,1)S(1)} %bitcast.26), channel_id=1, replica_groups=mesh['attn'=8,'zhi'=4,'zlo'=4,'tp'=4] {'attn','tp'}, dimensions={0} | all-to-all | bytes 2097152 | tf_op jit(solution)/shard_map/all_to_all | solution.py:180
  151.8 1.4 shard_map.141
  153.2 5.4 %all-to-all-start.6 = ((bf16[16,16,512]{2,1,0:T(8,128)(2,1)}), bf16[16,16,512]{2,1,0:T(8,128)(2,1)S(1)}, u32[]{:S(2)}, u32[]{:S(2)}) async-start(bf16[16,16,512]{2,1,0:T(8,128)(2,1)} %shard_map.141), calls=%async_computation.6 | async-start | bytes 524288 | tf_op jit(solution)/shard_map/all_to_all | solution.py:180
  158.7 18.3 %all-to-all-done.6 = bf16[16,16,512]{2,1,0:T(8,128)(2,1)S(1)} async-done(((bf16[16,16,512]{2,1,0:T(8,128)(2,1)}), bf16[16,16,512]{2,1,0:T(8,128)(2,1)S(1)}, u32[]{:S(2)}, u32[]{:S(2)}) %all-to-all-start.6) | async-done | bytes 262176 | tf_op jit(solution)/shard_map/all_to_all | solution.py:180
  177.1 7.8 %all_to_all.45 = bf16[4,4,512]{2,1,0:T(4,128)(2,1)S(1)} all-to-all(bf16[4,4,512]{2,1,0:T(4,128)(2,1)S(1)} %add_convert_fusion), channel_id=1, replica_groups=mesh['attn'=8,'zhi'=4,'zlo'=4,'tp'=4] {'tp'}, dimensions={0} | all-to-all | bytes 32768 | tf_op jit(solution)/shard_map/all_to_all | solution.py:180
  184.9 0.6 reshape.43
  (32 shorter events, 0.5 us)
Async XLA Ops:
  0.0 2.2 %copy-start.5 = (bf16[16,2048]{1,0:T(8,128)(2,1)S(1)}, bf16[16,2048]{1,0:T(8,128)(2,1)}, u32[]{:S(2)}) copy-start(bf16[16,2048]{1,0:T(8,128)(2,1)} %query.1) | copy-start | bytes 196612
  1.8 0.7 copy-start.6
  2.1 0.7 copy-start.9
  2.1 0.7 copy-start.8
  2.1 0.7 copy-start.10
  2.8 1.0 copy-start.1
  3.9 1.0 copy-start.2
  10.7 35.9 %copy-start.12 = (bf16[2048,128]{1,0:T(8,128)(2,1)S(1)}, bf16[2048,128]{1,0:T(8,128)(2,1)}, u32[]{:S(2)}) copy-start(bf16[2048,128]{1,0:T(8,128)(2,1)} %param.20) | copy-start | bytes 1572868
  105.8 0.7 copy-start.3
  106.6 5.9 %copy-start.11 = (bf16[1,2048,192]{1,2,0:T(8,128)(2,1)S(1)}, bf16[1,2048,192]{1,2,0:T(8,128)(2,1)}, u32[]{:S(2)}) copy-start(bf16[1,2048,192]{1,2,0:T(8,128)(2,1)} %param.25) | copy-start | bytes 2359300
  106.6 21.3 %all-to-all-start.4 = ((bf16[32,32,512]{2,1,0:T(8,128)(2,1)}), bf16[32,32,512]{2,1,0:T(8,128)(2,1)S(1)}, u32[]{:S(2)}, u32[]{:S(2)}) async-start(bf16[32,32,512]{2,1,0:T(8,128)(2,1)} %bitcast.4), calls=%async_computation.4 | async-start | bytes 2097152 | tf_op jit(solution)/shard_map/all_to_all | solution.py:180
  114.5 13.4 %copy-start.7 = (f32[2048]{0:T(1024)S(1)}, f32[2048]{0:T(1024)}, u32[]{:S(2)}) copy-start(f32[2048]{0:T(1024)} %param.22) | copy-start | bytes 24580
  127.9 1.1 copy-start
  130.6 21.2 %copy-start.4 = (bf16[2,256,256]{2,1,0:T(8,128)(2,1)S(1)}, bf16[2,256,256]{2,1,0:T(8,128)(2,1)}, u32[]{:S(2)}) copy-start(bf16[2,256,256]{2,1,0:T(8,128)(2,1)} %copy-done.3) | copy-start | bytes 786436
  153.2 23.8 %all-to-all-start.6 = ((bf16[16,16,512]{2,1,0:T(8,128)(2,1)}), bf16[16,16,512]{2,1,0:T(8,128)(2,1)S(1)}, u32[]{:S(2)}, u32[]{:S(2)}) async-start(bf16[16,16,512]{2,1,0:T(8,128)(2,1)} %shard_map.141), calls=%async_computation.6 | async-start | bytes 524288 | tf_op jit(solution)/shard_map/all_to_all | solution.py:180

commit v2 on v1

--- a/solution.py
+++ b/solution.py
@@ -23,15 +23,17 @@
 SLOTS = 32
 FF = 192
 TOPK = 8
+PIECES = 4
 BF16 = jnp.bfloat16
 F32 = jnp.float32
 
 VMEM = pl.BlockSpec(memory_space=pltpu.VMEM)
 SMEM = pl.BlockSpec(memory_space=pltpu.SMEM)
+ANY = pl.BlockSpec(memory_space=pl.ANY)
 PARAMS = pltpu.CompilerParams(vmem_limit_bytes=40 * 1024 * 1024)
 
 
-def call(kernel, outs, in_specs, scratch=()):
+def call(kernel, outs, in_specs, scratch=(), megabytes=4):
     shapes = [jax.ShapeDtypeStruct(s, d) for s, d in outs]
     single = len(shapes) == 1
     return pl.pallas_call(
@@ -41,41 +43,67 @@
         out_specs=VMEM if single else [VMEM] * len(shapes),
         scratch_shapes=list(scratch),
         compiler_params=PARAMS,
-    )
-
-
-def attention_kernel(place, lengths, query, keys, values, new_keys, new_values, resid, meta, out, q_rows, a_rows, extra):
+        cost_estimate=pl.CostEstimate(flops=0, bytes_accessed=megabytes << 20, transcendentals=0),
+    )
+
+
+def attention_kernel(
+    place, lengths, query, keys_hbm, values_hbm, new_keys, new_values, resid, routes, route_weight, out,
+    keys, values, q_rows, a_rows, extra, sems,
+):
+    share = ROWS // PIECES
+    copies = []
+    for n, (source, target) in enumerate(((keys_hbm, keys), (values_hbm, values))):
+        for c in range(PIECES):
+            part = pl.ds(c * share, share)
+            copies.append(pltpu.make_async_copy(source.at[part], target.at[part], sems.at[n * PIECES + c]))
+            copies[-1].start()
+    tp = place[2]
+    high = route_weight[...].astype(BF16)
+    low = (route_weight[...] - high.astype(F32)).astype(BF16)
+    pick = lax.rem(lax.broadcasted_iota(jnp.int32, (TOPK, LANES), 1), TOPK)
+    spread = jnp.where(pick == lax.broadcasted_iota(jnp.int32, (TOPK, LANES), 0), 1.0, 0.0).astype(BF16)
+    diagonal = lax.broadcasted_iota(jnp.int32, (ROWS, LANES), 1) // TOPK == lax.broadcasted_iota(
+        jnp.int32, (ROWS, LANES), 0
+    )
+    extra[...] = jnp.zeros_like(extra)
+    for n, table in enumerate((routes[...].astype(F32).astype(BF16), high, low)):
+        wide = jnp.dot(table, spread, preferred_element_type=F32)
+        line = jnp.sum(jnp.where(diagonal, wide, 0.0), axis=0, keepdims=True)
+        for e in range(EXPERT):
+            extra[e, pl.ds(lax.rem(tp + 1, 4) * 4 + n, 1), :] = line
+    for e in range(EXPERT):
+        extra[e, pl.ds(tp * 4, 4), :] = resid[:, e * LANES : (e + 1) * LANES].astype(F32)
+    out[:, 4 * ROWS : 5 * ROWS, :] = extra[...].astype(BF16)
     for h in range(HEADS):
         q_rows[:, h, :] = query[:, h * HEAD_SIZE : (h + 1) * HEAD_SIZE].astype(F32)
     scale = 1.0 / math.sqrt(HEAD_SIZE)
     position = lax.broadcasted_iota(jnp.int32, (HEADS, POSITIONS), 1)
-    new_k = new_keys[...].astype(F32)
-    new_v = new_values[...].astype(F32)
+    scores = []
     for r in range(ROWS):
-        q = q_rows[r]
-        scores = lax.dot_general(
-            q.astype(BF16), keys[r], (((1,), (1,)), ((), ())), preferred_element_type=F32
-        ) * scale
-        fresh = jnp.sum(q * new_k[r : r + 1, :], axis=1, keepdims=True) * scale
-        valid = position < lengths[r]
-        top = jnp.maximum(jnp.max(jnp.where(valid, scores, -jnp.inf), axis=1, keepdims=True), fresh)
-        expo = jnp.where(valid, jnp.exp(scores - top), 0.0)
-        fresh_expo = jnp.exp(fresh - top)
-        total = jnp.sum(expo, axis=1, keepdims=True) + fresh_expo
-        weights = (expo / total).astype(BF16)
-        fresh_weight = (fresh_expo / total).astype(BF16).astype(F32)
-        mixed = jnp.dot(weights, values[r], preferred_element_type=F32)
-        a_rows[:, r, :] = mixed + fresh_weight * new_v[r : r + 1, :]
-    tp = place[2]
-    extra[...] = jnp.zeros_like(extra)
-    for e in range(EXPERT):
-        extra[e, pl.ds(tp * 4, 4), :] = resid[:, e * LANES : (e + 1) * LANES].astype(F32)
-        extra[e, pl.ds(lax.rem(tp + 1, 4) * 4, 4), :] = meta[...]
+        if r % share == 0:
+            copies[r // share].wait()
+        product = lax.dot_general(
+            q_rows[r].astype(BF16), keys[r], (((1,), (1,)), ((), ())), preferred_element_type=F32
+        )
+        scores.append(jnp.where(position < lengths[r], product * scale, -jnp.inf))
+    scores = jnp.stack(scores)
+    fresh = jnp.sum(q_rows[...] * new_keys[...].astype(F32)[:, None, :], axis=2, keepdims=True) * scale
+    top = jnp.maximum(jnp.max(scores, axis=2, keepdims=True), fresh)
+    expo = jnp.exp(scores - top)
+    fresh_expo = jnp.exp(fresh - top)
+    total = jnp.sum(expo, axis=2, keepdims=True) + fresh_expo
+    weights = (expo / total).astype(BF16)
+    fresh_weight = (fresh_expo / total).astype(BF16).astype(F32)
+    added = fresh_weight * new_values[...].astype(F32)[:, None, :]
+    for r in range(ROWS):
+        if r % share == 0:
+            copies[PIECES + r // share].wait()
+        a_rows[:, r, :] = jnp.dot(weights[r], values[r], preferred_element_type=F32) + added[r]
     for lo in range(Z_LO):
         heads = a_rows[4 * lo : 4 * lo + 4].astype(BF16).reshape(4 * ROWS, HEAD_SIZE)
         for hi in range(Z_HI):
             out[hi * Z_LO + lo, 0 : 4 * ROWS, :] = heads
-    out[:, 4 * ROWS : 5 * ROWS, :] = extra[...].astype(BF16)
 
 
 def project_kernel(place, gathered, weight, out):
@@ -167,13 +195,33 @@
             out[:, t, :, hi * LANES : (hi + 1) * LANES] = part.astype(BF16).reshape(ATTN, SLOTS, LANES)
 
 
-def combine_kernel(parts, combine, out):
-    total = jnp.zeros((EXPERT * ROWS, QUARTER), F32)
+def combine_kernel(place, parts, combine, hidden, out, total, laid):
+    mine = place[0] * Z_LO + place[1]
+    row_group = lax.broadcasted_iota(jnp.int32, (EXPERT * ROWS, LANES), 0) // ROWS
+    for hi in range(Z_HI):
+        columns = slice(hi * LANES, (hi + 1) * LANES)
+        block = hidden[hi * Z_LO : (hi + 1) * Z_LO].reshape(EXPERT * ROWS, LANES).astype(F32)
+        total[:, columns] = jnp.where(row_group == mine, block, 0.0)
+    mixed = total[...]
     for t in range(TP):
         block = parts[:, t].reshape(ATTN * SLOTS, QUARTER)
-        total = total + jnp.dot(combine[0], block, preferred_element_type=F32)
-        total = total + jnp.dot(combine[1], block, preferred_element_type=F32)
-    out[...] = total.astype(BF16).reshape(EXPERT, ROWS, QUARTER)
+        mixed = mixed + jnp.dot(combine[0], block, preferred_element_type=F32)
+        mixed = mixed + jnp.dot(combine[1], block, preferred_element_type=F32)
+    total[...] = mixed
+    for n in range(EXPERT * TP):
+        for hi in range(Z_HI):
+            laid[n, hi * 4 : (hi + 1) * 4, :] = total[n * 4 : (n + 1) * 4, hi * LANES : (hi + 1) * LANES]
+    out[...] = laid[...].astype(BF16)
+
+
+def finish_kernel(parts, out):
+    for t in range(TP):
+        total = parts[t].astype(F32)
+        for e in range(1, EXPERT):
+            total = total + parts[e * TP + t].astype(F32)
+        for hi in range(Z_HI):
+            c = hi * TP + t
+            out[:, c * LANES : (c + 1) * LANES] = total[hi * 4 : (hi + 1) * 4, :].astype(BF16)
 
 
 def exchange(x, axes):
@@ -199,21 +247,25 @@
     z = ("zhi", "zlo")
     z_hi, z_lo, tp = (lax.axis_index(n) for n in ("zhi", "zlo", "tp"))
     place = jnp.stack([z_hi, z_lo, tp]).astype(jnp.int32)
-    high = route_weight.astype(BF16).astype(F32)
-    meta = jnp.stack(
-        [v.reshape(LANES) for v in (routes.astype(F32), high, route_weight - high, jnp.zeros_like(high))]
-    )
     weight = exchange(out_weight.reshape(Z_LO, D // Z_LO, LANES), "zlo")
     sent = call(
         attention_kernel,
         [((EXPERT, 5 * ROWS, LANES), BF16)],
-        [SMEM, SMEM] + [VMEM] * 7,
+        [SMEM, SMEM, VMEM, ANY, ANY] + [VMEM] * 5,
         [
+            pltpu.VMEM((ROWS, POSITIONS, HEAD_SIZE), BF16),
+            pltpu.VMEM((ROWS, POSITIONS, HEAD_SIZE), BF16),
             pltpu.VMEM((ROWS, HEADS, HEAD_SIZE), F32),
             pltpu.VMEM((HEADS, ROWS, HEAD_SIZE), F32),
             pltpu.VMEM((EXPERT, ROWS, LANES), F32),
+            pltpu.SemaphoreType.DMA((2 * PIECES,)),
         ],
-    )(place, lengths, query, cached_key_store, cached_value_store, token_keys, token_values, resid, meta)
+        megabytes=16,
+    )(
+        place, lengths, query, cached_key_store, cached_value_store,
+        token_keys, token_values, resid, routes, route_weight,
+    )
+    sent, weight = lax.optimization_barrier((sent, weight))
     gathered = exchange(sent, z)
     parts = call(project_kernel, [((Z_LO * TP, 64, LANES), BF16)], [SMEM, VMEM, VMEM])(place, gathered, weight)
     parts = exchange(parts, ("zlo", "tp"))
@@ -232,17 +284,14 @@
         [pltpu.VMEM((ATTN * SLOTS, D), F32), pltpu.VMEM((ATTN * SLOTS, D), BF16)],
     )(incoming.reshape(ATTN, TP, SLOTS, QUARTER), norm_gain.reshape(1, D), w_gate[0], w_up[0], w_down[0])
     returned = exchange(produced.reshape(ATTN * TP, SLOTS, QUARTER), ("attn", "tp"))
-    weighted = call(combine_kernel, [((EXPERT, ROWS, QUARTER), BF16)], [VMEM, VMEM])(
-        returned.reshape(ATTN, TP, SLOTS, QUARTER), combine
-    )
-    back = exchange(weighted, z)
-    own_hidden = lax.dynamic_slice_in_dim(
-        hidden.reshape(Z_HI, EXPERT, ROWS, LANES), z_hi * Z_LO + z_lo, 1, axis=1
-    )[:, 0]
-    own_hidden = own_hidden.transpose(1, 0, 2).reshape(ROWS, QUARTER).astype(F32)
-    mixed = (jnp.sum(back.astype(F32), axis=0) + own_hidden).astype(BF16)
-    mine = exchange(mixed.reshape(TP, ROWS // TP, QUARTER), "tp")
-    return mine.reshape(TP, ROWS // TP, Z_HI, LANES).transpose(1, 2, 0, 3).reshape(ROWS // TP, D)
+    weighted = call(
+        combine_kernel,
+        [((EXPERT * TP, ROWS, LANES), BF16)],
+        [SMEM, VMEM, VMEM, VMEM],
+        [pltpu.VMEM((EXPERT * ROWS, QUARTER), F32), pltpu.VMEM((EXPERT * TP, ROWS, LANES), F32)],
+    )(place, returned.reshape(ATTN, TP, SLOTS, QUARTER), combine, hidden)
+    back = exchange(weighted, (*z, "tp"))
+    return call(finish_kernel, [((ROWS // TP, D), BF16)], [VMEM])(back)
 
 
 def solution(mesh):

time: 188 us -> 175 us (0.931)
  waiting for transfers between devices: 31.7 us -> 21.7 us
  blocking collectives: 121 us -> 123 us
    all_to_all x2, waiting for transfers between devices: 31.7 us -> 21.7 us  [exchange(): return lax.all_to_all(x, axes, split_axis=0, concat_axis=0, tiled=True)]
    all_to_all x6 -> x5, blocking collectives: 121 us -> 123 us  [exchange(): return lax.all_to_all(x, axes, split_axis=0, concat_axis=0, tiled=True)]
    pallas_call x2 -> x3, Pallas kernels: 7.19 us -> 5.76 us  [the longest x1 3.77 us: shards(): call(attention_kernel, [((EXPERT, 5 * ROWS, LANES), BF16)], [SMEM, SMEM,...]
    unnamed x29 -> x32, local copies, waits for them, and re-layouts: 6.52 us -> 6.1 us
  transfers between devices with their start and end apart: 2 -> 2, of which waited for: 2 -> 2; matrix products, arithmetic and copies ran while one was open for 1% -> 1% of each run, Pallas kernels for 0% -> 2%
where the time goes in v2:
time: 175 us; the launch traced here: 173 us
  blocking collectives  123 us (70%)
  waiting for transfers between devices  21.7 us (12%)
  starting transfers between devices  11.9 us (7%)
  Pallas kernels  10.4 us (6%)
  local copies, waits for them, and re-layouts  6.1 us (3%)
    all_to_all x5, blocking collectives, exchange(): return lax.all_to_all(x, axes, split_axis=0, concat_axis=0, tiled=True)  123 us
    all_to_all x2, waiting for transfers between devices, exchange(): return lax.all_to_all(x, axes, split_axis=0, concat_axis=0, tiled=True)  21.7 us
    all_to_all x2, starting transfers between devices, exchange(): return lax.all_to_all(x, axes, split_axis=0, concat_axis=0, tiled=True)  11.9 us
    unnamed x32, local copies, waits for them, and re-layouts  6.1 us
    pallas_call x1, Pallas kernels, shards(): call(attention_kernel, [((EXPERT, 5 * ROWS, LANES), BF16)], [SMEM, SMEM,...  3.77 us
  transfers between devices with their start and end apart: 2, of which 2 were waited for; matrix products, arithmetic and copies ran while one was open for 1% of the time, Pallas kernels for 2%

profile of v2, /device:TPU:24, one launch (start us, length us, event | category | flops | bytes accessed | tf_op | source)
XLA Modules:
  0.0 173.3 jit_solution(17544599194983492898)
XLA Ops:
  0.0 6.0 %all-to-all-start = ((bf16[4,512,128]{2,1,0:T(8,128)(2,1)}), bf16[4,512,128]{2,1,0:T(8,128)(2,1)S(1)}, u32[]{:S(2)}, u32[]{:S(2)}) async-start(bf16[4,512,128]{2,1,0:T(8,128)(2,1)} %bitcast.19), calls=%async_computation | async-start | bytes 1048576 | tf_op jit(solution)/shard_map/all_to_all | solution.py:228
  6.0 0.7 copy-done.12
  6.7 0.1 copy.15.routes
  6.8 0.0 copy-done.13
  6.8 0.1 copy.16.route_weight
  6.9 0.1 pad_add_fusion.place
  7.0 0.0 copy-done.1
  7.0 0.0 copy-done.2
  7.0 0.5 copy-done.6
  7.5 0.0 copy-done.9
  7.5 0.1 copy-done.8
  7.6 0.8 copy-done.5
  8.4 3.8 %shard_map.136 = bf16[16,80,128]{2,1,0:T(8,128)(2,1)S(1)} custom-call(s32[3]{0:T(128)S(1)} %pad_add_fusion.place, s32[16]{0:T(128)S(1)} %copy-done.10, bf16[16,2048]{1,0:T(8,128)(2,1)S(1)} %copy-done.5, bf16[16,128,128]{2,1,0:T(8,128)(2,1)S(1)} %copy-done.1, bf16[16,128,128]{2,1,0:T(8,128)(2,1)S(1)} %copy-done.2, bf16[16,128]{1,0:T(8,128)(2,1)S(1)} %copy-done.8, ...), custom_call_target="tpu_custom_call" | custom-call | bytes 16777216 | tf_op jit(solution)/shard_map/pallas_call | solution.py:251
  12.2 8.3 %all-to-all-done.weight = bf16[4,512,128]{2,1,0:T(8,128)(2,1)S(1)} async-done(((bf16[4,512,128]{2,1,0:T(8,128)(2,1)}), bf16[4,512,128]{2,1,0:T(8,128)(2,1)S(1)}, u32[]{:S(2)}, u32[]{:S(2)}) %all-to-all-start) | async-done | bytes 524320 | tf_op jit(solution)/shard_map/all_to_all | solution.py:228
  20.5 33.2 %all_to_all.35.gathered = bf16[16,80,128]{2,1,0:T(8,128)(2,1)S(1)} all-to-all(bf16[16,80,128]{2,1,0:T(8,128)(2,1)S(1)} %shard_map.136), channel_id=1, replica_groups=mesh['attn'=8,'zhi'=4,'zlo'=4,'tp'=4] {'zhi','zlo'}, dimensions={0} | all-to-all | bytes 655360 | tf_op jit(solution)/shard_map/all_to_all | solution.py:228
  53.7 1.0 shard_map.137
  54.7 16.8 %all_to_all.36.parts = bf16[16,64,128]{2,1,0:T(8,128)(2,1)S(1)} all-to-all(bf16[16,64,128]{2,1,0:T(8,128)(2,1)S(1)} %shard_map.137), channel_id=1, replica_groups=mesh['attn'=8,'zhi'=4,'zlo'=4,'tp'=4] {'zlo','tp'}, dimensions={0} | all-to-all | bytes 524288 | tf_op jit(solution)/shard_map/all_to_all | solution.py:228
  71.6 22.2 %all_to_all.37.hidden = bf16[16,64,128]{2,1,0:T(8,128)(2,1)S(1)} all-to-all(bf16[16,64,128]{2,1,0:T(8,128)(2,1)S(1)} %shard_map.138), channel_id=1, replica_groups=mesh['attn'=8,'zhi'=4,'zlo'=4,'tp'=4] {'zhi','zlo'}, dimensions={0} | all-to-all | bytes 524288 | tf_op jit(solution)/shard_map/all_to_all | solution.py:228
  93.8 2.1 %shard_map.139 = (bf16[8,4,32,512]{3,2,1,0:T(8,128)(2,1)}, bf16[2,256,256]{2,1,0:T(8,128)(2,1)S(1)}) custom-call(s32[3]{0:T(128)S(1)} %pad_add_fusion.place, bf16[16,80,128]{2,1,0:T(8,128)(2,1)S(1)} %all_to_all.35.gathered, bf16[16,64,128]{2,1,0:T(8,128)(2,1)S(1)} %all_to_all.37.hidden), custom_call_target="tpu_custom_call" | custom-call | bytes 4194304 | tf_op jit(solution)/shard_map/pallas_call | solution.py:274
  95.8 0.7 copy-done.3
  96.5 5.9 %all-to-all-start.4 = ((bf16[32,32,512]{2,1,0:T(8,128)(2,1)}), bf16[32,32,512]{2,1,0:T(8,128)(2,1)S(1)}, u32[]{:S(2)}, u32[]{:S(2)}) async-start(bf16[32,32,512]{2,1,0:T(8,128)(2,1)} %bitcast.4), calls=%async_computation.4 | async-start | bytes 2097152 | tf_op jit(solution)/shard_map/all_to_all | solution.py:228
  102.5 0.5 copy.17
  103.0 1.4 copy.18
  104.4 0.0 copy-start.7
  104.4 13.4 %all-to-all-done.4 = bf16[32,32,512]{2,1,0:T(8,128)(2,1)S(1)} async-done(((bf16[32,32,512]{2,1,0:T(8,128)(2,1)}), bf16[32,32,512]{2,1,0:T(8,128)(2,1)S(1)}, u32[]{:S(2)}, u32[]{:S(2)}) %all-to-all-start.4) | async-done | bytes 1048608 | tf_op jit(solution)/shard_map/all_to_all | solution.py:228
  117.8 0.0 copy-done.7
  117.8 1.1 copy-done
  118.9 1.6 shard_map.140
  120.5 21.2 %all_to_all.38 = bf16[32,32,512]{2,1,0:T(8,128)(2,1)S(1)} all-to-all(bf16[32,32,512]{2,1,0:T(8,128)(2,1)S(1)} %bitcast.15), channel_id=1, replica_groups=mesh['attn'=8,'zhi'=4,'zlo'=4,'tp'=4] {'attn','tp'}, dimensions={0} | all-to-all | bytes 2097152 | tf_op jit(solution)/shard_map/all_to_all | solution.py:228
  141.7 1.3 shard_map.141
  143.1 29.6 %all_to_all.39.parts = bf16[64,16,128]{2,1,0:T(8,128)(2,1)S(1)} all-to-all(bf16[64,16,128]{2,1,0:T(8,128)(2,1)S(1)} %shard_map.141), channel_id=1, replica_groups=mesh['attn'=8,'zhi'=4,'zlo'=4,'tp'=4] {'zhi','zlo','tp'}, dimensions={0} | all-to-all | bytes 524288 | tf_op jit(solution)/shard_map/all_to_all | solution.py:228
  172.6 0.7 shard_map.142
  (17 shorter events, 0.1 us)
Async XLA Ops:
  0.0 7.0 %copy-start.1 = (bf16[16,128,128]{2,1,0:T(8,128)(2,1)S(1)}, bf16[16,128,128]{2,1,0:T(8,128)(2,1)}, u32[]{:S(2)}) copy-start(bf16[16,128,128]{2,1,0:T(8,128)(2,1)} %keys_hbm.1) | copy-start | bytes 1572868
  0.0 7.0 %copy-start.2 = (bf16[16,128,128]{2,1,0:T(8,128)(2,1)S(1)}, bf16[16,128,128]{2,1,0:T(8,128)(2,1)}, u32[]{:S(2)}) copy-start(bf16[16,128,128]{2,1,0:T(8,128)(2,1)} %values_hbm.1) | copy-start | bytes 1572868
  0.0 20.5 %all-to-all-start = ((bf16[4,512,128]{2,1,0:T(8,128)(2,1)}), bf16[4,512,128]{2,1,0:T(8,128)(2,1)S(1)}, u32[]{:S(2)}, u32[]{:S(2)}) async-start(bf16[4,512,128]{2,1,0:T(8,128)(2,1)} %bitcast.19), calls=%async_computation | async-start | bytes 1048576 | tf_op jit(solution)/shard_map/all_to_all | solution.py:228
  6.0 0.8 copy-start.13
  6.0 0.7 copy-start.12
  6.7 0.7 copy-start.6
  6.8 0.7 copy-start.9
  6.9 0.7 copy-start.8
  6.9 0.7 copy-start.10
  7.6 0.8 copy-start.5
  95.8 0.7 copy-start.3
  96.5 5.9 %copy-start.11 = (bf16[1,2048,192]{1,2,0:T(8,128)(2,1)S(1)}, bf16[1,2048,192]{1,2,0:T(8,128)(2,1)}, u32[]{:S(2)}) copy-start(bf16[1,2048,192]{1,2,0:T(8,128)(2,1)} %param.25) | copy-start | bytes 2359300
  96.5 21.3 %all-to-all-start.4 = ((bf16[32,32,512]{2,1,0:T(8,128)(2,1)}), bf16[32,32,512]{2,1,0:T(8,128)(2,1)S(1)}, u32[]{:S(2)}, u32[]{:S(2)}) async-start(bf16[32,32,512]{2,1,0:T(8,128)(2,1)} %bitcast.4), calls=%async_computation.4 | async-start | bytes 2097152 | tf_op jit(solution)/shard_map/all_to_all | solution.py:228
  104.4 13.4 %copy-start.7 = (f32[2048]{0:T(1024)S(1)}, f32[2048]{0:T(1024)}, u32[]{:S(2)}) copy-start(f32[2048]{0:T(1024)} %param.22) | copy-start | bytes 24580
  117.8 1.1 copy-start
  120.5 21.2 %copy-start.4 = (bf16[2,256,256]{2,1,0:T(8,128)(2,1)S(1)}, bf16[2,256,256]{2,1,0:T(8,128)(2,1)}, u32[]{:S(2)}) copy-start(bf16[2,256,256]{2,1,0:T(8,128)(2,1)} %copy-done.3) | copy-start | bytes 786436

commit v3 on v2

--- a/solution.py
+++ b/solution.py
@@ -20,7 +20,7 @@
 D = 2048
 LANES = 128
 QUARTER = D // TP
-SLOTS = 32
+CAP = 2
 FF = 192
 TOPK = 8
 PIECES = 4
@@ -30,7 +30,7 @@
 VMEM = pl.BlockSpec(memory_space=pltpu.VMEM)
 SMEM = pl.BlockSpec(memory_space=pltpu.SMEM)
 ANY = pl.BlockSpec(memory_space=pl.ANY)
-PARAMS = pltpu.CompilerParams(vmem_limit_bytes=40 * 1024 * 1024)
+PARAMS = pltpu.CompilerParams(vmem_limit_bytes=20 * 1024 * 1024)
 
 
 def call(kernel, outs, in_specs, scratch=(), megabytes=4):
@@ -130,7 +130,7 @@
         out[i] = total
 
 
-def select_kernel(place, gathered, hidden, out, combine):
+def routing_kernel(place, gathered, choice, combine):
     tp = place[2]
     mine = place[0] * Z_LO + place[1]
     extra = gathered[:, 4 * ROWS : 5 * ROWS, :].astype(F32)
@@ -156,26 +156,27 @@
     rank = dot(hit, earlier)
     weight_high = dot(hit_high, here)
     weight_low = dot(hit_low, here)
-    chosen = [jnp.where(rank == s, named, 0.0) for s in (0.0, 1.0)]
-
-    def laid(pair):
-        return jnp.concatenate(
-            [pair[s][a * EXPERT : (a + 1) * EXPERT, :] for a in range(ATTN) for s in range(2)], axis=0
-        )
-
-    choice = laid(chosen).astype(BF16)
-    combine[0] = jnp.transpose(laid([c * weight_high for c in chosen])).astype(BF16)
-    combine[1] = jnp.transpose(laid([c * weight_low for c in chosen])).astype(BF16)
+    for s in range(CAP):
+        chosen = jnp.where(rank == float(s), named, 0.0)
+        choice[s] = chosen.astype(BF16)
+        combine[s, 0] = jnp.transpose(chosen * weight_high).astype(BF16)
+        combine[s, 1] = jnp.transpose(chosen * weight_low).astype(BF16)
+
+
+def select_kernel(choice, hidden, out):
     for hi in range(Z_HI):
         block = hidden[hi * Z_LO : (hi + 1) * Z_LO].reshape(EXPERT * ROWS, LANES)
-        sent = jnp.dot(choice, block, preferred_element_type=F32).astype(BF16)
-        sent = sent.reshape(ATTN, SLOTS, LANES)
-        for t in range(TP):
-            out[:, t, :, hi * LANES : (hi + 1) * LANES] = sent
-
-
-def expert_kernel(tokens, gain, w_gate, w_up, w_down, out, x, normed):
-    slots = ATTN * SLOTS
+        for s in range(CAP):
+            sent = jnp.dot(choice[s], block, preferred_element_type=F32).astype(BF16)
+            sent = sent.reshape(ATTN, EXPERT, LANES)
+            for t in range(s, TP, CAP):
+                out[:, t, :, hi * LANES : (hi + 1) * LANES] = sent
+
+
+def expert_kernel(
+    tokens, gain, gate_a, up_a, down_a, gate_b, gate_c, up_b, up_c, down_b, down_c, out, x, normed
+):
+    slots = ATTN * EXPERT
     square = jnp.zeros((slots, LANES), F32)
     for hi in range(Z_HI):
         for t in range(TP):
@@ -185,14 +186,19 @@
             square = square + block * block
     factor = lax.rsqrt(jnp.sum(square, axis=1, keepdims=True) * (1.0 / D) + 1e-06)
     normed[...] = (x[...] * factor * gain[...]).astype(BF16)
-    gate = jnp.dot(normed[...], w_gate[...], preferred_element_type=F32)
-    up = jnp.dot(normed[...], w_up[...], preferred_element_type=F32)
+    rows = normed[...]
+    turned = (((1,), (1,)), ((), ()))
+    joined = lambda *refs: jnp.concatenate([r[...] for r in refs], axis=0)
+    gate = lax.dot_general(rows, joined(gate_a, gate_b, gate_c), turned, preferred_element_type=F32)
+    up = lax.dot_general(rows, joined(up_a, up_b, up_c), turned, preferred_element_type=F32)
     activated = (gate / (1.0 + jnp.exp(-gate)) * up).astype(BF16)
     for hi in range(Z_HI):
+        columns = slice(hi * QUARTER, (hi + 1) * QUARTER)
+        down = jnp.concatenate([r[:, columns] for r in (down_a, down_b, down_c)], axis=0)
+        part = jnp.dot(activated, down, preferred_element_type=F32).astype(BF16)
         for t in range(TP):
-            c = hi * TP + t
-            part = jnp.dot(activated, w_down[:, c * LANES : (c + 1) * LANES], preferred_element_type=F32)
-            out[:, t, :, hi * LANES : (hi + 1) * LANES] = part.astype(BF16).reshape(ATTN, SLOTS, LANES)
+            block = part[:, t * LANES : (t + 1) * LANES].reshape(ATTN, EXPERT, LANES)
+            out[:, t, :, hi * LANES : (hi + 1) * LANES] = block
 
 
 def combine_kernel(place, parts, combine, hidden, out, total, laid):
@@ -204,9 +210,9 @@
         total[:, columns] = jnp.where(row_group == mine, block, 0.0)
     mixed = total[...]
     for t in range(TP):
-        block = parts[:, t].reshape(ATTN * SLOTS, QUARTER)
-        mixed = mixed + jnp.dot(combine[0], block, preferred_element_type=F32)
-        mixed = mixed + jnp.dot(combine[1], block, preferred_element_type=F32)
+        block = parts[:, t].reshape(ATTN * EXPERT, QUARTER)
+        mixed = mixed + jnp.dot(combine[t % CAP, 0], block, preferred_element_type=F32)
+        mixed = mixed + jnp.dot(combine[t % CAP, 1], block, preferred_element_type=F32)
     total[...] = mixed
     for n in range(EXPERT * TP):
         for hi in range(Z_HI):
@@ -247,6 +253,11 @@
     z = ("zhi", "zlo")
     z_hi, z_lo, tp = (lax.axis_index(n) for n in ("zhi", "zlo", "tp"))
     place = jnp.stack([z_hi, z_lo, tp]).astype(jnp.int32)
+    own_part = (w_gate[0].T, w_up[0].T, w_down[0])
+    ring = {d: [(i, (i + d) % TP) for i in range(TP)] for d in (1, -1)}
+    taken = [
+        (lax.ppermute(w[: FF // 2], "tp", ring[-1]), lax.ppermute(w[FF // 2 :], "tp", ring[1])) for w in own_part
+    ]
     weight = exchange(out_weight.reshape(Z_LO, D // Z_LO, LANES), "zlo")
     sent = call(
         attention_kernel,
@@ -265,31 +276,37 @@
         place, lengths, query, cached_key_store, cached_value_store,
         token_keys, token_values, resid, routes, route_weight,
     )
-    sent, weight = lax.optimization_barrier((sent, weight))
+    sent, weight, gates = lax.optimization_barrier((sent, weight, taken[0]))
     gathered = exchange(sent, z)
     parts = call(project_kernel, [((Z_LO * TP, 64, LANES), BF16)], [SMEM, VMEM, VMEM])(place, gathered, weight)
+    parts, ups = lax.optimization_barrier((parts, taken[1]))
     parts = exchange(parts, ("zlo", "tp"))
     own = call(reduce_kernel, [((EXPERT, 64, LANES), BF16)], [VMEM])(parts)
     hidden = exchange(own, z)
-    outgoing, combine = call(
-        select_kernel,
-        [((ATTN, TP, SLOTS, QUARTER), BF16), ((2, EXPERT * ROWS, ATTN * SLOTS), BF16)],
-        [SMEM, VMEM, VMEM],
-    )(place, gathered, hidden)
-    incoming = exchange(outgoing.reshape(ATTN * TP, SLOTS, QUARTER), ("attn", "tp"))
+    choice, combine = call(
+        routing_kernel,
+        [
+            ((CAP, ATTN * EXPERT, EXPERT * ROWS), BF16),
+            ((CAP, 2, EXPERT * ROWS, ATTN * EXPERT), BF16),
+        ],
+        [SMEM, VMEM],
+    )(place, gathered)
+    outgoing = call(select_kernel, [((ATTN, TP, EXPERT, QUARTER), BF16)], [VMEM, VMEM])(choice, hidden)
+    outgoing, downs = lax.optimization_barrier((outgoing, taken[2]))
+    incoming = exchange(outgoing.reshape(ATTN * TP, EXPERT, QUARTER), ("attn", "tp"))
     produced = call(
         expert_kernel,
-        [((ATTN, TP, SLOTS, QUARTER), BF16)],
-        [VMEM] * 5,
-        [pltpu.VMEM((ATTN * SLOTS, D), F32), pltpu.VMEM((ATTN * SLOTS, D), BF16)],
-    )(incoming.reshape(ATTN, TP, SLOTS, QUARTER), norm_gain.reshape(1, D), w_gate[0], w_up[0], w_down[0])
-    returned = exchange(produced.reshape(ATTN * TP, SLOTS, QUARTER), ("attn", "tp"))
+        [((ATTN, TP, EXPERT, QUARTER), BF16)],
+        [VMEM] * 11,
+        [pltpu.VMEM((ATTN * EXPERT, D), F32), pltpu.VMEM((ATTN * EXPERT, D), BF16)],
+    )(incoming.reshape(ATTN, TP, EXPERT, QUARTER), norm_gain.reshape(1, D), *own_part, *gates, *ups, *downs)
+    returned = exchange(produced.reshape(ATTN * TP, EXPERT, QUARTER), ("attn", "tp"))
     weighted = call(
         combine_kernel,
         [((EXPERT * TP, ROWS, LANES), BF16)],
         [SMEM, VMEM, VMEM, VMEM],
         [pltpu.VMEM((EXPERT * ROWS, QUARTER), F32), pltpu.VMEM((EXPERT * TP, ROWS, LANES), F32)],
-    )(place, returned.reshape(ATTN, TP, SLOTS, QUARTER), combine, hidden)
+    )(place, returned.reshape(ATTN, TP, EXPERT, QUARTER), combine, hidden)
     back = exchange(weighted, (*z, "tp"))
     return call(finish_kernel, [((ROWS // TP, D), BF16)], [VMEM])(back)
 

time: 175 us -> 170 us (0.971)
  blocking collectives: 123 us -> 82.6 us
  starting transfers between devices: 11.9 us -> 45.3 us
  waiting for transfers between devices: 21.7 us -> 19.6 us
  Pallas kernels: 10.4 us -> 12.3 us
  local copies, waits for them, and re-layouts: 6.1 us -> 7.92 us
    all_to_all x5 -> x4, blocking collectives: 123 us -> 82.6 us  [exchange(): return lax.all_to_all(x, axes, split_axis=0, concat_axis=0, tiled=True)]
    ppermute x0 -> x6, starting transfers between devices: none -> 21.3 us  [the longest x3 12 us: shards(): lax.ppermute(w[:FF // 2], 'tp', ring[-1])]
    all_to_all x2 -> x3, starting transfers between devices: 11.9 us -> 24.1 us  [exchange(): return lax.all_to_all(x, axes, split_axis=0, concat_axis=0, tiled=True)]
    slice x0 -> x3, local copies, waits for them, and re-layouts: none -> 2.89 us  [shards(): w[FF // 2:]]
    all_to_all x2 -> x3, waiting for transfers between devices: 21.7 us -> 19.6 us  [exchange(): return lax.all_to_all(x, axes, split_axis=0, concat_axis=0, tiled=True)]
    unnamed x32 -> x40, local copies, waits for them, and re-layouts: 6.1 us -> 5.03 us
    pallas_call x2 -> x3, Pallas kernels: 3.63 us -> 4.14 us  [the longest x1 2.84 us: shards(): call(expert_kernel, [((ATTN, TP, EXPERT, QUARTER), BF16)], [VMEM] * 11, [...]
  transfers between devices with their start and end apart: 2 -> 9, of which waited for: 2 -> 2; matrix products, arithmetic and copies ran while one was open for 1% -> 2% of each run, Pallas kernels for 2% -> 4%
where the time goes in v3:
time: 170 us; the launch traced here: 168 us
  blocking collectives  82.6 us (49%)
  starting transfers between devices  45.3 us (27%)
  waiting for transfers between devices  19.6 us (12%)
  Pallas kernels  12.3 us (7%)
  local copies, waits for them, and re-layouts  7.92 us (5%)
    all_to_all x4, blocking collectives, exchange(): return lax.all_to_all(x, axes, split_axis=0, concat_axis=0, tiled=True)  82.6 us
    all_to_all x3, starting transfers between devices, exchange(): return lax.all_to_all(x, axes, split_axis=0, concat_axis=0, tiled=True)  24.1 us
    all_to_all x3, waiting for transfers between devices, exchange(): return lax.all_to_all(x, axes, split_axis=0, concat_axis=0, tiled=True)  19.6 us
    ppermute x3, starting transfers between devices, shards(): lax.ppermute(w[:FF // 2], 'tp', ring[-1])  12 us
    ppermute x3, starting transfers between devices, shards(): lax.ppermute(w[FF // 2:], 'tp', ring[1])  9.25 us
    unnamed x40, local copies, waits for them, and re-layouts  5.03 us
    pallas_call x1, Pallas kernels, shards(): call(attention_kernel, [((EXPERT, 5 * ROWS, LANES), BF16)], [SMEM, SMEM,...  4.51 us
  transfers between devices with their start and end apart: 9, of which 2 were waited for; matrix products, arithmetic and copies ran while one was open for 2% of the time, Pallas kernels for 4%

profile of v3, /device:TPU:24, one launch (start us, length us, event | category | flops | bytes accessed | tf_op | source)
XLA Modules:
  0.0 168.1 jit_solution(6373072346687183238)
XLA Ops:
  0.0 6.0 %all-to-all-start = ((bf16[4,512,128]{2,1,0:T(8,128)(2,1)}), bf16[4,512,128]{2,1,0:T(8,128)(2,1)S(1)}, u32[]{:S(2)}, u32[]{:S(2)}) async-start(bf16[4,512,128]{2,1,0:T(8,128)(2,1)} %bitcast.30), calls=%async_computation | async-start | bytes 1048576 | tf_op jit(solution)/shard_map/all_to_all | solution.py:234
  6.0 1.0 fusion.1
  7.0 3.4 %collective-permute-start.1 = (bf16[96,2048]{1,0:T(8,128)(2,1)}, bf16[96,2048]{1,0:T(8,128)(2,1)S(1)}, u32[]{:S(2)}, u32[]{:S(2)}) collective-permute-start(bf16[96,2048]{1,0:T(8,128)(2,1)} %get-tuple-element.33), channel_id=1, source_target_pairs={{0,1},{1,2},{2,3},{3,0},{4,5},{5,6},{6,7},{7,4},{8,9},{9,10},{10,1... | collective-permute-start | bytes 1179656 | tf_op jit(solution)/shard_map/ppermute | solution.py:259
  10.4 3.7 %collective-permute-start = (bf16[96,2048]{1,0:T(8,128)(2,1)}, bf16[96,2048]{1,0:T(8,128)(2,1)}, u32[]{:S(2)}, u32[]{:S(2)}) collective-permute-start(bf16[96,2048]{1,0:T(8,128)(2,1)} %get-tuple-element.34), channel_id=1, source_target_pairs={{0,3},{1,0},{2,1},{3,2},{4,7},{5,4},{6,5},{7,6},{8,11},{9,8},{10,9... | collective-permute-start | bytes 1179656 | tf_op jit(solution)/shard_map/ppermute | solution.py:259
  14.1 0.7 copy-done.17
  14.8 0.6 copy-done.18
  15.6 0.6 copy-done.14
  16.2 0.8 copy-done.9
  17.1 0.7 copy-done.10
  17.8 0.7 copy-done.15
  18.5 4.5 %shard_map.136 = bf16[16,80,128]{2,1,0:T(8,128)(2,1)} custom-call(s32[3]{0:T(128)S(1)} %pad_add_fusion.place, s32[16]{0:T(128)S(1)} %copy-done.16, bf16[16,2048]{1,0:T(8,128)(2,1)S(1)} %copy-done.9, bf16[16,128,128]{2,1,0:T(8,128)(2,1)S(1)} %copy-done.3, bf16[16,128,128]{2,1,0:T(8,128)(2,1)S(1)} %copy-done.4, bf16[16,128]{1,0:T(8,128)(2,1)S(1)} %copy-done.14, ...), custom_call_target="tpu_custom_call" | custom-call | bytes 16777216 | tf_op jit(solution)/shard_map/pallas_call | solution.py:262
  23.0 13.3 %all-to-all-start.1 = ((bf16[16,80,128]{2,1,0:T(8,128)(2,1)}), bf16[16,80,128]{2,1,0:T(8,128)(2,1)S(1)}, u32[]{:S(2)}, u32[]{:S(2)}) async-start(bf16[16,80,128]{2,1,0:T(8,128)(2,1)} %shard_map.136), calls=%async_computation.1 | async-start | bytes 655360 | tf_op jit(solution)/shard_map/all_to_all | solution.py:234
  36.4 1.0 fusion
  37.3 3.4 %collective-permute-start.3 = (bf16[96,2048]{1,0:T(8,128)(2,1)}, bf16[96,2048]{1,0:T(8,128)(2,1)S(1)}, u32[]{:S(2)}, u32[]{:S(2)}) collective-permute-start(bf16[96,2048]{1,0:T(8,128)(2,1)} %get-tuple-element.31), channel_id=1, source_target_pairs={{0,1},{1,2},{2,3},{3,0},{4,5},{5,6},{6,7},{7,4},{8,9},{9,10},{10,1... | collective-permute-start | bytes 1179656 | tf_op jit(solution)/shard_map/ppermute | solution.py:259
  40.7 3.8 %collective-permute-start.2 = (bf16[96,2048]{1,0:T(8,128)(2,1)}, bf16[96,2048]{1,0:T(8,128)(2,1)}, u32[]{:S(2)}, u32[]{:S(2)}) collective-permute-start(bf16[96,2048]{1,0:T(8,128)(2,1)} %get-tuple-element.32), channel_id=1, source_target_pairs={{0,3},{1,0},{2,1},{3,2},{4,7},{5,4},{6,5},{7,6},{8,11},{9,8},{10,9... | collective-permute-start | bytes 1179656 | tf_op jit(solution)/shard_map/ppermute | solution.py:259
  44.5 12.1 %all-to-all-done.1.gathered = bf16[16,80,128]{2,1,0:T(8,128)(2,1)S(1)} async-done(((bf16[16,80,128]{2,1,0:T(8,128)(2,1)}), bf16[16,80,128]{2,1,0:T(8,128)(2,1)S(1)}, u32[]{:S(2)}, u32[]{:S(2)}) %all-to-all-start.1) | async-done | bytes 327712 | tf_op jit(solution)/shard_map/all_to_all | solution.py:234
  56.6 1.0 shard_map.138
  57.6 16.5 %all_to_all.35.parts = bf16[16,64,128]{2,1,0:T(8,128)(2,1)S(1)} all-to-all(bf16[16,64,128]{2,1,0:T(8,128)(2,1)S(1)} %shard_map.138), channel_id=1, replica_groups=mesh['attn'=8,'zhi'=4,'zlo'=4,'tp'=4] {'zlo','tp'}, dimensions={0} | all-to-all | bytes 524288 | tf_op jit(solution)/shard_map/all_to_all | solution.py:234
  74.1 0.8 shard_map.139
  74.9 4.7 %all-to-all-start.3 = ((bf16[16,64,128]{2,1,0:T(8,128)(2,1)}), bf16[16,64,128]{2,1,0:T(8,128)(2,1)S(1)}, u32[]{:S(2)}, u32[]{:S(2)}) async-start(bf16[16,64,128]{2,1,0:T(8,128)(2,1)} %shard_map.139), calls=%async_computation.3 | async-start | bytes 524288 | tf_op jit(solution)/shard_map/all_to_all | solution.py:234
  79.6 0.9 slice_bitcast_fusion
  80.6 2.5 %collective-permute-start.5 = (bf16[96,2048]{1,0:T(8,128)(2,1)}, bf16[96,2048]{1,0:T(8,128)(2,1)}, u32[]{:S(2)}, u32[]{:S(2)}) collective-permute-start(bf16[96,2048]{1,0:T(8,128)(2,1)} %get-tuple-element.29), channel_id=1, source_target_pairs={{0,1},{1,2},{2,3},{3,0},{4,5},{5,6},{6,7},{7,4},{8,9},{9,10},{10,1... | collective-permute-start | bytes 1179656 | tf_op jit(solution)/shard_map/ppermute | solution.py:259
  83.0 4.6 %collective-permute-start.4 = (bf16[96,2048]{1,0:T(8,128)(2,1)}, bf16[96,2048]{1,0:T(8,128)(2,1)}, u32[]{:S(2)}, u32[]{:S(2)}) collective-permute-start(bf16[96,2048]{1,0:T(8,128)(2,1)} %get-tuple-element.30), channel_id=1, source_target_pairs={{0,3},{1,0},{2,1},{3,2},{4,7},{5,4},{6,5},{7,6},{8,11},{9,8},{10,9... | collective-permute-start | bytes 1179656 | tf_op jit(solution)/shard_map/ppermute | solution.py:259
  87.6 1.0 shard_map.137
  88.6 0.7 copy-done.7
  89.3 7.5 %all-to-all-done.3.hidden = bf16[16,64,128]{2,1,0:T(8,128)(2,1)S(1)} async-done(((bf16[16,64,128]{2,1,0:T(8,128)(2,1)}), bf16[16,64,128]{2,1,0:T(8,128)(2,1)S(1)}, u32[]{:S(2)}, u32[]{:S(2)}) %all-to-all-start.3) | async-done | bytes 262176 | tf_op jit(solution)/shard_map/all_to_all | solution.py:234
  97.1 15.3 %all_to_all.36 = bf16[32,16,512]{2,1,0:T(8,128)(2,1)S(1)} all-to-all(bf16[32,16,512]{2,1,0:T(8,128)(2,1)S(1)} %bitcast.26), channel_id=1, replica_groups=mesh['attn'=8,'zhi'=4,'zlo'=4,'tp'=4] {'attn','tp'}, dimensions={0} | all-to-all | bytes 1048576 | tf_op jit(solution)/shard_map/all_to_all | solution.py:234
  112.4 2.8 %shard_map.141 = bf16[8,4,16,512]{3,2,1,0:T(8,128)(2,1)S(1)} custom-call(bf16[8,4,16,512]{3,2,1,0:T(8,128)(2,1)S(1)} %bitcast.27, f32[1,2048]{1,0:T(1,128)S(1)} %bitcast.29, bf16[192,2048]{1,0:T(8,128)(2,1)S(1)} %bitcast.21, bf16[192,2048]{1,0:T(8,128)(2,1)S(1)} %bitcast.23, bf16[192,2048]{1,0:T(8,128)(2,1)S(1)} %bitcast.24, ...), custom_call_target="tpu_custom_call" | custom-call | bytes 4194304 | tf_op jit(solution)/shard_map/pallas_call | solution.py:297
  115.3 15.7 %all_to_all.37 = bf16[32,16,512]{2,1,0:T(8,128)(2,1)S(1)} all-to-all(bf16[32,16,512]{2,1,0:T(8,128)(2,1)S(1)} %bitcast.28), channel_id=1, replica_groups=mesh['attn'=8,'zhi'=4,'zlo'=4,'tp'=4] {'attn','tp'}, dimensions={0} | all-to-all | bytes 1048576 | tf_op jit(solution)/shard_map/all_to_all | solution.py:234
  131.0 1.3 shard_map.142
  132.3 35.2 %all_to_all.38.parts = bf16[64,16,128]{2,1,0:T(8,128)(2,1)S(1)} all-to-all(bf16[64,16,128]{2,1,0:T(8,128)(2,1)S(1)} %shard_map.142), channel_id=1, replica_groups=mesh['attn'=8,'zhi'=4,'zlo'=4,'tp'=4] {'zhi','zlo','tp'}, dimensions={0} | all-to-all | bytes 524288 | tf_op jit(solution)/shard_map/all_to_all | solution.py:234
  167.5 0.7 shard_map.143
  (42 shorter events, 0.6 us)
Async XLA Ops:
  0.0 6.0 %copy-start = (bf16[1,2048,192]{1,2,0:T(8,128)(2,1)S(1)}, bf16[1,2048,192]{1,2,0:T(8,128)(2,1)}, u32[]{:S(2)}) copy-start(bf16[1,2048,192]{1,2,0:T(8,128)(2,1)} %param.25) | copy-start | bytes 2359300
  0.0 23.0 %all-to-all-start = ((bf16[4,512,128]{2,1,0:T(8,128)(2,1)}), bf16[4,512,128]{2,1,0:T(8,128)(2,1)S(1)}, u32[]{:S(2)}, u32[]{:S(2)}) async-start(bf16[4,512,128]{2,1,0:T(8,128)(2,1)} %bitcast.30), calls=%async_computation | async-start | bytes 1048576 | tf_op jit(solution)/shard_map/all_to_all | solution.py:234
  6.0 9.6 %copy-start.3 = (bf16[16,128,128]{2,1,0:T(8,128)(2,1)S(1)}, bf16[16,128,128]{2,1,0:T(8,128)(2,1)}, u32[]{:S(2)}) copy-start(bf16[16,128,128]{2,1,0:T(8,128)(2,1)} %keys_hbm.1) | copy-start | bytes 1572868
  6.0 9.6 %copy-start.4 = (bf16[16,128,128]{2,1,0:T(8,128)(2,1)S(1)}, bf16[16,128,128]{2,1,0:T(8,128)(2,1)}, u32[]{:S(2)}) copy-start(bf16[16,128,128]{2,1,0:T(8,128)(2,1)} %values_hbm.1) | copy-start | bytes 1572868
  7.0 16.0 %collective-permute-start.1 = (bf16[96,2048]{1,0:T(8,128)(2,1)}, bf16[96,2048]{1,0:T(8,128)(2,1)S(1)}, u32[]{:S(2)}, u32[]{:S(2)}) collective-permute-start(bf16[96,2048]{1,0:T(8,128)(2,1)} %get-tuple-element.33), channel_id=1, source_target_pairs={{0,1},{1,2},{2,3},{3,0},{4,5},{5,6},{6,7},{7,4},{8,9},{9,10},{10,1... | collective-permute-start | bytes 1179656 | tf_op jit(solution)/shard_map/ppermute | solution.py:259
  10.4 12.6 %collective-permute-start = (bf16[96,2048]{1,0:T(8,128)(2,1)}, bf16[96,2048]{1,0:T(8,128)(2,1)}, u32[]{:S(2)}, u32[]{:S(2)}) collective-permute-start(bf16[96,2048]{1,0:T(8,128)(2,1)} %get-tuple-element.34), channel_id=1, source_target_pairs={{0,3},{1,0},{2,1},{3,2},{4,7},{5,4},{6,5},{7,6},{8,11},{9,8},{10,9... | collective-permute-start | bytes 1179656 | tf_op jit(solution)/shard_map/ppermute | solution.py:259
  14.1 0.7 copy-start.17
  14.8 0.7 copy-start.18
  15.5 0.7 copy-start.14
  15.5 0.7 copy-start.16
  16.2 0.8 copy-start.9
  17.1 0.7 copy-start.10
  17.8 0.7 copy-start.15
  18.5 4.5 %copy-start.11 = (s32[3]{0:T(128)}, s32[3]{0:T(128)S(1)}, u32[]{:S(2)}) copy-start(s32[3]{0:T(128)S(1)} %pad_add_fusion.place) | copy-start | bytes 40
  18.5 17.9 %copy-start.1 = (bf16[1,2048,192]{1,2,0:T(8,128)(2,1)S(1)}, bf16[1,2048,192]{1,2,0:T(8,128)(2,1)}, u32[]{:S(2)}) copy-start(bf16[1,2048,192]{1,2,0:T(8,128)(2,1)} %param.26) | copy-start | bytes 2359300
  23.0 33.6 %all-to-all-start.1 = ((bf16[16,80,128]{2,1,0:T(8,128)(2,1)}), bf16[16,80,128]{2,1,0:T(8,128)(2,1)S(1)}, u32[]{:S(2)}, u32[]{:S(2)}) async-start(bf16[16,80,128]{2,1,0:T(8,128)(2,1)} %shard_map.136), calls=%async_computation.1 | async-start | bytes 655360 | tf_op jit(solution)/shard_map/all_to_all | solution.py:234
  37.3 19.3 %copy-start.12 = (s32[3]{0:T(128)S(1)}, s32[3]{0:T(128)}, u32[]{:S(2)}) copy-start(s32[3]{0:T(128)} %copy-done.11) | copy-start | bytes 40
  37.3 20.3 %collective-permute-start.3 = (bf16[96,2048]{1,0:T(8,128)(2,1)}, bf16[96,2048]{1,0:T(8,128)(2,1)S(1)}, u32[]{:S(2)}, u32[]{:S(2)}) collective-permute-start(bf16[96,2048]{1,0:T(8,128)(2,1)} %get-tuple-element.31), channel_id=1, source_target_pairs={{0,1},{1,2},{2,3},{3,0},{4,5},{5,6},{6,7},{7,4},{8,9},{9,10},{10,1... | collective-permute-start | bytes 1179656 | tf_op jit(solution)/shard_map/ppermute | solution.py:259
  40.7 16.9 %collective-permute-start.2 = (bf16[96,2048]{1,0:T(8,128)(2,1)}, bf16[96,2048]{1,0:T(8,128)(2,1)}, u32[]{:S(2)}, u32[]{:S(2)}) collective-permute-start(bf16[96,2048]{1,0:T(8,128)(2,1)} %get-tuple-element.32), channel_id=1, source_target_pairs={{0,3},{1,0},{2,1},{3,2},{4,7},{5,4},{6,5},{7,6},{8,11},{9,8},{10,9... | collective-permute-start | bytes 1179656 | tf_op jit(solution)/shard_map/ppermute | solution.py:259
  57.6 22.0 %copy-start.2 = (bf16[1,192,2048]{2,1,0:T(8,128)(2,1)S(1)}, bf16[1,192,2048]{2,1,0:T(8,128)(2,1)}, u32[]{:S(2)}) copy-start(bf16[1,192,2048]{2,1,0:T(8,128)(2,1)} %param.27) | copy-start | bytes 2359300
  57.6 17.2 %copy-start.5 = (bf16[96,2048]{1,0:T(8,128)(2,1)}, bf16[96,2048]{1,0:T(8,128)(2,1)S(1)}, u32[]{:S(2)}) copy-start(bf16[96,2048]{1,0:T(8,128)(2,1)S(1)} %collective-permute-done.3.up_c) | copy-start | bytes 1179652
  74.9 21.9 %all-to-all-start.3 = ((bf16[16,64,128]{2,1,0:T(8,128)(2,1)}), bf16[16,64,128]{2,1,0:T(8,128)(2,1)S(1)}, u32[]{:S(2)}, u32[]{:S(2)}) async-start(bf16[16,64,128]{2,1,0:T(8,128)(2,1)} %shard_map.139), calls=%async_computation.3 | async-start | bytes 524288 | tf_op jit(solution)/shard_map/all_to_all | solution.py:234
  80.6 16.6 %collective-permute-start.5 = (bf16[96,2048]{1,0:T(8,128)(2,1)}, bf16[96,2048]{1,0:T(8,128)(2,1)}, u32[]{:S(2)}, u32[]{:S(2)}) collective-permute-start(bf16[96,2048]{1,0:T(8,128)(2,1)} %get-tuple-element.29), channel_id=1, source_target_pairs={{0,1},{1,2},{2,3},{3,0},{4,5},{5,6},{6,7},{7,4},{8,9},{9,10},{10,1... | collective-permute-start | bytes 1179656 | tf_op jit(solution)/shard_map/ppermute | solution.py:259
  83.0 14.1 %collective-permute-start.4 = (bf16[96,2048]{1,0:T(8,128)(2,1)}, bf16[96,2048]{1,0:T(8,128)(2,1)}, u32[]{:S(2)}, u32[]{:S(2)}) collective-permute-start(bf16[96,2048]{1,0:T(8,128)(2,1)} %get-tuple-element.30), channel_id=1, source_target_pairs={{0,3},{1,0},{2,1},{3,2},{4,7},{5,4},{6,5},{7,6},{8,11},{9,8},{10,9... | collective-permute-start | bytes 1179656 | tf_op jit(solution)/shard_map/ppermute | solution.py:259
  88.6 0.7 copy-start.7
  97.1 15.3 %copy-start.6 = (bf16[96,2048]{1,0:T(8,128)(2,1)S(1)}, bf16[96,2048]{1,0:T(8,128)(2,1)}, u32[]{:S(2)}) copy-start(bf16[96,2048]{1,0:T(8,128)(2,1)} %copy-done.5) | copy-start | bytes 1179652
  97.1 15.3 %copy-start.13 = (f32[2048]{0:T(1024)S(1)}, f32[2048]{0:T(1024)}, u32[]{:S(2)}) copy-start(f32[2048]{0:T(1024)} %param.22) | copy-start | bytes 24580
  115.3 15.7 %copy-start.8 = (bf16[2,2,256,128]{3,2,1,0:T(8,128)(2,1)S(1)}, bf16[2,2,256,128]{3,2,1,0:T(8,128)(2,1)}, u32[]{:S(2)}) copy-start(bf16[2,2,256,128]{3,2,1,0:T(8,128)(2,1)} %copy-done.7) | copy-start | bytes 786436

commit v4 on v3

v4 whole, which is shorter than its diff:
```python
import math

import jax
import jax.numpy as jnp
from jax import lax
from jax.experimental import pallas as pl
from jax.experimental.pallas import tpu as pltpu
from jax.sharding import Mesh
from jax.sharding import PartitionSpec as P

HEADS = 16
HEAD_SIZE = 128
POSITIONS = 128
ROWS = 16
ATTN = 8
Z_HI = 8
Z_LO = 2
EXPERT = Z_HI * Z_LO
TP = 4
D = 2048
LANES = 128
QUARTER = D // TP
CHUNKS = 4
BLOCK = 64
SENT_HEADS = HEADS // Z_LO
SENT = SENT_HEADS * ROWS
MORE = 8
CAP = 2
FF = 192
TOPK = 8
PIECES = 4
BF16 = jnp.bfloat16
F32 = jnp.float32

VMEM = pl.BlockSpec(memory_space=pltpu.VMEM)
SMEM = pl.BlockSpec(memory_space=pltpu.SMEM)
ANY = pl.BlockSpec(memory_space=pl.ANY)


def call(kernel, outs, in_specs, scratch=(), megabytes=4, limit=20):
    shapes = [jax.ShapeDtypeStruct(s, d) for s, d in outs]
    single = len(shapes) == 1
    return pl.pallas_call(
        kernel,
        out_shape=shapes[0] if single else shapes,
        in_specs=in_specs,
        out_specs=VMEM if single else [VMEM] * len(shapes),
        scratch_shapes=list(scratch),
        compiler_params=pltpu.CompilerParams(vmem_limit_bytes=limit << 20),
        cost_estimate=pl.CostEstimate(flops=0, bytes_accessed=megabytes << 20, transcendentals=0),
    )


def attention_kernel(
    lengths, query_hbm, keys_hbm, values_hbm, new_keys_hbm, new_values_hbm, resid_hbm, routes_hbm, route_weight_hbm,
    out, query, keys, values, new_keys, new_values, resid, routes, route_weight, q_rows, a_rows, extra, sems,
):
    share = ROWS // PIECES
    copies = []

    def bring(source, target):
        copies.append(pltpu.make_async_copy(source, target, sems.at[len(copies)]))
        copies[-1].start()

    bring(query_hbm, query)
    for source, target in ((keys_hbm, keys), (values_hbm, values)):
        for c in range(PIECES):
            bring(source.at[pl.ds(c * share, share)], target.at[pl.ds(c * share, share)])
    for source, target in (
        (new_keys_hbm, new_keys),
        (new_values_hbm, new_values),
        (routes_hbm, routes),
        (route_weight_hbm, route_weight),
        (resid_hbm, resid),
    ):
        bring(source, target)
    copies[0].wait()
    for h in range(HEADS):
        q_rows[:, h, :] = query[:, h * HEAD_SIZE : (h + 1) * HEAD_SIZE].astype(F32)
    scale = 1.0 / math.sqrt(HEAD_SIZE)
    position = lax.broadcasted_iota(jnp.int32, (HEADS, POSITIONS), 1)
    scores = []
    for r in range(ROWS):
        if r % share == 0:
            copies[1 + r // share].wait()
        product = lax.dot_general(
            q_rows[r].astype(BF16), keys[r], (((1,), (1,)), ((), ())), preferred_element_type=F32
        )
        scores.append(jnp.where(position < lengths[r], product * scale, -jnp.inf))
    scores = jnp.stack(scores)
    for copy in copies[1 + 2 * PIECES :]:
        copy.wait()
    high = route_weight[...].astype(BF16)
    low = (route_weight[...] - high.astype(F32)).astype(BF16)
    pick = lax.rem(lax.broadcasted_iota(jnp.int32, (TOPK, LANES), 1), TOPK)
    spread = jnp.where(pick == lax.broadcasted_iota(jnp.int32, (TOPK, LANES), 0), 1.0, 0.0).astype(BF16)
    diagonal = lax.broadcasted_iota(jnp.int32, (ROWS, LANES), 1) // TOPK == lax.broadcasted_iota(
        jnp.int32, (ROWS, LANES), 0
    )
    lines = [jnp.zeros((1, LANES), F32)]
    for table in (routes[...].astype(F32).astype(BF16), high, low):
        wide = lax.dot_general(table, spread, (((0,), (0,)), ((), ())), preferred_element_type=F32)
        lines.insert(-1, jnp.sum(jnp.where(diagonal, wide, 0.0), axis=0, keepdims=True))
    for e in range(EXPERT):
        extra[e, 0:4, :] = resid[:, e * LANES : (e + 1) * LANES].astype(F32)
        for n, line in enumerate(lines):
            extra[e, 4 + n : 5 + n, :] = line
    out[:, SENT : SENT + MORE, :] = extra[...].astype(BF16)
    fresh = jnp.sum(q_rows[...] * new_keys[...].astype(F32)[:, None, :], axis=2, keepdims=True) * scale
    top = jnp.maximum(jnp.max(scores, axis=2, keepdims=True), fresh)
    expo = jnp.exp(scores - top)
    fresh_expo = jnp.exp(fresh - top)
    total = jnp.sum(expo, axis=2, keepdims=True) + fresh_expo
    weights = (expo / total).astype(BF16)
    fresh_weight = (fresh_expo / total).astype(BF16).astype(F32)
    added = fresh_weight * new_values[...].astype(F32)[:, None, :]
    for r in range(ROWS):
        if r % share == 0:
            copies[1 + PIECES + r // share].wait()
        a_rows[:, r, :] = jnp.dot(weights[r], values[r], preferred_element_type=F32) + added[r]
    for lo in range(Z_LO):
        heads = a_rows[SENT_HEADS * lo : SENT_HEADS * (lo + 1)].astype(BF16).reshape(SENT, HEAD_SIZE)
        for hi in range(Z_HI):
            out[hi * Z_LO + lo, 0:SENT, :] = heads


def project_kernel(gathered, own_weight, other_weight, out):
    heads = [gathered[:, h * ROWS : (h + 1) * ROWS, :].reshape(EXPERT * ROWS, HEAD_SIZE) for h in range(SENT_HEADS)]
    rows = jnp.concatenate(heads, axis=1)
    hi, lo, tp = (lax.axis_index(n) for n in ("zhi", "zlo", "tp"))
    extra = gathered[:, SENT : SENT + MORE, :].astype(F32)
    four = jnp.concatenate([extra[:, 0:4, :]] * 4, axis=1)
    line = lax.broadcasted_iota(jnp.int32, four.shape, 1)
    resid = jnp.where((line >= tp * 4) & (line < tp * 4 + 4), four, 0.0).reshape(EXPERT * ROWS, LANES)
    parts = (
        (lo, jnp.dot(rows, own_weight[lo], preferred_element_type=F32) + resid),
        (1 - lo, jnp.dot(rows, other_weight[...], preferred_element_type=F32)),
    )
    parity = lax.rem(hi, 2)
    for th, part in parts:
        part = part.astype(BF16)
        for h in range(2):
            for i in range(Z_LO):
                first = (h * Z_LO + i) * BLOCK
                out[i, pl.ds(th * 2 + (parity ^ h), 1), :, :] = part[None, first : first + BLOCK, :]


def reduce_kernel(parts, out):
    total = parts[0].astype(F32)
    for i in range(1, Z_LO * TP):
        total = total + parts[i].astype(F32)
    total = total.astype(BF16)
    for i in range(EXPERT):
        out[i] = total


def routing_kernel(gathered, choice, combine):
    mine = lax.axis_index(("zhi", "zlo"))
    extra = gathered[:, SENT : SENT + MORE, :].astype(F32)
    route, high, low = (extra[:, n, :] for n in (4, 5, 6))
    pick_row = lax.broadcasted_iota(jnp.int32, (LANES, EXPERT * ROWS), 0) // TOPK
    row = lax.rem(lax.broadcasted_iota(jnp.int32, (LANES, EXPERT * ROWS), 1), ROWS)
    here = jnp.where(pick_row == row, 1.0, 0.0).astype(BF16)
    earlier = jnp.where(pick_row < row, 1.0, 0.0).astype(BF16)
    hits = [jnp.where(route == (a * EXPERT + mine).astype(F32), 1.0, 0.0) for a in range(ATTN)]
    hit = jnp.concatenate(hits, axis=0)
    hit_high = jnp.concatenate([m * high for m in hits], axis=0)
    hit_low = jnp.concatenate([m * low for m in hits], axis=0)
    shape = (ATTN * EXPERT, EXPERT * ROWS)
    own = lax.rem(lax.broadcasted_iota(jnp.int32, shape, 0), EXPERT) == (
        lax.broadcasted_iota(jnp.int32, shape, 1) // ROWS
    )
    dot = lambda a, b: jnp.dot(a.astype(BF16), b, preferred_element_type=F32)
    named = jnp.where(own, dot(hit, here), 0.0)
    rank = dot(hit, earlier)
    weight_high = dot(hit_high, here)
    weight_low = dot(hit_low, here)
    chosen = [jnp.where(rank == float(s), named, 0.0) for s in range(CAP)]
    for s in range(CAP):
        choice[s] = chosen[s].astype(BF16)
    for n, weight in enumerate((weight_high, weight_low)):
        combine[n] = jnp.transpose(jnp.concatenate([c * weight for c in chosen], axis=0)).astype(BF16)


def select_kernel(choice, hidden, out):
    tl = lax.rem(lax.axis_index("tp"), 2)
    half = EXPERT * ROWS // 2
    groups = EXPERT // 2
    picks = []
    for s in range(CAP):
        whole = choice[s].astype(F32).reshape(ATTN, EXPERT, EXPERT * ROWS)
        for h in range(2):
            pick = whole[:, h * groups : (h + 1) * groups, h * half : (h + 1) * half]
            picks.append(pick.reshape(ATTN * groups, half).astype(BF16))
    for k in range(CHUNKS):
        blocks = [hidden[pl.ds((2 * k + (tl ^ h)) * Z_LO, Z_LO)].reshape(half, LANES) for h in range(2)]
        for s in range(CAP):
            sent = [
                jnp.dot(picks[2 * s + h], blocks[h], preferred_element_type=F32).reshape(ATTN, groups, LANES)
                for h in range(2)
            ]
            sent = jnp.concatenate(sent, axis=1).astype(BF16)
            for t in range(s, TP, CAP):
                out[:, t, :, k * LANES : (k + 1) * LANES] = sent


def expert_kernel(
    tokens, gain, gate_a, up_a, down_a, gate_b, gate_c, up_b, up_c, down_b, down_c, out, x, normed
):
    slots = ATTN * EXPERT
    square = jnp.zeros((slots, LANES), F32)
    early = lax.rem(lax.broadcasted_iota(jnp.int32, (slots, LANES), 0), EXPERT) < EXPERT // 2
    for k in range(CHUNKS):
        pieces = [
            tokens[:, t, :, k * LANES : (k + 1) * LANES].reshape(slots, LANES).astype(F32) for t in range(TP)
        ]
        for p in range(2):
            for th in range(2):
                c = 4 * k + 2 * p + th
                block = jnp.where(early, pieces[2 * th + p], pieces[2 * th + 1 - p])
                x[:, c * LANES : (c + 1) * LANES] = block
                square = square + block * block
    factor = lax.rsqrt(jnp.sum(square, axis=1, keepdims=True) * (1.0 / D) + 1e-06)
    normed[...] = (x[...] * factor * gain[...]).astype(BF16)
    rows = normed[...]
    turned = (((1,), (1,)), ((), ()))
    joined = lambda *refs: jnp.concatenate([r[...] for r in refs], axis=0)
    gate = lax.dot_general(joined(gate_a, gate_b, gate_c), rows, turned, preferred_element_type=F32)
    up = lax.dot_general(joined(up_a, up_b, up_c), rows, turned, preferred_element_type=F32)
    activated = jnp.transpose(gate / (1.0 + jnp.exp(-gate)) * up).astype(BF16)
    for k in range(CHUNKS):
        columns = slice(k * QUARTER, (k + 1) * QUARTER)
        down = jnp.concatenate([r[:, columns] for r in (down_a, down_b, down_c)], axis=0)
        part = jnp.dot(activated, down, preferred_element_type=F32)
        piece = lambda p, th: part[:, (2 * p + th) * LANES : (2 * p + th + 1) * LANES]
        for th in range(2):
            for tl in range(2):
                block = jnp.where(early, piece(tl, th), piece(1 - tl, th)).astype(BF16)
                out[:, 2 * th + tl, :, k * LANES : (k + 1) * LANES] = block.reshape(ATTN, EXPERT, LANES)


def combine_kernel(parts, combine, own, out, total, laid):
    mixed = jnp.zeros((EXPERT * ROWS, QUARTER), F32)
    for t in range(0, TP, CAP):
        block = jnp.concatenate([parts[:, t + s].reshape(ATTN * EXPERT, QUARTER) for s in range(CAP)], axis=0)
        for n in range(2):
            mixed = mixed + jnp.dot(combine[n], block, preferred_element_type=F32)
    for k in range(CHUNKS):
        total[k] = mixed[:, k * LANES : (k + 1) * LANES]
    hi, lo, tp = (lax.axis_index(n) for n in ("zhi", "zlo", "tp"))
    h = lax.rem(tp, 2) ^ lax.rem(hi, 2)
    rows = pl.ds(pl.multiple_of((h * Z_LO + lo) * BLOCK, BLOCK), BLOCK)
    k = lax.div(hi, 2)
    total[k, rows, :] = total[k, rows, :] + own[0].astype(F32)
    for n in range(EXPERT * TP):
        for k in range(CHUNKS):
            laid[n, k * 4 : (k + 1) * 4, :] = total[k, n * 4 : (n + 1) * 4, :]
    out[...] = laid[...].astype(BF16)


def finish_kernel(parts, out):
    totals = []
    for t in range(TP):
        total = parts[t].astype(F32)
        for e in range(1, EXPERT):
            total = total + parts[e * TP + t].astype(F32)
        totals.append(total)
    h = lax.div(lax.axis_index("zhi"), Z_HI // 2)
    for th in range(2):
        for tl in range(2):
            for k in range(CHUNKS):
                c = 4 * k + 2 * (tl ^ h) + th
                columns = pl.ds(pl.multiple_of(c * LANES, LANES), LANES)
                out[:, columns] = totals[2 * th + tl][k * 4 : (k + 1) * 4, :].astype(BF16)


def exchange(x, axes):
    return lax.all_to_all(x, axes, split_axis=0, concat_axis=0, tiled=True)


def shards(
    query,
    cached_key_store,
    cached_value_store,
    token_keys,
    token_values,
    lengths,
    out_weight,
    resid,
    norm_gain,
    routes,
    route_weight,
    w_gate,
    w_up,
    w_down,
):
    z = ("zhi", "zlo")
    z_lo = lax.axis_index("zlo")
    own_part = (w_gate[0].T, w_up[0].T, w_down[0])
    ring = {d: [(i, (i + d) % TP) for i in range(TP)] for d in (1, -1)}
    taken = [
        (lax.ppermute(w[: FF // 2], "tp", ring[-1]), lax.ppermute(w[FF // 2 :], "tp", ring[1])) for w in own_part
    ]
    halves = out_weight.reshape(Z_LO, D // Z_LO, LANES)
    other_weight = lax.ppermute(
        lax.dynamic_index_in_dim(halves, 1 - z_lo, 0, keepdims=False), "zlo", [(0, 1), (1, 0)]
    )
    sent = call(
        attention_kernel,
        [((EXPERT, SENT + MORE, LANES), BF16)],
        [SMEM] + [ANY] * 8,
        [
            pltpu.VMEM((ROWS, HEADS * HEAD_SIZE), BF16),
            pltpu.VMEM((ROWS, POSITIONS, HEAD_SIZE), BF16),
            pltpu.VMEM((ROWS, POSITIONS, HEAD_SIZE), BF16),
            pltpu.VMEM((ROWS, HEAD_SIZE), BF16),
            pltpu.VMEM((ROWS, HEAD_SIZE), BF16),
            pltpu.VMEM((ROWS // TP, D), BF16),
            pltpu.VMEM((TOPK, ROWS), jnp.int32),
            pltpu.VMEM((TOPK, ROWS), F32),
            pltpu.VMEM((ROWS, HEADS, HEAD_SIZE), F32),
            pltpu.VMEM((HEADS, ROWS, HEAD_SIZE), F32),
            pltpu.VMEM((EXPERT, MORE, LANES), F32),
            pltpu.SemaphoreType.DMA((2 * PIECES + 6,)),
        ],
        megabytes=16,
        limit=56,
    )(
        lengths, query, cached_key_store, cached_value_store,
        token_keys, token_values, resid, routes.T, route_weight.T,
    )
    sent, other_weight = lax.optimization_barrier((sent, other_weight))
    gathered = exchange(sent, z)
    parts = call(project_kernel, [((Z_LO, TP, BLOCK, LANES), BF16)], [VMEM] * 3)(
        gathered, halves, other_weight
    )
    parts, ups, gates = lax.optimization_barrier((parts, taken[1], taken[0]))
    parts = exchange(parts.reshape(Z_LO * TP, BLOCK, LANES), ("zlo", "tp"))
    own = call(reduce_kernel, [((EXPERT, BLOCK, LANES), BF16)], [VMEM])(parts)
    hidden = exchange(own, z)
    choice, combine = call(
        routing_kernel,
        [
            ((CAP, ATTN * EXPERT, EXPERT * ROWS), BF16),
            ((2, EXPERT * ROWS, CAP * ATTN * EXPERT), BF16),
        ],
        [VMEM],
    )(gathered)
    outgoing = call(select_kernel, [((ATTN, TP, EXPERT, QUARTER), BF16)], [VMEM, VMEM])(choice, hidden)
    outgoing, downs = lax.optimization_barrier((outgoing, taken[2]))
    incoming = exchange(outgoing.reshape(ATTN * TP, EXPERT, QUARTER), ("attn", "tp"))
    produced = call(
        expert_kernel,
        [((ATTN, TP, EXPERT, QUARTER), BF16)],
        [VMEM] * 11,
        [pltpu.VMEM((ATTN * EXPERT, D), F32), pltpu.VMEM((ATTN * EXPERT, D), BF16)],
    )(incoming.reshape(ATTN, TP, EXPERT, QUARTER), norm_gain.reshape(1, D), *own_part, *gates, *ups, *downs)
    returned = exchange(produced.reshape(ATTN * TP, EXPERT, QUARTER), ("attn", "tp"))
    weighted = call(
        combine_kernel,
        [((EXPERT * TP, ROWS, LANES), BF16)],
        [VMEM, VMEM, VMEM],
        [pltpu.VMEM((CHUNKS, EXPERT * ROWS, LANES), F32), pltpu.VMEM((EXPERT * TP, ROWS, LANES), F32)],
    )(returned.reshape(ATTN, TP, EXPERT, QUARTER), combine, own)
    back = exchange(weighted, (*z, "tp"))
    return call(finish_kernel, [((ROWS // TP, D), BF16)], [VMEM])(back)


def solution(mesh):
    fine = Mesh(mesh.devices.reshape(ATTN, Z_HI, Z_LO, TP), ("attn", "zhi", "zlo", "tp"))
    rows = ("attn", "zhi", "zlo")
    in_specs = (
        P(rows, "tp"),
        P(rows, None, "tp"),
        P(rows, None, "tp"),
        P(rows, "tp"),
        P(rows, "tp"),
        P(rows),
        P("tp", ("zhi", "zlo")),
        P((*rows, "tp"), None),
        P(),
        P(rows, None),
        P(rows, None),
        P(rows, None, "tp"),
        P(rows, None, "tp"),
        P(rows, "tp", None),
    )
    out_specs = P((*rows, "tp"), None)
    return jax.shard_map(shards, mesh=fine, in_specs=in_specs, out_specs=out_specs, check_vma=False)
```

time: 170 us -> 165 us (0.971)
  blocking collectives: 82.6 us -> 78 us
  waiting for transfers between devices: 19.6 us -> 22.7 us
  local copies, waits for them, and re-layouts: 7.92 us -> 5.38 us
    all_to_all x4, blocking collectives: 82.6 us -> 78 us  [exchange(): return lax.all_to_all(x, axes, split_axis=0, concat_axis=0, tiled=True)]
    ppermute x0 -> x1, starting transfers between devices: none -> 3.83 us  [shards(): lax.ppermute(lax.dynamic_index_in_dim(halves, 1 - z_lo, 0, keepdims=False...]
    unnamed x40 -> x18, local copies, waits for them, and re-layouts: 5.03 us -> 1.58 us
    all_to_all x3 -> x2, starting transfers between devices: 24.1 us -> 20.9 us  [exchange(): return lax.all_to_all(x, axes, split_axis=0, concat_axis=0, tiled=True)]
    ppermute x0 -> x1, waiting for transfers between devices: none -> 2.03 us  [shards(): lax.ppermute(lax.dynamic_index_in_dim(halves, 1 - z_lo, 0, keepdims=False...]
    all_to_all x3 -> x2, waiting for transfers between devices: 19.6 us -> 20.7 us  [exchange(): return lax.all_to_all(x, axes, split_axis=0, concat_axis=0, tiled=True)]
  transfers between devices with their start and end apart: 9 -> 9, of which waited for: 2 -> 3; matrix products, arithmetic and copies ran while one was open for 2% -> 2% of each run, Pallas kernels for 4% -> 3%
where the time goes in v4:
time: 165 us; the launch traced here: 163 us
  blocking collectives  78 us (47%)
  starting transfers between devices  45.8 us (28%)
  waiting for transfers between devices  22.7 us (14%)
  Pallas kernels  11.3 us (7%)
  local copies, waits for them, and re-layouts  5.38 us (3%)
    all_to_all x4, blocking collectives, exchange(): return lax.all_to_all(x, axes, split_axis=0, concat_axis=0, tiled=True)  78 us
    all_to_all x2, starting transfers between devices, exchange(): return lax.all_to_all(x, axes, split_axis=0, concat_axis=0, tiled=True)  20.9 us
    all_to_all x2, waiting for transfers between devices, exchange(): return lax.all_to_all(x, axes, split_axis=0, concat_axis=0, tiled=True)  20.7 us
    ppermute x3, starting transfers between devices, shards(): lax.ppermute(w[:FF // 2], 'tp', ring[-1])  13.2 us
    ppermute x3, starting transfers between devices, shards(): lax.ppermute(w[FF // 2:], 'tp', ring[1])  7.97 us
    pallas_call x1, Pallas kernels, shards(): call(attention_kernel, [((EXPERT, SENT + MORE, LANES), BF16)], [SMEM] + [...  4.24 us
    ppermute x1, starting transfers between devices, shards(): lax.ppermute(lax.dynamic_index_in_dim(halves, 1 - z_lo, 0, keepdims=False...  3.83 us
  transfers between devices with their start and end apart: 9, of which 3 were waited for; matrix products, arithmetic and copies ran while one was open for 2% of the time, Pallas kernels for 3%

profile of v4, /device:TPU:24, one launch (start us, length us, event | category | flops | bytes accessed | tf_op | source)
XLA Modules:
  0.0 163.4 jit_solution(4583384075423310544)
XLA Ops:
  0.0 1.0 dynamic-slice_bitcast_fusion
  1.0 3.8 %collective-permute-start = (bf16[1024,128]{1,0:T(8,128)(2,1)S(1)}, bf16[1024,128]{1,0:T(8,128)(2,1)S(1)}, u32[]{:S(2)}, u32[]{:S(2)}) collective-permute-start(bf16[1024,128]{1,0:T(8,128)(2,1)S(1)} %dynamic-slice_bitcast_fusion), channel_id=1, source_target_pairs={{0,4},{4,0},{1,5},{5,1},{2,6},{6,2},{3,7},{7,3},{8,12},{12,8},{9,1... | collective-permute-start | bytes 786440 | tf_op jit(solution)/shard_map/ppermute | solution.py:305
  4.8 4.2 %shard_map.136 = bf16[16,136,128]{2,1,0:T(8,128)(2,1)} custom-call(s32[16]{0:T(128)} %lengths.1, bf16[16,2048]{1,0:T(8,128)(2,1)} %query_hbm.1, bf16[16,128,128]{2,1,0:T(8,128)(2,1)} %keys_hbm.1, bf16[16,128,128]{2,1,0:T(8,128)(2,1)} %values_hbm.1, bf16[16,128]{1,0:T(8,128)(2,1)} %new_keys_hbm.1, bf16[16,128]{1,0:T(8,128)(2,1)} %new_values_hbm.1, ...), custom_call_target="tpu_custom_call" | custom-call | bytes 16777216 | tf_op jit(solution)/shard_map/pallas_call | solution.py:308
  9.1 2.0 %collective-permute-done.other_weight = bf16[1024,128]{1,0:T(8,128)(2,1)S(1)} collective-permute-done((bf16[1024,128]{1,0:T(8,128)(2,1)S(1)}, bf16[1024,128]{1,0:T(8,128)(2,1)S(1)}, u32[]{:S(2)}, u32[]{:S(2)}) %collective-permute-start) | collective-permute-done | bytes 262176 | tf_op jit(solution)/shard_map/ppermute | solution.py:305
  11.1 15.0 %all-to-all-start = ((bf16[16,136,128]{2,1,0:T(8,128)(2,1)}), bf16[16,136,128]{2,1,0:T(8,128)(2,1)S(1)}, u32[]{:S(2)}, u32[]{:S(2)}) async-start(bf16[16,136,128]{2,1,0:T(8,128)(2,1)} %shard_map.136), calls=%async_computation | async-start | bytes 1114112 | tf_op jit(solution)/shard_map/all_to_all | solution.py:278
  26.1 0.0 copy-start.1
  26.1 1.0 fusion
  27.1 3.4 %collective-permute-start.4 = (bf16[96,2048]{1,0:T(8,128)(2,1)}, bf16[96,2048]{1,0:T(8,128)(2,1)S(1)}, u32[]{:S(2)}, u32[]{:S(2)}) collective-permute-start(bf16[96,2048]{1,0:T(8,128)(2,1)} %get-tuple-element.31), channel_id=1, source_target_pairs={{0,1},{1,2},{2,3},{3,0},{4,5},{5,6},{6,7},{7,4},{8,9},{9,10},{10,1... | collective-permute-start | bytes 1179656 | tf_op jit(solution)/shard_map/ppermute | solution.py:302
  30.5 3.7 %collective-permute-start.3 = (bf16[96,2048]{1,0:T(8,128)(2,1)}, bf16[96,2048]{1,0:T(8,128)(2,1)}, u32[]{:S(2)}, u32[]{:S(2)}) collective-permute-start(bf16[96,2048]{1,0:T(8,128)(2,1)} %get-tuple-element.32), channel_id=1, source_target_pairs={{0,3},{1,0},{2,1},{3,2},{4,7},{5,4},{6,5},{7,6},{8,11},{9,8},{10,9... | collective-permute-start | bytes 1179656 | tf_op jit(solution)/shard_map/ppermute | solution.py:302
  34.2 0.0 copy-start.3
  34.2 0.9 fusion.1
  35.1 2.2 %collective-permute-start.2 = (bf16[96,2048]{1,0:T(8,128)(2,1)}, bf16[96,2048]{1,0:T(8,128)(2,1)}, u32[]{:S(2)}, u32[]{:S(2)}) collective-permute-start(bf16[96,2048]{1,0:T(8,128)(2,1)} %get-tuple-element.33), channel_id=1, source_target_pairs={{0,1},{1,2},{2,3},{3,0},{4,5},{5,6},{6,7},{7,4},{8,9},{9,10},{10,1... | collective-permute-start | bytes 1179656 | tf_op jit(solution)/shard_map/ppermute | solution.py:302
  37.3 4.9 %collective-permute-start.1 = (bf16[96,2048]{1,0:T(8,128)(2,1)}, bf16[96,2048]{1,0:T(8,128)(2,1)}, u32[]{:S(2)}, u32[]{:S(2)}) collective-permute-start(bf16[96,2048]{1,0:T(8,128)(2,1)} %get-tuple-element.34), channel_id=1, source_target_pairs={{0,3},{1,0},{2,1},{3,2},{4,7},{5,4},{6,5},{7,6},{8,11},{9,8},{10,9... | collective-permute-start | bytes 1179656 | tf_op jit(solution)/shard_map/ppermute | solution.py:302
  42.2 12.5 %all-to-all-done.gathered = bf16[16,136,128]{2,1,0:T(8,128)(2,1)S(1)} async-done(((bf16[16,136,128]{2,1,0:T(8,128)(2,1)}), bf16[16,136,128]{2,1,0:T(8,128)(2,1)S(1)}, u32[]{:S(2)}, u32[]{:S(2)}) %all-to-all-start) | async-done | bytes 557088 | tf_op jit(solution)/shard_map/all_to_all | solution.py:278
  54.7 0.4 shard_map.138
  55.2 12.8 %all_to_all.30.parts = bf16[8,64,128]{2,1,0:T(8,128)(2,1)S(1)} all-to-all(bf16[8,64,128]{2,1,0:T(8,128)(2,1)S(1)} %bitcast.33), channel_id=1, replica_groups=mesh['attn'=8,'zhi'=8,'zlo'=2,'tp'=4] {'zlo','tp'}, dimensions={0} | all-to-all | bytes 262144 | tf_op jit(solution)/shard_map/all_to_all | solution.py:278
  68.0 0.7 shard_map.139.own
  68.8 5.8 %all-to-all-start.2 = ((bf16[16,64,128]{2,1,0:T(8,128)(2,1)}), bf16[16,64,128]{2,1,0:T(8,128)(2,1)S(1)}, u32[]{:S(2)}, u32[]{:S(2)}) async-start(bf16[16,64,128]{2,1,0:T(8,128)(2,1)} %shard_map.139.own), calls=%async_computation.2 | async-start | bytes 524288 | tf_op jit(solution)/shard_map/all_to_all | solution.py:278
  74.6 0.9 slice_bitcast_fusion
  75.6 2.4 %collective-permute-start.6 = (bf16[96,2048]{1,0:T(8,128)(2,1)}, bf16[96,2048]{1,0:T(8,128)(2,1)}, u32[]{:S(2)}, u32[]{:S(2)}) collective-permute-start(bf16[96,2048]{1,0:T(8,128)(2,1)} %get-tuple-element.29), channel_id=1, source_target_pairs={{0,1},{1,2},{2,3},{3,0},{4,5},{5,6},{6,7},{7,4},{8,9},{9,10},{10,1... | collective-permute-start | bytes 1179656 | tf_op jit(solution)/shard_map/ppermute | solution.py:302
  78.0 4.6 %collective-permute-start.5 = (bf16[96,2048]{1,0:T(8,128)(2,1)}, bf16[96,2048]{1,0:T(8,128)(2,1)}, u32[]{:S(2)}, u32[]{:S(2)}) collective-permute-start(bf16[96,2048]{1,0:T(8,128)(2,1)} %get-tuple-element.30), channel_id=1, source_target_pairs={{0,3},{1,0},{2,1},{3,2},{4,7},{5,4},{6,5},{7,6},{8,11},{9,8},{10,9... | collective-permute-start | bytes 1179656 | tf_op jit(solution)/shard_map/ppermute | solution.py:302
  82.6 0.4 shard_map.137
  83.1 0.6 copy-done.6
  83.7 8.2 %all-to-all-done.2.hidden = bf16[16,64,128]{2,1,0:T(8,128)(2,1)S(1)} async-done(((bf16[16,64,128]{2,1,0:T(8,128)(2,1)}), bf16[16,64,128]{2,1,0:T(8,128)(2,1)S(1)}, u32[]{:S(2)}, u32[]{:S(2)}) %all-to-all-start.2) | async-done | bytes 262176 | tf_op jit(solution)/shard_map/all_to_all | solution.py:278
  91.9 0.9 copy-done.7
  92.8 0.3 shard_map.140
  93.1 15.2 %all_to_all.31 = bf16[32,16,512]{2,1,0:T(8,128)(2,1)S(1)} all-to-all(bf16[32,16,512]{2,1,0:T(8,128)(2,1)S(1)} %bitcast.27), channel_id=1, replica_groups=mesh['attn'=8,'zhi'=8,'zlo'=2,'tp'=4] {'attn','tp'}, dimensions={0} | all-to-all | bytes 1048576 | tf_op jit(solution)/shard_map/all_to_all | solution.py:278
  108.3 3.0 %shard_map.141 = bf16[8,4,16,512]{3,2,1,0:T(8,128)(2,1)S(1)} custom-call(bf16[8,4,16,512]{3,2,1,0:T(8,128)(2,1)S(1)} %bitcast.29, f32[1,2048]{1,0:T(1,128)S(1)} %bitcast.34, bf16[192,2048]{1,0:T(8,128)(2,1)S(1)} %bitcast.23, bf16[192,2048]{1,0:T(8,128)(2,1)S(1)} %bitcast.25, bf16[192,2048]{1,0:T(8,128)(2,1)S(1)} %bitcast.26, ...), custom_call_target="tpu_custom_call" | custom-call | bytes 4194304 | tf_op jit(solution)/shard_map/pallas_call | solution.py:352
  111.3 15.5 %all_to_all.32 = bf16[32,16,512]{2,1,0:T(8,128)(2,1)S(1)} all-to-all(bf16[32,16,512]{2,1,0:T(8,128)(2,1)S(1)} %bitcast.30), channel_id=1, replica_groups=mesh['attn'=8,'zhi'=8,'zlo'=2,'tp'=4] {'attn','tp'}, dimensions={0} | all-to-all | bytes 1048576 | tf_op jit(solution)/shard_map/all_to_all | solution.py:278
  126.9 1.5 shard_map.142
  128.4 34.4 %all_to_all.33.parts = bf16[64,16,128]{2,1,0:T(8,128)(2,1)S(1)} all-to-all(bf16[64,16,128]{2,1,0:T(8,128)(2,1)S(1)} %shard_map.142), channel_id=1, replica_groups=mesh['attn'=8,'zhi'=8,'zlo'=2,'tp'=4] {'zhi','zlo','tp'}, dimensions={0} | all-to-all | bytes 524288 | tf_op jit(solution)/shard_map/all_to_all | solution.py:278
  162.8 0.7 shard_map.143
  (20 shorter events, 0.1 us)
Async XLA Ops:
  1.0 10.1 %collective-permute-start = (bf16[1024,128]{1,0:T(8,128)(2,1)S(1)}, bf16[1024,128]{1,0:T(8,128)(2,1)S(1)}, u32[]{:S(2)}, u32[]{:S(2)}) collective-permute-start(bf16[1024,128]{1,0:T(8,128)(2,1)S(1)} %dynamic-slice_bitcast_fusion), channel_id=1, source_target_pairs={{0,4},{4,0},{1,5},{5,1},{2,6},{6,2},{3,7},{7,3},{8,12},{12,8},{9,1... | collective-permute-start | bytes 786440 | tf_op jit(solution)/shard_map/ppermute | solution.py:305
  9.1 17.1 %copy-start = (bf16[1,2048,192]{1,2,0:T(8,128)(2,1)S(1)}, bf16[1,2048,192]{1,2,0:T(8,128)(2,1)}, u32[]{:S(2)}) copy-start(bf16[1,2048,192]{1,2,0:T(8,128)(2,1)} %param.25) | copy-start | bytes 2359300
  11.1 43.6 %all-to-all-start = ((bf16[16,136,128]{2,1,0:T(8,128)(2,1)}), bf16[16,136,128]{2,1,0:T(8,128)(2,1)S(1)}, u32[]{:S(2)}, u32[]{:S(2)}) async-start(bf16[16,136,128]{2,1,0:T(8,128)(2,1)} %shard_map.136), calls=%async_computation | async-start | bytes 1114112 | tf_op jit(solution)/shard_map/all_to_all | solution.py:278
  26.1 8.0 %copy-start.1 = (bf16[1,2048,192]{1,2,0:T(8,128)(2,1)S(1)}, bf16[1,2048,192]{1,2,0:T(8,128)(2,1)}, u32[]{:S(2)}) copy-start(bf16[1,2048,192]{1,2,0:T(8,128)(2,1)} %param.26) | copy-start | bytes 2359300
  27.1 28.0 %collective-permute-start.4 = (bf16[96,2048]{1,0:T(8,128)(2,1)}, bf16[96,2048]{1,0:T(8,128)(2,1)S(1)}, u32[]{:S(2)}, u32[]{:S(2)}) collective-permute-start(bf16[96,2048]{1,0:T(8,128)(2,1)} %get-tuple-element.31), channel_id=1, source_target_pairs={{0,1},{1,2},{2,3},{3,0},{4,5},{5,6},{6,7},{7,4},{8,9},{9,10},{10,1... | collective-permute-start | bytes 1179656 | tf_op jit(solution)/shard_map/ppermute | solution.py:302
  30.5 24.7 %collective-permute-start.3 = (bf16[96,2048]{1,0:T(8,128)(2,1)}, bf16[96,2048]{1,0:T(8,128)(2,1)}, u32[]{:S(2)}, u32[]{:S(2)}) collective-permute-start(bf16[96,2048]{1,0:T(8,128)(2,1)} %get-tuple-element.32), channel_id=1, source_target_pairs={{0,3},{1,0},{2,1},{3,2},{4,7},{5,4},{6,5},{7,6},{8,11},{9,8},{10,9... | collective-permute-start | bytes 1179656 | tf_op jit(solution)/shard_map/ppermute | solution.py:302
  34.2 20.5 %copy-start.3 = (bf16[2048,128]{1,0:T(8,128)(2,1)S(1)}, bf16[2048,128]{1,0:T(8,128)(2,1)}, u32[]{:S(2)}) copy-start(bf16[2048,128]{1,0:T(8,128)(2,1)} %param.20) | copy-start | bytes 1572868
  35.1 20.1 %collective-permute-start.2 = (bf16[96,2048]{1,0:T(8,128)(2,1)}, bf16[96,2048]{1,0:T(8,128)(2,1)}, u32[]{:S(2)}, u32[]{:S(2)}) collective-permute-start(bf16[96,2048]{1,0:T(8,128)(2,1)} %get-tuple-element.33), channel_id=1, source_target_pairs={{0,1},{1,2},{2,3},{3,0},{4,5},{5,6},{6,7},{7,4},{8,9},{9,10},{10,1... | collective-permute-start | bytes 1179656 | tf_op jit(solution)/shard_map/ppermute | solution.py:302
  37.3 17.9 %collective-permute-start.1 = (bf16[96,2048]{1,0:T(8,128)(2,1)}, bf16[96,2048]{1,0:T(8,128)(2,1)}, u32[]{:S(2)}, u32[]{:S(2)}) collective-permute-start(bf16[96,2048]{1,0:T(8,128)(2,1)} %get-tuple-element.34), channel_id=1, source_target_pairs={{0,3},{1,0},{2,1},{3,2},{4,7},{5,4},{6,5},{7,6},{8,11},{9,8},{10,9... | collective-permute-start | bytes 1179656 | tf_op jit(solution)/shard_map/ppermute | solution.py:302
  55.1 19.5 %copy-start.2 = (bf16[1,192,2048]{2,1,0:T(8,128)(2,1)S(1)}, bf16[1,192,2048]{2,1,0:T(8,128)(2,1)}, u32[]{:S(2)}) copy-start(bf16[1,192,2048]{2,1,0:T(8,128)(2,1)} %param.27) | copy-start | bytes 2359300
  55.1 13.6 %copy-start.4 = (bf16[96,2048]{1,0:T(8,128)(2,1)}, bf16[96,2048]{1,0:T(8,128)(2,1)S(1)}, u32[]{:S(2)}) copy-start(bf16[96,2048]{1,0:T(8,128)(2,1)S(1)} %collective-permute-done.4.gate_c) | copy-start | bytes 1179652
  68.8 23.1 %all-to-all-start.2 = ((bf16[16,64,128]{2,1,0:T(8,128)(2,1)}), bf16[16,64,128]{2,1,0:T(8,128)(2,1)S(1)}, u32[]{:S(2)}, u32[]{:S(2)}) async-start(bf16[16,64,128]{2,1,0:T(8,128)(2,1)} %shard_map.139.own), calls=%async_computation.2 | async-start | bytes 524288 | tf_op jit(solution)/shard_map/all_to_all | solution.py:278
  75.6 17.5 %collective-permute-start.6 = (bf16[96,2048]{1,0:T(8,128)(2,1)}, bf16[96,2048]{1,0:T(8,128)(2,1)}, u32[]{:S(2)}, u32[]{:S(2)}) collective-permute-start(bf16[96,2048]{1,0:T(8,128)(2,1)} %get-tuple-element.29), channel_id=1, source_target_pairs={{0,1},{1,2},{2,3},{3,0},{4,5},{5,6},{6,7},{7,4},{8,9},{9,10},{10,1... | collective-permute-start | bytes 1179656 | tf_op jit(solution)/shard_map/ppermute | solution.py:302
  78.0 15.1 %collective-permute-start.5 = (bf16[96,2048]{1,0:T(8,128)(2,1)}, bf16[96,2048]{1,0:T(8,128)(2,1)}, u32[]{:S(2)}, u32[]{:S(2)}) collective-permute-start(bf16[96,2048]{1,0:T(8,128)(2,1)} %get-tuple-element.30), channel_id=1, source_target_pairs={{0,3},{1,0},{2,1},{3,2},{4,7},{5,4},{6,5},{7,6},{8,11},{9,8},{10,9... | collective-permute-start | bytes 1179656 | tf_op jit(solution)/shard_map/ppermute | solution.py:302
  83.1 0.6 copy-start.6
  91.9 0.9 copy-start.7
  93.1 15.2 %copy-start.5 = (bf16[96,2048]{1,0:T(8,128)(2,1)S(1)}, bf16[96,2048]{1,0:T(8,128)(2,1)}, u32[]{:S(2)}) copy-start(bf16[96,2048]{1,0:T(8,128)(2,1)} %copy-done.4) | copy-start | bytes 1179652
  93.1 15.2 %copy-start.8 = (f32[2048]{0:T(1024)S(1)}, f32[2048]{0:T(1024)}, u32[]{:S(2)}) copy-start(f32[2048]{0:T(1024)} %param.22) | copy-start | bytes 24580

commit v5 on v4

--- a/solution.py
+++ b/solution.py
@@ -145,16 +145,17 @@
                 out[i, pl.ds(th * 2 + (parity ^ h), 1), :, :] = part[None, first : first + BLOCK, :]
 
 
-def reduce_kernel(parts, out):
+def reduce_kernel(parts, own, out):
     total = parts[0].astype(F32)
     for i in range(1, Z_LO * TP):
         total = total + parts[i].astype(F32)
     total = total.astype(BF16)
+    own[...] = total
     for i in range(EXPERT):
         out[i] = total
 
 
-def routing_kernel(gathered, choice, combine):
+def routing_kernel(gathered, tables):
     mine = lax.axis_index(("zhi", "zlo"))
     extra = gathered[:, SENT : SENT + MORE, :].astype(F32)
     route, high, low = (extra[:, n, :] for n in (4, 5, 6))
@@ -176,19 +177,19 @@
     weight_high = dot(hit_high, here)
     weight_low = dot(hit_low, here)
     chosen = [jnp.where(rank == float(s), named, 0.0) for s in range(CAP)]
-    for s in range(CAP):
-        choice[s] = chosen[s].astype(BF16)
+    tables[0] = jnp.concatenate(chosen, axis=0).astype(BF16)
     for n, weight in enumerate((weight_high, weight_low)):
-        combine[n] = jnp.transpose(jnp.concatenate([c * weight for c in chosen], axis=0)).astype(BF16)
-
-
-def select_kernel(choice, hidden, out):
+        tables[1 + n] = jnp.transpose(jnp.concatenate([c * weight for c in chosen], axis=0)).astype(BF16)
+
+
+def select_kernel(tables, hidden, out):
     tl = lax.rem(lax.axis_index("tp"), 2)
     half = EXPERT * ROWS // 2
     groups = EXPERT // 2
     picks = []
     for s in range(CAP):
-        whole = choice[s].astype(F32).reshape(ATTN, EXPERT, EXPERT * ROWS)
+        whole = tables[0, s * ATTN * EXPERT : (s + 1) * ATTN * EXPERT].astype(F32)
+        whole = whole.reshape(ATTN, EXPERT, EXPERT * ROWS)
         for h in range(2):
             pick = whole[:, h * groups : (h + 1) * groups, h * half : (h + 1) * half]
             picks.append(pick.reshape(ATTN * groups, half).astype(BF16))
@@ -239,19 +240,19 @@
                 out[:, 2 * th + tl, :, k * LANES : (k + 1) * LANES] = block.reshape(ATTN, EXPERT, LANES)
 
 
-def combine_kernel(parts, combine, own, out, total, laid):
+def combine_kernel(parts, tables, own, out, total, laid):
     mixed = jnp.zeros((EXPERT * ROWS, QUARTER), F32)
     for t in range(0, TP, CAP):
         block = jnp.concatenate([parts[:, t + s].reshape(ATTN * EXPERT, QUARTER) for s in range(CAP)], axis=0)
         for n in range(2):
-            mixed = mixed + jnp.dot(combine[n], block, preferred_element_type=F32)
+            mixed = mixed + jnp.dot(tables[1 + n], block, preferred_element_type=F32)
     for k in range(CHUNKS):
         total[k] = mixed[:, k * LANES : (k + 1) * LANES]
     hi, lo, tp = (lax.axis_index(n) for n in ("zhi", "zlo", "tp"))
     h = lax.rem(tp, 2) ^ lax.rem(hi, 2)
     rows = pl.ds(pl.multiple_of((h * Z_LO + lo) * BLOCK, BLOCK), BLOCK)
     k = lax.div(hi, 2)
-    total[k, rows, :] = total[k, rows, :] + own[0].astype(F32)
+    total[k, rows, :] = total[k, rows, :] + own[...].astype(F32)
     for n in range(EXPERT * TP):
         for k in range(CHUNKS):
             laid[n, k * 4 : (k + 1) * 4, :] = total[k, n * 4 : (n + 1) * 4, :]
@@ -295,7 +296,6 @@
     w_down,
 ):
     z = ("zhi", "zlo")
-    z_lo = lax.axis_index("zlo")
     own_part = (w_gate[0].T, w_up[0].T, w_down[0])
     ring = {d: [(i, (i + d) % TP) for i in range(TP)] for d in (1, -1)}
     taken = [
@@ -303,7 +303,7 @@
     ]
     halves = out_weight.reshape(Z_LO, D // Z_LO, LANES)
     other_weight = lax.ppermute(
-        lax.dynamic_index_in_dim(halves, 1 - z_lo, 0, keepdims=False), "zlo", [(0, 1), (1, 0)]
+        lax.dynamic_index_in_dim(halves, 1 - lax.axis_index("zlo"), 0, keepdims=False), "zlo", [(0, 1), (1, 0)]
     )
     sent = call(
         attention_kernel,
@@ -336,17 +336,10 @@
     )
     parts, ups, gates = lax.optimization_barrier((parts, taken[1], taken[0]))
     parts = exchange(parts.reshape(Z_LO * TP, BLOCK, LANES), ("zlo", "tp"))
-    own = call(reduce_kernel, [((EXPERT, BLOCK, LANES), BF16)], [VMEM])(parts)
-    hidden = exchange(own, z)
-    choice, combine = call(
-        routing_kernel,
-        [
-            ((CAP, ATTN * EXPERT, EXPERT * ROWS), BF16),
-            ((2, EXPERT * ROWS, CAP * ATTN * EXPERT), BF16),
-        ],
-        [VMEM],
-    )(gathered)
-    outgoing = call(select_kernel, [((ATTN, TP, EXPERT, QUARTER), BF16)], [VMEM, VMEM])(choice, hidden)
+    own, spread = call(reduce_kernel, [((BLOCK, LANES), BF16), ((EXPERT, BLOCK, LANES), BF16)], [VMEM])(parts)
+    hidden = exchange(spread, z)
+    tables = call(routing_kernel, [((3, EXPERT * ROWS, CAP * ATTN * EXPERT), BF16)], [VMEM])(gathered)
+    outgoing = call(select_kernel, [((ATTN, TP, EXPERT, QUARTER), BF16)], [VMEM, VMEM])(tables, hidden)
     outgoing, downs = lax.optimization_barrier((outgoing, taken[2]))
     incoming = exchange(outgoing.reshape(ATTN * TP, EXPERT, QUARTER), ("attn", "tp"))
     produced = call(
@@ -361,7 +354,7 @@
         [((EXPERT * TP, ROWS, LANES), BF16)],
         [VMEM, VMEM, VMEM],
         [pltpu.VMEM((CHUNKS, EXPERT * ROWS, LANES), F32), pltpu.VMEM((EXPERT * TP, ROWS, LANES), F32)],
-    )(returned.reshape(ATTN, TP, EXPERT, QUARTER), combine, own)
+    )(returned.reshape(ATTN, TP, EXPERT, QUARTER), tables, own)
     back = exchange(weighted, (*z, "tp"))
     return call(finish_kernel, [((ROWS // TP, D), BF16)], [VMEM])(back)
 

time: 165 us -> 164 us (level)
  local copies, waits for them, and re-layouts: 5.38 us -> 3.68 us
  transfers between devices with their start and end apart: 9 -> 9, of which waited for: 3 -> 3; matrix products, arithmetic and copies ran while one was open for 2% -> 2% of each run, Pallas kernels for 3% -> 4%
where the time goes in v5:
time: 164 us; the launch traced here: 163 us
  blocking collectives  77.8 us (47%)
  starting transfers between devices  45.9 us (28%)
  waiting for transfers between devices  23.5 us (14%)
  Pallas kernels  11.5 us (7%)
  local copies, waits for them, and re-layouts  3.68 us (2%)
    all_to_all x4, blocking collectives, exchange(): return lax.all_to_all(x, axes, split_axis=0, concat_axis=0, tiled=True)  77.8 us
    all_to_all x2, waiting for transfers between devices, exchange(): return lax.all_to_all(x, axes, split_axis=0, concat_axis=0, tiled=True)  21.5 us
    all_to_all x2, starting transfers between devices, exchange(): return lax.all_to_all(x, axes, split_axis=0, concat_axis=0, tiled=True)  20.9 us
    ppermute x3, starting transfers between devices, shards(): lax.ppermute(w[:FF // 2], 'tp', ring[-1])  13.2 us
    ppermute x3, starting transfers between devices, shards(): lax.ppermute(w[FF // 2:], 'tp', ring[1])  7.97 us
    pallas_call x1, Pallas kernels, shards(): call(attention_kernel, [((EXPERT, SENT + MORE, LANES), BF16)], [SMEM] + [...  4.26 us
    ppermute x1, starting transfers between devices, shards(): lax.ppermute(lax.dynamic_index_in_dim(halves, 1 - lax.axis_index('zlo'),...  3.83 us
  transfers between devices with their start and end apart: 9, of which 3 were waited for; matrix products, arithmetic and copies ran while one was open for 2% of the time, Pallas kernels for 4%

profile of v5, /device:TPU:24, one launch (start us, length us, event | category | flops | bytes accessed | tf_op | source)
XLA Modules:
  0.0 162.6 jit_solution(1677094200354554171)
XLA Ops:
  0.0 1.0 dynamic-slice_bitcast_fusion
  1.0 3.8 %collective-permute-start = (bf16[1024,128]{1,0:T(8,128)(2,1)S(1)}, bf16[1024,128]{1,0:T(8,128)(2,1)S(1)}, u32[]{:S(2)}, u32[]{:S(2)}) collective-permute-start(bf16[1024,128]{1,0:T(8,128)(2,1)S(1)} %dynamic-slice_bitcast_fusion), channel_id=1, source_target_pairs={{0,4},{4,0},{1,5},{5,1},{2,6},{6,2},{3,7},{7,3},{8,12},{12,8},{9,1... | collective-permute-start | bytes 786440 | tf_op jit(solution)/shard_map/ppermute | solution.py:305
  4.8 4.3 %shard_map.136 = bf16[16,136,128]{2,1,0:T(8,128)(2,1)} custom-call(s32[16]{0:T(128)} %lengths.1, bf16[16,2048]{1,0:T(8,128)(2,1)} %query_hbm.1, bf16[16,128,128]{2,1,0:T(8,128)(2,1)} %keys_hbm.1, bf16[16,128,128]{2,1,0:T(8,128)(2,1)} %values_hbm.1, bf16[16,128]{1,0:T(8,128)(2,1)} %new_keys_hbm.1, bf16[16,128]{1,0:T(8,128)(2,1)} %new_values_hbm.1, ...), custom_call_target="tpu_custom_call" | custom-call | bytes 16777216 | tf_op jit(solution)/shard_map/pallas_call | solution.py:308
  9.1 0.0 copy-start
  9.1 2.0 %collective-permute-done.other_weight = bf16[1024,128]{1,0:T(8,128)(2,1)S(1)} collective-permute-done((bf16[1024,128]{1,0:T(8,128)(2,1)S(1)}, bf16[1024,128]{1,0:T(8,128)(2,1)S(1)}, u32[]{:S(2)}, u32[]{:S(2)}) %collective-permute-start) | collective-permute-done | bytes 262176 | tf_op jit(solution)/shard_map/ppermute | solution.py:305
  11.1 15.0 %all-to-all-start = ((bf16[16,136,128]{2,1,0:T(8,128)(2,1)}), bf16[16,136,128]{2,1,0:T(8,128)(2,1)S(1)}, u32[]{:S(2)}, u32[]{:S(2)}) async-start(bf16[16,136,128]{2,1,0:T(8,128)(2,1)} %shard_map.136), calls=%async_computation | async-start | bytes 1114112 | tf_op jit(solution)/shard_map/all_to_all | solution.py:279
  26.1 0.0 copy-start.1
  26.1 0.8 fusion
  27.0 3.4 %collective-permute-start.4 = (bf16[96,2048]{1,0:T(8,128)(2,1)}, bf16[96,2048]{1,0:T(8,128)(2,1)}, u32[]{:S(2)}, u32[]{:S(2)}) collective-permute-start(bf16[96,2048]{1,0:T(8,128)(2,1)} %get-tuple-element.31), channel_id=1, source_target_pairs={{0,1},{1,2},{2,3},{3,0},{4,5},{5,6},{6,7},{7,4},{8,9},{9,10},{10,1... | collective-permute-start | bytes 1179656 | tf_op jit(solution)/shard_map/ppermute | solution.py:302
  30.3 3.7 %collective-permute-start.3 = (bf16[96,2048]{1,0:T(8,128)(2,1)S(1)}, bf16[96,2048]{1,0:T(8,128)(2,1)}, u32[]{:S(2)}, u32[]{:S(2)}) collective-permute-start(bf16[96,2048]{1,0:T(8,128)(2,1)S(1)} %get-tuple-element.32), channel_id=1, source_target_pairs={{0,3},{1,0},{2,1},{3,2},{4,7},{5,4},{6,5},{7,6},{8,11},{9,8},{10,9... | collective-permute-start | bytes 1179656 | tf_op jit(solution)/shard_map/ppermute | solution.py:302
  34.0 0.0 copy-start.3
  34.0 0.9 fusion.1
  35.0 2.2 %collective-permute-start.2 = (bf16[96,2048]{1,0:T(8,128)(2,1)}, bf16[96,2048]{1,0:T(8,128)(2,1)}, u32[]{:S(2)}, u32[]{:S(2)}) collective-permute-start(bf16[96,2048]{1,0:T(8,128)(2,1)} %get-tuple-element.33), channel_id=1, source_target_pairs={{0,1},{1,2},{2,3},{3,0},{4,5},{5,6},{6,7},{7,4},{8,9},{9,10},{10,1... | collective-permute-start | bytes 1179656 | tf_op jit(solution)/shard_map/ppermute | solution.py:302
  37.1 4.9 %collective-permute-start.1 = (bf16[96,2048]{1,0:T(8,128)(2,1)}, bf16[96,2048]{1,0:T(8,128)(2,1)}, u32[]{:S(2)}, u32[]{:S(2)}) collective-permute-start(bf16[96,2048]{1,0:T(8,128)(2,1)} %get-tuple-element.34), channel_id=1, source_target_pairs={{0,3},{1,0},{2,1},{3,2},{4,7},{5,4},{6,5},{7,6},{8,11},{9,8},{10,9... | collective-permute-start | bytes 1179656 | tf_op jit(solution)/shard_map/ppermute | solution.py:302
  42.0 12.7 %all-to-all-done.gathered = bf16[16,136,128]{2,1,0:T(8,128)(2,1)S(1)} async-done(((bf16[16,136,128]{2,1,0:T(8,128)(2,1)}), bf16[16,136,128]{2,1,0:T(8,128)(2,1)S(1)}, u32[]{:S(2)}, u32[]{:S(2)}) %all-to-all-start) | async-done | bytes 557088 | tf_op jit(solution)/shard_map/all_to_all | solution.py:279
  54.7 0.4 shard_map.138
  55.2 12.8 %all_to_all.30.parts = bf16[8,64,128]{2,1,0:T(8,128)(2,1)S(1)} all-to-all(bf16[8,64,128]{2,1,0:T(8,128)(2,1)S(1)} %bitcast.33), channel_id=1, replica_groups=mesh['attn'=8,'zhi'=8,'zlo'=2,'tp'=4] {'zlo','tp'}, dimensions={0} | all-to-all | bytes 262144 | tf_op jit(solution)/shard_map/all_to_all | solution.py:279
  68.0 0.7 shard_map.139
  68.7 5.9 %all-to-all-start.2 = ((bf16[16,64,128]{2,1,0:T(8,128)(2,1)}), bf16[16,64,128]{2,1,0:T(8,128)(2,1)}, u32[]{:S(2)}, u32[]{:S(2)}) async-start(bf16[16,64,128]{2,1,0:T(8,128)(2,1)} %get-tuple-element.20), calls=%async_computation.2 | async-start | bytes 524288 | tf_op jit(solution)/shard_map/all_to_all | solution.py:279
  74.7 0.9 slice_bitcast_fusion
  75.6 2.4 %collective-permute-start.6 = (bf16[96,2048]{1,0:T(8,128)(2,1)}, bf16[96,2048]{1,0:T(8,128)(2,1)}, u32[]{:S(2)}, u32[]{:S(2)}) collective-permute-start(bf16[96,2048]{1,0:T(8,128)(2,1)} %get-tuple-element.29), channel_id=1, source_target_pairs={{0,1},{1,2},{2,3},{3,0},{4,5},{5,6},{6,7},{7,4},{8,9},{9,10},{10,1... | collective-permute-start | bytes 1179656 | tf_op jit(solution)/shard_map/ppermute | solution.py:302
  78.0 4.6 %collective-permute-start.5 = (bf16[96,2048]{1,0:T(8,128)(2,1)}, bf16[96,2048]{1,0:T(8,128)(2,1)}, u32[]{:S(2)}, u32[]{:S(2)}) collective-permute-start(bf16[96,2048]{1,0:T(8,128)(2,1)} %get-tuple-element.30), channel_id=1, source_target_pairs={{0,3},{1,0},{2,1},{3,2},{4,7},{5,4},{6,5},{7,6},{8,11},{9,8},{10,9... | collective-permute-start | bytes 1179656 | tf_op jit(solution)/shard_map/ppermute | solution.py:302
  82.6 0.4 shard_map.137.tables
  83.1 8.8 %all-to-all-done.2.hidden = bf16[16,64,128]{2,1,0:T(8,128)(2,1)} async-done(((bf16[16,64,128]{2,1,0:T(8,128)(2,1)}), bf16[16,64,128]{2,1,0:T(8,128)(2,1)}, u32[]{:S(2)}, u32[]{:S(2)}) %all-to-all-start.2) | async-done | bytes 262176 | tf_op jit(solution)/shard_map/all_to_all | solution.py:279
  91.9 1.2 shard_map.140
  93.2 0.0 copy-start.4
  93.2 15.0 %all_to_all.31 = bf16[32,16,512]{2,1,0:T(8,128)(2,1)S(1)} all-to-all(bf16[32,16,512]{2,1,0:T(8,128)(2,1)S(1)} %bitcast.28), channel_id=1, replica_groups=mesh['attn'=8,'zhi'=8,'zlo'=2,'tp'=4] {'attn','tp'}, dimensions={0} | all-to-all | bytes 1048576 | tf_op jit(solution)/shard_map/all_to_all | solution.py:279
  108.2 3.2 %shard_map.141 = bf16[8,4,16,512]{3,2,1,0:T(8,128)(2,1)S(1)} custom-call(bf16[8,4,16,512]{3,2,1,0:T(8,128)(2,1)S(1)} %bitcast.29, f32[1,2048]{1,0:T(1,128)S(1)} %bitcast.34, bf16[192,2048]{1,0:T(8,128)(2,1)S(1)} %bitcast.23, bf16[192,2048]{1,0:T(8,128)(2,1)S(1)} %bitcast.25, bf16[192,2048]{1,0:T(8,128)(2,1)S(1)} %bitcast.26, ...), custom_call_target="tpu_custom_call" | custom-call | bytes 4194304 | tf_op jit(solution)/shard_map/pallas_call | solution.py:345
  111.4 15.5 %all_to_all.32 = bf16[32,16,512]{2,1,0:T(8,128)(2,1)S(1)} all-to-all(bf16[32,16,512]{2,1,0:T(8,128)(2,1)S(1)} %bitcast.30), channel_id=1, replica_groups=mesh['attn'=8,'zhi'=8,'zlo'=2,'tp'=4] {'attn','tp'}, dimensions={0} | all-to-all | bytes 1048576 | tf_op jit(solution)/shard_map/all_to_all | solution.py:279
  126.9 0.6 shard_map.142
  127.5 34.4 %all_to_all.33.parts = bf16[64,16,128]{2,1,0:T(8,128)(2,1)S(1)} all-to-all(bf16[64,16,128]{2,1,0:T(8,128)(2,1)S(1)} %shard_map.142), channel_id=1, replica_groups=mesh['attn'=8,'zhi'=8,'zlo'=2,'tp'=4] {'zhi','zlo','tp'}, dimensions={0} | all-to-all | bytes 524288 | tf_op jit(solution)/shard_map/all_to_all | solution.py:279
  161.9 0.7 shard_map.143
  (12 shorter events, 0.0 us)
Async XLA Ops:
  1.0 10.1 %collective-permute-start = (bf16[1024,128]{1,0:T(8,128)(2,1)S(1)}, bf16[1024,128]{1,0:T(8,128)(2,1)S(1)}, u32[]{:S(2)}, u32[]{:S(2)}) collective-permute-start(bf16[1024,128]{1,0:T(8,128)(2,1)S(1)} %dynamic-slice_bitcast_fusion), channel_id=1, source_target_pairs={{0,4},{4,0},{1,5},{5,1},{2,6},{6,2},{3,7},{7,3},{8,12},{12,8},{9,1... | collective-permute-start | bytes 786440 | tf_op jit(solution)/shard_map/ppermute | solution.py:305
  9.1 17.0 %copy-start = (bf16[1,2048,192]{1,2,0:T(8,128)(2,1)S(1)}, bf16[1,2048,192]{1,2,0:T(8,128)(2,1)}, u32[]{:S(2)}) copy-start(bf16[1,2048,192]{1,2,0:T(8,128)(2,1)} %param.25) | copy-start | bytes 2359300
  11.1 43.6 %all-to-all-start = ((bf16[16,136,128]{2,1,0:T(8,128)(2,1)}), bf16[16,136,128]{2,1,0:T(8,128)(2,1)S(1)}, u32[]{:S(2)}, u32[]{:S(2)}) async-start(bf16[16,136,128]{2,1,0:T(8,128)(2,1)} %shard_map.136), calls=%async_computation | async-start | bytes 1114112 | tf_op jit(solution)/shard_map/all_to_all | solution.py:279
  26.1 7.9 %copy-start.1 = (bf16[1,2048,192]{1,2,0:T(8,128)(2,1)S(1)}, bf16[1,2048,192]{1,2,0:T(8,128)(2,1)}, u32[]{:S(2)}) copy-start(bf16[1,2048,192]{1,2,0:T(8,128)(2,1)} %param.26) | copy-start | bytes 2359300
  27.0 28.2 %collective-permute-start.4 = (bf16[96,2048]{1,0:T(8,128)(2,1)}, bf16[96,2048]{1,0:T(8,128)(2,1)}, u32[]{:S(2)}, u32[]{:S(2)}) collective-permute-start(bf16[96,2048]{1,0:T(8,128)(2,1)} %get-tuple-element.31), channel_id=1, source_target_pairs={{0,1},{1,2},{2,3},{3,0},{4,5},{5,6},{6,7},{7,4},{8,9},{9,10},{10,1... | collective-permute-start | bytes 1179656 | tf_op jit(solution)/shard_map/ppermute | solution.py:302
  30.3 24.8 %collective-permute-start.3 = (bf16[96,2048]{1,0:T(8,128)(2,1)S(1)}, bf16[96,2048]{1,0:T(8,128)(2,1)}, u32[]{:S(2)}, u32[]{:S(2)}) collective-permute-start(bf16[96,2048]{1,0:T(8,128)(2,1)S(1)} %get-tuple-element.32), channel_id=1, source_target_pairs={{0,3},{1,0},{2,1},{3,2},{4,7},{5,4},{6,5},{7,6},{8,11},{9,8},{10,9... | collective-permute-start | bytes 1179656 | tf_op jit(solution)/shard_map/ppermute | solution.py:302
  34.0 20.7 %copy-start.3 = (bf16[2048,128]{1,0:T(8,128)(2,1)S(1)}, bf16[2048,128]{1,0:T(8,128)(2,1)}, u32[]{:S(2)}) copy-start(bf16[2048,128]{1,0:T(8,128)(2,1)} %param.20) | copy-start | bytes 1572868
  35.0 20.2 %collective-permute-start.2 = (bf16[96,2048]{1,0:T(8,128)(2,1)}, bf16[96,2048]{1,0:T(8,128)(2,1)}, u32[]{:S(2)}, u32[]{:S(2)}) collective-permute-start(bf16[96,2048]{1,0:T(8,128)(2,1)} %get-tuple-element.33), channel_id=1, source_target_pairs={{0,1},{1,2},{2,3},{3,0},{4,5},{5,6},{6,7},{7,4},{8,9},{9,10},{10,1... | collective-permute-start | bytes 1179656 | tf_op jit(solution)/shard_map/ppermute | solution.py:302
  37.1 18.0 %collective-permute-start.1 = (bf16[96,2048]{1,0:T(8,128)(2,1)}, bf16[96,2048]{1,0:T(8,128)(2,1)}, u32[]{:S(2)}, u32[]{:S(2)}) collective-permute-start(bf16[96,2048]{1,0:T(8,128)(2,1)} %get-tuple-element.34), channel_id=1, source_target_pairs={{0,3},{1,0},{2,1},{3,2},{4,7},{5,4},{6,5},{7,6},{8,11},{9,8},{10,9... | collective-permute-start | bytes 1179656 | tf_op jit(solution)/shard_map/ppermute | solution.py:302
  55.1 19.5 %copy-start.2 = (bf16[1,192,2048]{2,1,0:T(8,128)(2,1)S(1)}, bf16[1,192,2048]{2,1,0:T(8,128)(2,1)}, u32[]{:S(2)}) copy-start(bf16[1,192,2048]{2,1,0:T(8,128)(2,1)} %param.27) | copy-start | bytes 2359300
  68.7 23.2 %all-to-all-start.2 = ((bf16[16,64,128]{2,1,0:T(8,128)(2,1)}), bf16[16,64,128]{2,1,0:T(8,128)(2,1)}, u32[]{:S(2)}, u32[]{:S(2)}) async-start(bf16[16,64,128]{2,1,0:T(8,128)(2,1)} %get-tuple-element.20), calls=%async_computation.2 | async-start | bytes 524288 | tf_op jit(solution)/shard_map/all_to_all | solution.py:279
  75.6 17.6 %collective-permute-start.6 = (bf16[96,2048]{1,0:T(8,128)(2,1)}, bf16[96,2048]{1,0:T(8,128)(2,1)}, u32[]{:S(2)}, u32[]{:S(2)}) collective-permute-start(bf16[96,2048]{1,0:T(8,128)(2,1)} %get-tuple-element.29), channel_id=1, source_target_pairs={{0,1},{1,2},{2,3},{3,0},{4,5},{5,6},{6,7},{7,4},{8,9},{9,10},{10,1... | collective-permute-start | bytes 1179656 | tf_op jit(solution)/shard_map/ppermute | solution.py:302
  78.0 15.2 %collective-permute-start.5 = (bf16[96,2048]{1,0:T(8,128)(2,1)}, bf16[96,2048]{1,0:T(8,128)(2,1)}, u32[]{:S(2)}, u32[]{:S(2)}) collective-permute-start(bf16[96,2048]{1,0:T(8,128)(2,1)} %get-tuple-element.30), channel_id=1, source_target_pairs={{0,3},{1,0},{2,1},{3,2},{4,7},{5,4},{6,5},{7,6},{8,11},{9,8},{10,9... | collective-permute-start | bytes 1179656 | tf_op jit(solution)/shard_map/ppermute | solution.py:302
  93.2 15.1 %copy-start.4 = (f32[2048]{0:T(1024)S(1)}, f32[2048]{0:T(1024)}, u32[]{:S(2)}) copy-start(f32[2048]{0:T(1024)} %param.22) | copy-start | bytes 24580

commit v6 on v5

--- a/solution.py
+++ b/solution.py
@@ -124,7 +124,7 @@
             out[hi * Z_LO + lo, 0:SENT, :] = heads
 
 
-def project_kernel(gathered, own_weight, other_weight, out):
+def project_kernel(gathered, own_weight, own_lines, other_lines, out, lines):
     heads = [gathered[:, h * ROWS : (h + 1) * ROWS, :].reshape(EXPERT * ROWS, HEAD_SIZE) for h in range(SENT_HEADS)]
     rows = jnp.concatenate(heads, axis=1)
     hi, lo, tp = (lax.axis_index(n) for n in ("zhi", "zlo", "tp"))
@@ -132,9 +132,13 @@
     four = jnp.concatenate([extra[:, 0:4, :]] * 4, axis=1)
     line = lax.broadcasted_iota(jnp.int32, four.shape, 1)
     resid = jnp.where((line >= tp * 4) & (line < tp * 4 + 4), four, 0.0).reshape(EXPERT * ROWS, LANES)
+    core = lax.rem(lax.axis_index("attn"), 2)
+    lines[pl.ds(core, 1)] = own_lines[...][None]
+    lines[pl.ds(1 - core, 1)] = other_lines[...][None]
+    other_weight = lines[...].reshape(D // Z_LO, LANES)
     parts = (
         (lo, jnp.dot(rows, own_weight[lo], preferred_element_type=F32) + resid),
-        (1 - lo, jnp.dot(rows, other_weight[...], preferred_element_type=F32)),
+        (1 - lo, jnp.dot(rows, other_weight, preferred_element_type=F32)),
     )
     parity = lax.rem(hi, 2)
     for th, part in parts:
@@ -155,7 +159,7 @@
         out[i] = total
 
 
-def routing_kernel(gathered, tables):
+def routing_kernel(gathered, picks, tables):
     mine = lax.axis_index(("zhi", "zlo"))
     extra = gathered[:, SENT : SENT + MORE, :].astype(F32)
     route, high, low = (extra[:, n, :] for n in (4, 5, 6))
@@ -177,27 +181,25 @@
     weight_high = dot(hit_high, here)
     weight_low = dot(hit_low, here)
     chosen = [jnp.where(rank == float(s), named, 0.0) for s in range(CAP)]
-    tables[0] = jnp.concatenate(chosen, axis=0).astype(BF16)
+    half = EXPERT * ROWS // 2
+    for s in range(CAP):
+        whole = chosen[s].reshape(ATTN, EXPERT, EXPERT * ROWS)
+        for h in range(2):
+            pick = whole[:, h * (EXPERT // 2) : (h + 1) * (EXPERT // 2), h * half : (h + 1) * half]
+            picks[s, h] = pick.reshape(half // 2, half).astype(BF16)
     for n, weight in enumerate((weight_high, weight_low)):
-        tables[1 + n] = jnp.transpose(jnp.concatenate([c * weight for c in chosen], axis=0)).astype(BF16)
-
-
-def select_kernel(tables, hidden, out):
+        tables[n] = jnp.transpose(jnp.concatenate([c * weight for c in chosen], axis=0)).astype(BF16)
+
+
+def select_kernel(picks, hidden, out):
     tl = lax.rem(lax.axis_index("tp"), 2)
     half = EXPERT * ROWS // 2
     groups = EXPERT // 2
-    picks = []
-    for s in range(CAP):
-        whole = tables[0, s * ATTN * EXPERT : (s + 1) * ATTN * EXPERT].astype(F32)
-        whole = whole.reshape(ATTN, EXPERT, EXPERT * ROWS)
-        for h in range(2):
-            pick = whole[:, h * groups : (h + 1) * groups, h * half : (h + 1) * half]
-            picks.append(pick.reshape(ATTN * groups, half).astype(BF16))
     for k in range(CHUNKS):
         blocks = [hidden[pl.ds((2 * k + (tl ^ h)) * Z_LO, Z_LO)].reshape(half, LANES) for h in range(2)]
         for s in range(CAP):
             sent = [
-                jnp.dot(picks[2 * s + h], blocks[h], preferred_element_type=F32).reshape(ATTN, groups, LANES)
+                jnp.dot(picks[s, h], blocks[h], preferred_element_type=F32).reshape(ATTN, groups, LANES)
                 for h in range(2)
             ]
             sent = jnp.concatenate(sent, axis=1).astype(BF16)
@@ -245,7 +247,7 @@
     for t in range(0, TP, CAP):
         block = jnp.concatenate([parts[:, t + s].reshape(ATTN * EXPERT, QUARTER) for s in range(CAP)], axis=0)
         for n in range(2):
-            mixed = mixed + jnp.dot(tables[1 + n], block, preferred_element_type=F32)
+            mixed = mixed + jnp.dot(tables[n], block, preferred_element_type=F32)
     for k in range(CHUNKS):
         total[k] = mixed[:, k * LANES : (k + 1) * LANES]
     hi, lo, tp = (lax.axis_index(n) for n in ("zhi", "zlo", "tp"))
@@ -302,9 +304,10 @@
         (lax.ppermute(w[: FF // 2], "tp", ring[-1]), lax.ppermute(w[FF // 2 :], "tp", ring[1])) for w in own_part
     ]
     halves = out_weight.reshape(Z_LO, D // Z_LO, LANES)
-    other_weight = lax.ppermute(
-        lax.dynamic_index_in_dim(halves, 1 - lax.axis_index("zlo"), 0, keepdims=False), "zlo", [(0, 1), (1, 0)]
-    )
+    quarters = out_weight.reshape(2 * Z_LO, D // Z_LO // 2, LANES)
+    core = lax.rem(lax.axis_index("attn"), 2)
+    mine = (1 - lax.axis_index("zlo")) * 2 + core
+    own_lines = lax.ppermute(lax.dynamic_index_in_dim(quarters, mine, 0, keepdims=False), "zlo", [(0, 1), (1, 0)])
     sent = call(
         attention_kernel,
         [((EXPERT, SENT + MORE, LANES), BF16)],
@@ -329,17 +332,25 @@
         lengths, query, cached_key_store, cached_value_store,
         token_keys, token_values, resid, routes.T, route_weight.T,
     )
-    sent, other_weight = lax.optimization_barrier((sent, other_weight))
+    sent, own_lines = lax.optimization_barrier((sent, own_lines))
+    other_lines = lax.ppermute(own_lines, "attn", [(i, i ^ 1) for i in range(ATTN)])
     gathered = exchange(sent, z)
-    parts = call(project_kernel, [((Z_LO, TP, BLOCK, LANES), BF16)], [VMEM] * 3)(
-        gathered, halves, other_weight
+    parts = call(project_kernel, [((Z_LO, TP, BLOCK, LANES), BF16)], [VMEM] * 4, [pltpu.VMEM((2, D // Z_LO // 2, LANES), BF16)])(
+        gathered, halves, own_lines, other_lines
     )
     parts, ups, gates = lax.optimization_barrier((parts, taken[1], taken[0]))
     parts = exchange(parts.reshape(Z_LO * TP, BLOCK, LANES), ("zlo", "tp"))
     own, spread = call(reduce_kernel, [((BLOCK, LANES), BF16), ((EXPERT, BLOCK, LANES), BF16)], [VMEM])(parts)
     hidden = exchange(spread, z)
-    tables = call(routing_kernel, [((3, EXPERT * ROWS, CAP * ATTN * EXPERT), BF16)], [VMEM])(gathered)
-    outgoing = call(select_kernel, [((ATTN, TP, EXPERT, QUARTER), BF16)], [VMEM, VMEM])(tables, hidden)
+    picks, tables = call(
+        routing_kernel,
+        [
+            ((CAP, 2, ATTN * EXPERT // 2, EXPERT * ROWS // 2), BF16),
+            ((2, EXPERT * ROWS, CAP * ATTN * EXPERT), BF16),
+        ],
+        [VMEM],
+    )(gathered)
+    outgoing = call(select_kernel, [((ATTN, TP, EXPERT, QUARTER), BF16)], [VMEM, VMEM])(picks, hidden)
     outgoing, downs = lax.optimization_barrier((outgoing, taken[2]))
     incoming = exchange(outgoing.reshape(ATTN * TP, EXPERT, QUARTER), ("attn", "tp"))
     produced = call(

time: 164 us -> 162 us (0.988)
  waiting for transfers between devices: 23.5 us -> 20.4 us
  Pallas kernels: 11.5 us -> 9.67 us
    all_to_all x2, waiting for transfers between devices: 21.5 us -> 19.1 us  [exchange(): return lax.all_to_all(x, axes, split_axis=0, concat_axis=0, tiled=True)]
    ppermute x1 -> x2, starting transfers between devices: 3.83 us -> 5.75 us  [the longest x1 3.83 us: shards(): lax.ppermute(lax.dynamic_index_in_dim(quarters, mine, 0, keepdims=False),...]
  transfers between devices with their start and end apart: 9 -> 10, of which waited for: 3 -> 3; matrix products, arithmetic and copies ran while one was open for 2% -> 2% of each run, Pallas kernels for 4% -> 3%
where the time goes in v6:
time: 162 us; the launch traced here: 160 us
  blocking collectives  78.3 us (48%)
  starting transfers between devices  47.2 us (29%)
  waiting for transfers between devices  20.4 us (13%)
  Pallas kernels  9.67 us (6%)
  local copies, waits for them, and re-layouts  4.49 us (3%)
    all_to_all x4, blocking collectives, exchange(): return lax.all_to_all(x, axes, split_axis=0, concat_axis=0, tiled=True)  78.3 us
    all_to_all x2, starting transfers between devices, exchange(): return lax.all_to_all(x, axes, split_axis=0, concat_axis=0, tiled=True)  20.4 us
    all_to_all x2, waiting for transfers between devices, exchange(): return lax.all_to_all(x, axes, split_axis=0, concat_axis=0, tiled=True)  19.1 us
    ppermute x3, starting transfers between devices, shards(): lax.ppermute(w[:FF // 2], 'tp', ring[-1])  13.2 us
    ppermute x3, starting transfers between devices, shards(): lax.ppermute(w[FF // 2:], 'tp', ring[1])  7.97 us
    pallas_call x1, Pallas kernels, shards(): call(attention_kernel, [((EXPERT, SENT + MORE, LANES), BF16)], [SMEM] + [...  4.25 us
    ppermute x1, starting transfers between devices, shards(): lax.ppermute(lax.dynamic_index_in_dim(quarters, mine, 0, keepdims=False),...  3.83 us
  transfers between devices with their start and end apart: 10, of which 3 were waited for; matrix products, arithmetic and copies ran while one was open for 2% of the time, Pallas kernels for 3%

profile of v6, /device:TPU:24, one launch (start us, length us, event | category | flops | bytes accessed | tf_op | source)
XLA Modules:
  0.0 160.5 jit_solution(11041326904462381300)
XLA Ops:
  0.0 0.9 dynamic-slice_bitcast_fusion
  0.9 3.8 %collective-permute-start = (bf16[512,128]{1,0:T(8,128)(2,1)S(1)}, bf16[512,128]{1,0:T(8,128)(2,1)S(1)}, u32[]{:S(2)}, u32[]{:S(2)}) collective-permute-start(bf16[512,128]{1,0:T(8,128)(2,1)S(1)} %dynamic-slice_bitcast_fusion), channel_id=1, source_target_pairs={{0,4},{4,0},{1,5},{5,1},{2,6},{6,2},{3,7},{7,3},{8,12},{12,8},{9,1... | collective-permute-start | bytes 393224 | tf_op jit(solution)/shard_map/ppermute | solution.py:310
  4.8 4.3 %shard_map.136 = bf16[16,136,128]{2,1,0:T(8,128)(2,1)} custom-call(s32[16]{0:T(128)} %lengths.1, bf16[16,2048]{1,0:T(8,128)(2,1)} %query_hbm.1, bf16[16,128,128]{2,1,0:T(8,128)(2,1)} %keys_hbm.1, bf16[16,128,128]{2,1,0:T(8,128)(2,1)} %values_hbm.1, bf16[16,128]{1,0:T(8,128)(2,1)} %new_keys_hbm.1, bf16[16,128]{1,0:T(8,128)(2,1)} %new_values_hbm.1, ...), custom_call_target="tpu_custom_call" | custom-call | bytes 16777216 | tf_op jit(solution)/shard_map/pallas_call | solution.py:311
  9.0 0.0 copy-start
  9.0 14.4 %all-to-all-start = ((bf16[16,136,128]{2,1,0:T(8,128)(2,1)}), bf16[16,136,128]{2,1,0:T(8,128)(2,1)S(1)}, u32[]{:S(2)}, u32[]{:S(2)}) async-start(bf16[16,136,128]{2,1,0:T(8,128)(2,1)} %shard_map.136), calls=%async_computation | async-start | bytes 1114112 | tf_op jit(solution)/shard_map/all_to_all | solution.py:281
  23.5 0.0 copy-start.1
  23.5 1.0 fusion
  24.5 3.4 %collective-permute-start.5 = (bf16[96,2048]{1,0:T(8,128)(2,1)}, bf16[96,2048]{1,0:T(8,128)(2,1)S(1)}, u32[]{:S(2)}, u32[]{:S(2)}) collective-permute-start(bf16[96,2048]{1,0:T(8,128)(2,1)} %get-tuple-element.35), channel_id=1, source_target_pairs={{0,1},{1,2},{2,3},{3,0},{4,5},{5,6},{6,7},{7,4},{8,9},{9,10},{10,1... | collective-permute-start | bytes 1179656 | tf_op jit(solution)/shard_map/ppermute | solution.py:304
  27.9 3.7 %collective-permute-start.4 = (bf16[96,2048]{1,0:T(8,128)(2,1)}, bf16[96,2048]{1,0:T(8,128)(2,1)}, u32[]{:S(2)}, u32[]{:S(2)}) collective-permute-start(bf16[96,2048]{1,0:T(8,128)(2,1)} %get-tuple-element.36), channel_id=1, source_target_pairs={{0,3},{1,0},{2,1},{3,2},{4,7},{5,4},{6,5},{7,6},{8,11},{9,8},{10,9... | collective-permute-start | bytes 1179656 | tf_op jit(solution)/shard_map/ppermute | solution.py:304
  31.5 0.0 copy-start.3
  31.5 0.9 fusion.1
  32.5 2.2 %collective-permute-start.3 = (bf16[96,2048]{1,0:T(8,128)(2,1)}, bf16[96,2048]{1,0:T(8,128)(2,1)}, u32[]{:S(2)}, u32[]{:S(2)}) collective-permute-start(bf16[96,2048]{1,0:T(8,128)(2,1)} %get-tuple-element.37), channel_id=1, source_target_pairs={{0,1},{1,2},{2,3},{3,0},{4,5},{5,6},{6,7},{7,4},{8,9},{9,10},{10,1... | collective-permute-start | bytes 1179656 | tf_op jit(solution)/shard_map/ppermute | solution.py:304
  34.7 4.9 %collective-permute-start.2 = (bf16[96,2048]{1,0:T(8,128)(2,1)}, bf16[96,2048]{1,0:T(8,128)(2,1)}, u32[]{:S(2)}, u32[]{:S(2)}) collective-permute-start(bf16[96,2048]{1,0:T(8,128)(2,1)} %get-tuple-element.38), channel_id=1, source_target_pairs={{0,3},{1,0},{2,1},{3,2},{4,7},{5,4},{6,5},{7,6},{8,11},{9,8},{10,9... | collective-permute-start | bytes 1179656 | tf_op jit(solution)/shard_map/ppermute | solution.py:304
  39.5 1.9 %collective-permute-start.1 = (bf16[512,128]{1,0:T(8,128)(2,1)S(1)}, bf16[512,128]{1,0:T(8,128)(2,1)S(1)}, u32[]{:S(2)}, u32[]{:S(2)}) collective-permute-start(bf16[512,128]{1,0:T(8,128)(2,1)S(1)} %collective-permute-done.own_lines), channel_id=1, source_target_pairs={{0,64},{64,0},{128,192},{192,128},{256,320},{320,256},{384,448},{4... | collective-permute-start | bytes 393224 | tf_op jit(solution)/shard_map/ppermute | solution.py:336
  41.5 1.3 collective-permute-done.1.other_lines
  42.8 10.3 %all-to-all-done.gathered = bf16[16,136,128]{2,1,0:T(8,128)(2,1)S(1)} async-done(((bf16[16,136,128]{2,1,0:T(8,128)(2,1)}), bf16[16,136,128]{2,1,0:T(8,128)(2,1)S(1)}, u32[]{:S(2)}, u32[]{:S(2)}) %all-to-all-start) | async-done | bytes 557088 | tf_op jit(solution)/shard_map/all_to_all | solution.py:281
  53.1 0.4 shard_map.138
  53.6 12.3 %all_to_all.30.parts = bf16[8,64,128]{2,1,0:T(8,128)(2,1)S(1)} all-to-all(bf16[8,64,128]{2,1,0:T(8,128)(2,1)S(1)} %bitcast.34), channel_id=1, replica_groups=mesh['attn'=8,'zhi'=8,'zlo'=2,'tp'=4] {'zlo','tp'}, dimensions={0} | all-to-all | bytes 262144 | tf_op jit(solution)/shard_map/all_to_all | solution.py:281
  66.0 0.7 copy-done.6
  66.7 5.9 %all-to-all-start.2 = ((bf16[16,64,128]{2,1,0:T(8,128)(2,1)}), bf16[16,64,128]{2,1,0:T(8,128)(2,1)S(1)}, u32[]{:S(2)}, u32[]{:S(2)}) async-start(bf16[16,64,128]{2,1,0:T(8,128)(2,1)} %copy-done.6), calls=%async_computation.2 | async-start | bytes 524288 | tf_op jit(solution)/shard_map/all_to_all | solution.py:281
  72.6 1.0 slice_bitcast_fusion
  73.5 2.4 %collective-permute-start.7 = (bf16[96,2048]{1,0:T(8,128)(2,1)}, bf16[96,2048]{1,0:T(8,128)(2,1)}, u32[]{:S(2)}, u32[]{:S(2)}) collective-permute-start(bf16[96,2048]{1,0:T(8,128)(2,1)} %get-tuple-element.33), channel_id=1, source_target_pairs={{0,1},{1,2},{2,3},{3,0},{4,5},{5,6},{6,7},{7,4},{8,9},{9,10},{10,1... | collective-permute-start | bytes 1179656 | tf_op jit(solution)/shard_map/ppermute | solution.py:304
  76.0 4.6 %collective-permute-start.6 = (bf16[96,2048]{1,0:T(8,128)(2,1)}, bf16[96,2048]{1,0:T(8,128)(2,1)}, u32[]{:S(2)}, u32[]{:S(2)}) collective-permute-start(bf16[96,2048]{1,0:T(8,128)(2,1)} %get-tuple-element.34), channel_id=1, source_target_pairs={{0,3},{1,0},{2,1},{3,2},{4,7},{5,4},{6,5},{7,6},{8,11},{9,8},{10,9... | collective-permute-start | bytes 1179656 | tf_op jit(solution)/shard_map/ppermute | solution.py:304
  80.6 0.4 shard_map.137
  81.0 8.8 %all-to-all-done.2.hidden = bf16[16,64,128]{2,1,0:T(8,128)(2,1)S(1)} async-done(((bf16[16,64,128]{2,1,0:T(8,128)(2,1)}), bf16[16,64,128]{2,1,0:T(8,128)(2,1)S(1)}, u32[]{:S(2)}, u32[]{:S(2)}) %all-to-all-start.2) | async-done | bytes 262176 | tf_op jit(solution)/shard_map/all_to_all | solution.py:281
  89.8 0.3 shard_map.140
  90.1 15.2 %all_to_all.31 = bf16[32,16,512]{2,1,0:T(8,128)(2,1)S(1)} all-to-all(bf16[32,16,512]{2,1,0:T(8,128)(2,1)S(1)} %bitcast.28), channel_id=1, replica_groups=mesh['attn'=8,'zhi'=8,'zlo'=2,'tp'=4] {'attn','tp'}, dimensions={0} | all-to-all | bytes 1048576 | tf_op jit(solution)/shard_map/all_to_all | solution.py:281
  105.3 3.0 %shard_map.141 = bf16[8,4,16,512]{3,2,1,0:T(8,128)(2,1)S(1)} custom-call(bf16[8,4,16,512]{3,2,1,0:T(8,128)(2,1)S(1)} %bitcast.30, f32[1,2048]{1,0:T(1,128)S(1)} %bitcast.35, bf16[192,2048]{1,0:T(8,128)(2,1)S(1)} %bitcast.24, bf16[192,2048]{1,0:T(8,128)(2,1)S(1)} %bitcast.26, bf16[192,2048]{1,0:T(8,128)(2,1)S(1)} %bitcast.27, ...), custom_call_target="tpu_custom_call" | custom-call | bytes 4194304 | tf_op jit(solution)/shard_map/pallas_call | solution.py:356
  108.4 15.5 %all_to_all.32 = bf16[32,16,512]{2,1,0:T(8,128)(2,1)S(1)} all-to-all(bf16[32,16,512]{2,1,0:T(8,128)(2,1)S(1)} %bitcast.31), channel_id=1, replica_groups=mesh['attn'=8,'zhi'=8,'zlo'=2,'tp'=4] {'attn','tp'}, dimensions={0} | all-to-all | bytes 1048576 | tf_op jit(solution)/shard_map/all_to_all | solution.py:281
  123.9 0.6 shard_map.142
  124.5 35.3 %all_to_all.33.parts = bf16[64,16,128]{2,1,0:T(8,128)(2,1)S(1)} all-to-all(bf16[64,16,128]{2,1,0:T(8,128)(2,1)S(1)} %shard_map.142), channel_id=1, replica_groups=mesh['attn'=8,'zhi'=8,'zlo'=2,'tp'=4] {'zhi','zlo','tp'}, dimensions={0} | all-to-all | bytes 524288 | tf_op jit(solution)/shard_map/all_to_all | solution.py:281
  159.8 0.7 shard_map.143
  (20 shorter events, 0.1 us)
Async XLA Ops:
  0.9 8.1 %collective-permute-start = (bf16[512,128]{1,0:T(8,128)(2,1)S(1)}, bf16[512,128]{1,0:T(8,128)(2,1)S(1)}, u32[]{:S(2)}, u32[]{:S(2)}) collective-permute-start(bf16[512,128]{1,0:T(8,128)(2,1)S(1)} %dynamic-slice_bitcast_fusion), channel_id=1, source_target_pairs={{0,4},{4,0},{1,5},{5,1},{2,6},{6,2},{3,7},{7,3},{8,12},{12,8},{9,1... | collective-permute-start | bytes 393224 | tf_op jit(solution)/shard_map/ppermute | solution.py:310
  9.0 14.5 %copy-start = (bf16[1,2048,192]{1,2,0:T(8,128)(2,1)S(1)}, bf16[1,2048,192]{1,2,0:T(8,128)(2,1)}, u32[]{:S(2)}) copy-start(bf16[1,2048,192]{1,2,0:T(8,128)(2,1)} %param.25) | copy-start | bytes 2359300
  9.0 44.1 %all-to-all-start = ((bf16[16,136,128]{2,1,0:T(8,128)(2,1)}), bf16[16,136,128]{2,1,0:T(8,128)(2,1)S(1)}, u32[]{:S(2)}, u32[]{:S(2)}) async-start(bf16[16,136,128]{2,1,0:T(8,128)(2,1)} %shard_map.136), calls=%async_computation | async-start | bytes 1114112 | tf_op jit(solution)/shard_map/all_to_all | solution.py:281
  23.5 8.0 %copy-start.1 = (bf16[1,2048,192]{1,2,0:T(8,128)(2,1)S(1)}, bf16[1,2048,192]{1,2,0:T(8,128)(2,1)}, u32[]{:S(2)}) copy-start(bf16[1,2048,192]{1,2,0:T(8,128)(2,1)} %param.26) | copy-start | bytes 2359300
  24.5 29.1 %collective-permute-start.5 = (bf16[96,2048]{1,0:T(8,128)(2,1)}, bf16[96,2048]{1,0:T(8,128)(2,1)S(1)}, u32[]{:S(2)}, u32[]{:S(2)}) collective-permute-start(bf16[96,2048]{1,0:T(8,128)(2,1)} %get-tuple-element.35), channel_id=1, source_target_pairs={{0,1},{1,2},{2,3},{3,0},{4,5},{5,6},{6,7},{7,4},{8,9},{9,10},{10,1... | collective-permute-start | bytes 1179656 | tf_op jit(solution)/shard_map/ppermute | solution.py:304
  27.9 25.7 %collective-permute-start.4 = (bf16[96,2048]{1,0:T(8,128)(2,1)}, bf16[96,2048]{1,0:T(8,128)(2,1)}, u32[]{:S(2)}, u32[]{:S(2)}) collective-permute-start(bf16[96,2048]{1,0:T(8,128)(2,1)} %get-tuple-element.36), channel_id=1, source_target_pairs={{0,3},{1,0},{2,1},{3,2},{4,7},{5,4},{6,5},{7,6},{8,11},{9,8},{10,9... | collective-permute-start | bytes 1179656 | tf_op jit(solution)/shard_map/ppermute | solution.py:304
  31.5 21.6 %copy-start.3 = (bf16[2048,128]{1,0:T(8,128)(2,1)S(1)}, bf16[2048,128]{1,0:T(8,128)(2,1)}, u32[]{:S(2)}) copy-start(bf16[2048,128]{1,0:T(8,128)(2,1)} %param.20) | copy-start | bytes 1572868
  32.5 21.1 %collective-permute-start.3 = (bf16[96,2048]{1,0:T(8,128)(2,1)}, bf16[96,2048]{1,0:T(8,128)(2,1)}, u32[]{:S(2)}, u32[]{:S(2)}) collective-permute-start(bf16[96,2048]{1,0:T(8,128)(2,1)} %get-tuple-element.37), channel_id=1, source_target_pairs={{0,1},{1,2},{2,3},{3,0},{4,5},{5,6},{6,7},{7,4},{8,9},{9,10},{10,1... | collective-permute-start | bytes 1179656 | tf_op jit(solution)/shard_map/ppermute | solution.py:304
  34.7 18.9 %collective-permute-start.2 = (bf16[96,2048]{1,0:T(8,128)(2,1)}, bf16[96,2048]{1,0:T(8,128)(2,1)}, u32[]{:S(2)}, u32[]{:S(2)}) collective-permute-start(bf16[96,2048]{1,0:T(8,128)(2,1)} %get-tuple-element.38), channel_id=1, source_target_pairs={{0,3},{1,0},{2,1},{3,2},{4,7},{5,4},{6,5},{7,6},{8,11},{9,8},{10,9... | collective-permute-start | bytes 1179656 | tf_op jit(solution)/shard_map/ppermute | solution.py:304
  39.5 3.2 %collective-permute-start.1 = (bf16[512,128]{1,0:T(8,128)(2,1)S(1)}, bf16[512,128]{1,0:T(8,128)(2,1)S(1)}, u32[]{:S(2)}, u32[]{:S(2)}) collective-permute-start(bf16[512,128]{1,0:T(8,128)(2,1)S(1)} %collective-permute-done.own_lines), channel_id=1, source_target_pairs={{0,64},{64,0},{128,192},{192,128},{256,320},{320,256},{384,448},{4... | collective-permute-start | bytes 393224 | tf_op jit(solution)/shard_map/ppermute | solution.py:336
  53.5 19.0 %copy-start.2 = (bf16[1,192,2048]{2,1,0:T(8,128)(2,1)S(1)}, bf16[1,192,2048]{2,1,0:T(8,128)(2,1)}, u32[]{:S(2)}) copy-start(bf16[1,192,2048]{2,1,0:T(8,128)(2,1)} %param.27) | copy-start | bytes 2359300
  53.6 13.1 %copy-start.4 = (bf16[96,2048]{1,0:T(8,128)(2,1)}, bf16[96,2048]{1,0:T(8,128)(2,1)S(1)}, u32[]{:S(2)}) copy-start(bf16[96,2048]{1,0:T(8,128)(2,1)S(1)} %collective-permute-done.5.gate_c) | copy-start | bytes 1179652
  65.9 0.7 copy-start.6
  66.7 23.2 %all-to-all-start.2 = ((bf16[16,64,128]{2,1,0:T(8,128)(2,1)}), bf16[16,64,128]{2,1,0:T(8,128)(2,1)S(1)}, u32[]{:S(2)}, u32[]{:S(2)}) async-start(bf16[16,64,128]{2,1,0:T(8,128)(2,1)} %copy-done.6), calls=%async_computation.2 | async-start | bytes 524288 | tf_op jit(solution)/shard_map/all_to_all | solution.py:281
  73.5 16.6 %collective-permute-start.7 = (bf16[96,2048]{1,0:T(8,128)(2,1)}, bf16[96,2048]{1,0:T(8,128)(2,1)}, u32[]{:S(2)}, u32[]{:S(2)}) collective-permute-start(bf16[96,2048]{1,0:T(8,128)(2,1)} %get-tuple-element.33), channel_id=1, source_target_pairs={{0,1},{1,2},{2,3},{3,0},{4,5},{5,6},{6,7},{7,4},{8,9},{9,10},{10,1... | collective-permute-start | bytes 1179656 | tf_op jit(solution)/shard_map/ppermute | solution.py:304
  76.0 14.2 %collective-permute-start.6 = (bf16[96,2048]{1,0:T(8,128)(2,1)}, bf16[96,2048]{1,0:T(8,128)(2,1)}, u32[]{:S(2)}, u32[]{:S(2)}) collective-permute-start(bf16[96,2048]{1,0:T(8,128)(2,1)} %get-tuple-element.34), channel_id=1, source_target_pairs={{0,3},{1,0},{2,1},{3,2},{4,7},{5,4},{6,5},{7,6},{8,11},{9,8},{10,9... | collective-permute-start | bytes 1179656 | tf_op jit(solution)/shard_map/ppermute | solution.py:304
  90.1 15.2 %copy-start.5 = (bf16[96,2048]{1,0:T(8,128)(2,1)S(1)}, bf16[96,2048]{1,0:T(8,128)(2,1)}, u32[]{:S(2)}) copy-start(bf16[96,2048]{1,0:T(8,128)(2,1)} %copy-done.4) | copy-start | bytes 1179652
  90.1 15.2 %copy-start.7 = (f32[2048]{0:T(1024)S(1)}, f32[2048]{0:T(1024)}, u32[]{:S(2)}) copy-start(f32[2048]{0:T(1024)} %param.22) | copy-start | bytes 24580

commit v7 on v6

--- a/solution.py
+++ b/solution.py
@@ -24,6 +24,7 @@
 BLOCK = 64
 SENT_HEADS = HEADS // Z_LO
 SENT = SENT_HEADS * ROWS
+SERVED = 8
 MORE = 8
 CAP = 2
 FF = 192
@@ -145,64 +146,72 @@
         part = part.astype(BF16)
         for h in range(2):
             for i in range(Z_LO):
-                first = (h * Z_LO + i) * BLOCK
-                out[i, pl.ds(th * 2 + (parity ^ h), 1), :, :] = part[None, first : first + BLOCK, :]
-
-
-def reduce_kernel(parts, own, out):
+                groups = [part[e * ROWS : (e + 1) * ROWS, :] for e in range(8 * h + i, 8 * h + 8, 2)]
+                out[i, pl.ds(th * 2 + (parity ^ h), 1), :, :] = jnp.concatenate(groups, axis=0)[None]
+
+
+def reduce_kernel(parts, out):
     total = parts[0].astype(F32)
     for i in range(1, Z_LO * TP):
         total = total + parts[i].astype(F32)
     total = total.astype(BF16)
-    own[...] = total
     for i in range(EXPERT):
         out[i] = total
 
 
 def routing_kernel(gathered, picks, tables):
-    mine = lax.axis_index(("zhi", "zlo"))
-    extra = gathered[:, SENT : SENT + MORE, :].astype(F32)
-    route, high, low = (extra[:, n, :] for n in (4, 5, 6))
+    hi, lo = lax.axis_index("zhi"), lax.axis_index("zlo")
+    dot = lambda a, b: jnp.dot(a.astype(BF16), b, preferred_element_type=F32)
     pick_row = lax.broadcasted_iota(jnp.int32, (LANES, EXPERT * ROWS), 0) // TOPK
     row = lax.rem(lax.broadcasted_iota(jnp.int32, (LANES, EXPERT * ROWS), 1), ROWS)
     here = jnp.where(pick_row == row, 1.0, 0.0).astype(BF16)
     earlier = jnp.where(pick_row < row, 1.0, 0.0).astype(BF16)
-    hits = [jnp.where(route == (a * EXPERT + mine).astype(F32), 1.0, 0.0) for a in range(ATTN)]
+
+    extra = gathered[:, SENT : SENT + MORE, :].astype(F32)
+    order = [2 * q + i for i in range(Z_LO) for q in range(SERVED)]
+    route = jnp.concatenate([extra[e : e + 1] for e in order], axis=0)[:, 4, :]
+    hit = jnp.concatenate(
+        [jnp.where(route == (a * EXPERT + hi * Z_LO + lo).astype(F32), 1.0, 0.0) for a in range(ATTN)], axis=0
+    )
+    shape = (ATTN * EXPERT, EXPERT * ROWS)
+    j = lax.rem(lax.broadcasted_iota(jnp.int32, shape, 0), EXPERT)
+    u = lax.broadcasted_iota(jnp.int32, shape, 1) // ROWS
+    own = 2 * lax.rem(j, 8) + j // 8 == 8 * (u // 8) + 2 * lax.rem(u, 4) + lax.rem(u // 4, 2)
+    named = jnp.where(own, dot(hit, here), 0.0)
+    rank = dot(hit, earlier)
+    for s in range(CAP):
+        picks[s] = jnp.where(rank == float(s), named, 0.0).astype(BF16)
+
+    served = [gathered[pl.ds(2 * q + lo, 1), SENT : SENT + MORE, :].astype(F32) for q in range(SERVED)]
+    served = jnp.concatenate(served, axis=0)
+    route, high, low = (served[:, n, :] for n in (4, 5, 6))
+    hits = [
+        jnp.where(route == (a * EXPERT + hi * Z_LO + other).astype(F32), 1.0, 0.0)
+        for a in range(ATTN)
+        for other in range(Z_LO)
+    ]
     hit = jnp.concatenate(hits, axis=0)
     hit_high = jnp.concatenate([m * high for m in hits], axis=0)
     hit_low = jnp.concatenate([m * low for m in hits], axis=0)
-    shape = (ATTN * EXPERT, EXPERT * ROWS)
-    own = lax.rem(lax.broadcasted_iota(jnp.int32, shape, 0), EXPERT) == (
+    shape = (ATTN * Z_LO * SERVED, SERVED * ROWS)
+    own = lax.rem(lax.broadcasted_iota(jnp.int32, shape, 0), SERVED) == (
         lax.broadcasted_iota(jnp.int32, shape, 1) // ROWS
     )
-    dot = lambda a, b: jnp.dot(a.astype(BF16), b, preferred_element_type=F32)
+    here, earlier = here[:, : SERVED * ROWS], earlier[:, : SERVED * ROWS]
     named = jnp.where(own, dot(hit, here), 0.0)
     rank = dot(hit, earlier)
-    weight_high = dot(hit_high, here)
-    weight_low = dot(hit_low, here)
     chosen = [jnp.where(rank == float(s), named, 0.0) for s in range(CAP)]
-    half = EXPERT * ROWS // 2
-    for s in range(CAP):
-        whole = chosen[s].reshape(ATTN, EXPERT, EXPERT * ROWS)
-        for h in range(2):
-            pick = whole[:, h * (EXPERT // 2) : (h + 1) * (EXPERT // 2), h * half : (h + 1) * half]
-            picks[s, h] = pick.reshape(half // 2, half).astype(BF16)
-    for n, weight in enumerate((weight_high, weight_low)):
+    for n, weight in enumerate((dot(hit_high, here), dot(hit_low, here))):
         tables[n] = jnp.transpose(jnp.concatenate([c * weight for c in chosen], axis=0)).astype(BF16)
 
 
 def select_kernel(picks, hidden, out):
     tl = lax.rem(lax.axis_index("tp"), 2)
-    half = EXPERT * ROWS // 2
-    groups = EXPERT // 2
     for k in range(CHUNKS):
-        blocks = [hidden[pl.ds((2 * k + (tl ^ h)) * Z_LO, Z_LO)].reshape(half, LANES) for h in range(2)]
+        rows = [hidden[pl.ds((2 * k + (tl ^ h)) * Z_LO, Z_LO)].reshape(Z_LO * BLOCK, LANES) for h in range(2)]
+        rows = jnp.concatenate(rows, axis=0)
         for s in range(CAP):
-            sent = [
-                jnp.dot(picks[s, h], blocks[h], preferred_element_type=F32).reshape(ATTN, groups, LANES)
-                for h in range(2)
-            ]
-            sent = jnp.concatenate(sent, axis=1).astype(BF16)
+            sent = jnp.dot(picks[s], rows, preferred_element_type=F32).astype(BF16).reshape(ATTN, EXPERT, LANES)
             for t in range(s, TP, CAP):
                 out[:, t, :, k * LANES : (k + 1) * LANES] = sent
 
@@ -212,7 +221,7 @@
 ):
     slots = ATTN * EXPERT
     square = jnp.zeros((slots, LANES), F32)
-    early = lax.rem(lax.broadcasted_iota(jnp.int32, (slots, LANES), 0), EXPERT) < EXPERT // 2
+    early = lax.rem(lax.broadcasted_iota(jnp.int32, (slots, LANES), 0), SERVED) < SERVED // 2
     for k in range(CHUNKS):
         pieces = [
             tokens[:, t, :, k * LANES : (k + 1) * LANES].reshape(slots, LANES).astype(F32) for t in range(TP)
@@ -238,24 +247,28 @@
         piece = lambda p, th: part[:, (2 * p + th) * LANES : (2 * p + th + 1) * LANES]
         for th in range(2):
             for tl in range(2):
-                block = jnp.where(early, piece(tl, th), piece(1 - tl, th)).astype(BF16)
-                out[:, 2 * th + tl, :, k * LANES : (k + 1) * LANES] = block.reshape(ATTN, EXPERT, LANES)
-
-
-def combine_kernel(parts, tables, own, out, total, laid):
-    mixed = jnp.zeros((EXPERT * ROWS, QUARTER), F32)
+                block = jnp.where(early, piece(tl, th), piece(1 - tl, th)).reshape(ATTN, Z_LO, SERVED, LANES)
+                out[:, :, 2 * th + tl, :, k * LANES : (k + 1) * LANES] = block.astype(BF16)
+
+
+def combine_kernel(parts, tables, spread, out, total, laid, own, sem):
+    fetch = pltpu.make_async_copy(spread.at[0], own, sem)
+    fetch.start()
+    mixed = jnp.zeros((SERVED * ROWS, QUARTER), F32)
     for t in range(0, TP, CAP):
-        block = jnp.concatenate([parts[:, t + s].reshape(ATTN * EXPERT, QUARTER) for s in range(CAP)], axis=0)
+        block = [parts[:, :, t + s].astype(F32).reshape(ATTN * Z_LO * SERVED, QUARTER).astype(BF16) for s in range(CAP)]
+        block = jnp.concatenate(block, axis=0)
         for n in range(2):
             mixed = mixed + jnp.dot(tables[n], block, preferred_element_type=F32)
     for k in range(CHUNKS):
         total[k] = mixed[:, k * LANES : (k + 1) * LANES]
-    hi, lo, tp = (lax.axis_index(n) for n in ("zhi", "zlo", "tp"))
+    hi, tp = lax.axis_index("zhi"), lax.axis_index("tp")
     h = lax.rem(tp, 2) ^ lax.rem(hi, 2)
-    rows = pl.ds(pl.multiple_of((h * Z_LO + lo) * BLOCK, BLOCK), BLOCK)
+    rows = pl.ds(pl.multiple_of(h * BLOCK, BLOCK), BLOCK)
     k = lax.div(hi, 2)
+    fetch.wait()
     total[k, rows, :] = total[k, rows, :] + own[...].astype(F32)
-    for n in range(EXPERT * TP):
+    for n in range(Z_HI * TP):
         for k in range(CHUNKS):
             laid[n, k * 4 : (k + 1) * 4, :] = total[k, n * 4 : (n + 1) * 4, :]
     out[...] = laid[...].astype(BF16)
@@ -265,7 +278,7 @@
     totals = []
     for t in range(TP):
         total = parts[t].astype(F32)
-        for e in range(1, EXPERT):
+        for e in range(1, Z_HI):
             total = total + parts[e * TP + t].astype(F32)
         totals.append(total)
     h = lax.div(lax.axis_index("zhi"), Z_HI // 2)
@@ -340,13 +353,13 @@
     )
     parts, ups, gates = lax.optimization_barrier((parts, taken[1], taken[0]))
     parts = exchange(parts.reshape(Z_LO * TP, BLOCK, LANES), ("zlo", "tp"))
-    own, spread = call(reduce_kernel, [((BLOCK, LANES), BF16), ((EXPERT, BLOCK, LANES), BF16)], [VMEM])(parts)
+    spread = call(reduce_kernel, [((EXPERT, BLOCK, LANES), BF16)], [VMEM])(parts)
     hidden = exchange(spread, z)
     picks, tables = call(
         routing_kernel,
         [
-            ((CAP, 2, ATTN * EXPERT // 2, EXPERT * ROWS // 2), BF16),
-            ((2, EXPERT * ROWS, CAP * ATTN * EXPERT), BF16),
+            ((CAP, ATTN * EXPERT, EXPERT * ROWS), BF16),
+            ((2, SERVED * ROWS, CAP * ATTN * Z_LO * SERVED), BF16),
         ],
         [VMEM],
     )(gathered)
@@ -355,18 +368,23 @@
     incoming = exchange(outgoing.reshape(ATTN * TP, EXPERT, QUARTER), ("attn", "tp"))
     produced = call(
         expert_kernel,
-        [((ATTN, TP, EXPERT, QUARTER), BF16)],
+        [((ATTN, Z_LO, TP, SERVED, QUARTER), BF16)],
         [VMEM] * 11,
         [pltpu.VMEM((ATTN * EXPERT, D), F32), pltpu.VMEM((ATTN * EXPERT, D), BF16)],
     )(incoming.reshape(ATTN, TP, EXPERT, QUARTER), norm_gain.reshape(1, D), *own_part, *gates, *ups, *downs)
-    returned = exchange(produced.reshape(ATTN * TP, EXPERT, QUARTER), ("attn", "tp"))
+    returned = exchange(produced.reshape(ATTN * Z_LO * TP, SERVED, QUARTER), ("attn", "zlo", "tp"))
     weighted = call(
         combine_kernel,
-        [((EXPERT * TP, ROWS, LANES), BF16)],
-        [VMEM, VMEM, VMEM],
-        [pltpu.VMEM((CHUNKS, EXPERT * ROWS, LANES), F32), pltpu.VMEM((EXPERT * TP, ROWS, LANES), F32)],
-    )(returned.reshape(ATTN, TP, EXPERT, QUARTER), tables, own)
-    back = exchange(weighted, (*z, "tp"))
+        [((Z_HI * TP, ROWS, LANES), BF16)],
+        [VMEM, VMEM, ANY],
+        [
+            pltpu.VMEM((CHUNKS, SERVED * ROWS, LANES), F32),
+            pltpu.VMEM((Z_HI * TP, ROWS, LANES), F32),
+            pltpu.VMEM((BLOCK, LANES), BF16),
+            pltpu.SemaphoreType.DMA,
+        ],
+    )(returned.reshape(ATTN, Z_LO, TP, SERVED, QUARTER), tables, spread)
+    back = exchange(weighted, ("zhi", "tp"))
     return call(finish_kernel, [((ROWS // TP, D), BF16)], [VMEM])(back)
 
 

time: 162 us -> 158 us (0.975)
  blocking collectives: 78.3 us -> 73.2 us
    all_to_all x4, blocking collectives: 78.3 us -> 73.2 us  [exchange(): return lax.all_to_all(x, axes, split_axis=0, concat_axis=0, tiled=True)]
  transfers between devices with their start and end apart: 10 -> 10, of which waited for: 3 -> 3; matrix products, arithmetic and copies ran while one was open for 2% -> 2% of each run, Pallas kernels for 3% -> 4%
where the time goes in v7:
time: 158 us; the launch traced here: 156 us
  blocking collectives  73.2 us (46%)
  starting transfers between devices  47.2 us (30%)
  waiting for transfers between devices  20.4 us (13%)
  Pallas kernels  10.7 us (7%)
  local copies, waits for them, and re-layouts  3.79 us (2%)
    all_to_all x4, blocking collectives, exchange(): return lax.all_to_all(x, axes, split_axis=0, concat_axis=0, tiled=True)  73.2 us
    all_to_all x2, starting transfers between devices, exchange(): return lax.all_to_all(x, axes, split_axis=0, concat_axis=0, tiled=True)  20.4 us
    all_to_all x2, waiting for transfers between devices, exchange(): return lax.all_to_all(x, axes, split_axis=0, concat_axis=0, tiled=True)  19.1 us
    ppermute x3, starting transfers between devices, shards(): lax.ppermute(w[:FF // 2], 'tp', ring[-1])  13.2 us
    ppermute x3, starting transfers between devices, shards(): lax.ppermute(w[FF // 2:], 'tp', ring[1])  7.97 us
    pallas_call x1, Pallas kernels, shards(): call(attention_kernel, [((EXPERT, SENT + MORE, LANES), BF16)], [SMEM] + [...  4.25 us
    ppermute x1, starting transfers between devices, shards(): lax.ppermute(lax.dynamic_index_in_dim(quarters, mine, 0, keepdims=False),...  3.83 us
  transfers between devices with their start and end apart: 10, of which 3 were waited for; matrix products, arithmetic and copies ran while one was open for 2% of the time, Pallas kernels for 4%

profile of v7, /device:TPU:24, one launch (start us, length us, event | category | flops | bytes accessed | tf_op | source)
XLA Modules:
  0.0 155.6 jit_solution(17362969284963198412)
XLA Ops:
  0.0 0.9 dynamic-slice_bitcast_fusion
  0.9 3.8 %collective-permute-start = (bf16[512,128]{1,0:T(8,128)(2,1)S(1)}, bf16[512,128]{1,0:T(8,128)(2,1)S(1)}, u32[]{:S(2)}, u32[]{:S(2)}) collective-permute-start(bf16[512,128]{1,0:T(8,128)(2,1)S(1)} %dynamic-slice_bitcast_fusion), channel_id=1, source_target_pairs={{0,4},{4,0},{1,5},{5,1},{2,6},{6,2},{3,7},{7,3},{8,12},{12,8},{9,1... | collective-permute-start | bytes 393224 | tf_op jit(solution)/shard_map/ppermute | solution.py:323
  4.8 4.3 %shard_map.136 = bf16[16,136,128]{2,1,0:T(8,128)(2,1)} custom-call(s32[16]{0:T(128)} %lengths.1, bf16[16,2048]{1,0:T(8,128)(2,1)} %query_hbm.1, bf16[16,128,128]{2,1,0:T(8,128)(2,1)} %keys_hbm.1, bf16[16,128,128]{2,1,0:T(8,128)(2,1)} %values_hbm.1, bf16[16,128]{1,0:T(8,128)(2,1)} %new_keys_hbm.1, bf16[16,128]{1,0:T(8,128)(2,1)} %new_values_hbm.1, ...), custom_call_target="tpu_custom_call" | custom-call | bytes 16777216 | tf_op jit(solution)/shard_map/pallas_call | solution.py:324
  9.0 0.0 copy-start
  9.0 14.4 %all-to-all-start = ((bf16[16,136,128]{2,1,0:T(8,128)(2,1)}), bf16[16,136,128]{2,1,0:T(8,128)(2,1)S(1)}, u32[]{:S(2)}, u32[]{:S(2)}) async-start(bf16[16,136,128]{2,1,0:T(8,128)(2,1)} %shard_map.136), calls=%async_computation | async-start | bytes 1114112 | tf_op jit(solution)/shard_map/all_to_all | solution.py:294
  23.5 0.0 copy-start.1
  23.5 1.0 fusion
  24.5 3.4 %collective-permute-start.5 = (bf16[96,2048]{1,0:T(8,128)(2,1)}, bf16[96,2048]{1,0:T(8,128)(2,1)S(1)}, u32[]{:S(2)}, u32[]{:S(2)}) collective-permute-start(bf16[96,2048]{1,0:T(8,128)(2,1)} %get-tuple-element.31), channel_id=1, source_target_pairs={{0,1},{1,2},{2,3},{3,0},{4,5},{5,6},{6,7},{7,4},{8,9},{9,10},{10,1... | collective-permute-start | bytes 1179656 | tf_op jit(solution)/shard_map/ppermute | solution.py:317
  27.9 3.7 %collective-permute-start.4 = (bf16[96,2048]{1,0:T(8,128)(2,1)}, bf16[96,2048]{1,0:T(8,128)(2,1)}, u32[]{:S(2)}, u32[]{:S(2)}) collective-permute-start(bf16[96,2048]{1,0:T(8,128)(2,1)} %get-tuple-element.32), channel_id=1, source_target_pairs={{0,3},{1,0},{2,1},{3,2},{4,7},{5,4},{6,5},{7,6},{8,11},{9,8},{10,9... | collective-permute-start | bytes 1179656 | tf_op jit(solution)/shard_map/ppermute | solution.py:317
  31.5 0.0 copy-start.3
  31.5 0.9 fusion.1
  32.5 2.2 %collective-permute-start.3 = (bf16[96,2048]{1,0:T(8,128)(2,1)}, bf16[96,2048]{1,0:T(8,128)(2,1)}, u32[]{:S(2)}, u32[]{:S(2)}) collective-permute-start(bf16[96,2048]{1,0:T(8,128)(2,1)} %get-tuple-element.33), channel_id=1, source_target_pairs={{0,1},{1,2},{2,3},{3,0},{4,5},{5,6},{6,7},{7,4},{8,9},{9,10},{10,1... | collective-permute-start | bytes 1179656 | tf_op jit(solution)/shard_map/ppermute | solution.py:317
  34.7 4.9 %collective-permute-start.2 = (bf16[96,2048]{1,0:T(8,128)(2,1)}, bf16[96,2048]{1,0:T(8,128)(2,1)}, u32[]{:S(2)}, u32[]{:S(2)}) collective-permute-start(bf16[96,2048]{1,0:T(8,128)(2,1)} %get-tuple-element.34), channel_id=1, source_target_pairs={{0,3},{1,0},{2,1},{3,2},{4,7},{5,4},{6,5},{7,6},{8,11},{9,8},{10,9... | collective-permute-start | bytes 1179656 | tf_op jit(solution)/shard_map/ppermute | solution.py:317
  39.5 1.9 %collective-permute-start.1 = (bf16[512,128]{1,0:T(8,128)(2,1)S(1)}, bf16[512,128]{1,0:T(8,128)(2,1)S(1)}, u32[]{:S(2)}, u32[]{:S(2)}) collective-permute-start(bf16[512,128]{1,0:T(8,128)(2,1)S(1)} %collective-permute-done.own_lines), channel_id=1, source_target_pairs={{0,64},{64,0},{128,192},{192,128},{256,320},{320,256},{384,448},{4... | collective-permute-start | bytes 393224 | tf_op jit(solution)/shard_map/ppermute | solution.py:349
  41.5 1.3 collective-permute-done.1.other_lines
  42.8 10.3 %all-to-all-done.gathered = bf16[16,136,128]{2,1,0:T(8,128)(2,1)S(1)} async-done(((bf16[16,136,128]{2,1,0:T(8,128)(2,1)}), bf16[16,136,128]{2,1,0:T(8,128)(2,1)S(1)}, u32[]{:S(2)}, u32[]{:S(2)}) %all-to-all-start) | async-done | bytes 557088 | tf_op jit(solution)/shard_map/all_to_all | solution.py:294
  53.1 0.4 shard_map.138
  53.6 12.3 %all_to_all.30.parts = bf16[8,64,128]{2,1,0:T(8,128)(2,1)S(1)} all-to-all(bf16[8,64,128]{2,1,0:T(8,128)(2,1)S(1)} %bitcast.34), channel_id=1, replica_groups=mesh['attn'=8,'zhi'=8,'zlo'=2,'tp'=4] {'zlo','tp'}, dimensions={0} | all-to-all | bytes 262144 | tf_op jit(solution)/shard_map/all_to_all | solution.py:294
  65.9 0.7 shard_map.139.spread
  66.7 5.9 %all-to-all-start.2 = ((bf16[16,64,128]{2,1,0:T(8,128)(2,1)}), bf16[16,64,128]{2,1,0:T(8,128)(2,1)S(1)}, u32[]{:S(2)}, u32[]{:S(2)}) async-start(bf16[16,64,128]{2,1,0:T(8,128)(2,1)} %shard_map.139.spread), calls=%async_computation.2 | async-start | bytes 524288 | tf_op jit(solution)/shard_map/all_to_all | solution.py:294
  72.6 0.9 slice_bitcast_fusion
  73.5 2.4 %collective-permute-start.7 = (bf16[96,2048]{1,0:T(8,128)(2,1)}, bf16[96,2048]{1,0:T(8,128)(2,1)}, u32[]{:S(2)}, u32[]{:S(2)}) collective-permute-start(bf16[96,2048]{1,0:T(8,128)(2,1)} %get-tuple-element.29), channel_id=1, source_target_pairs={{0,1},{1,2},{2,3},{3,0},{4,5},{5,6},{6,7},{7,4},{8,9},{9,10},{10,1... | collective-permute-start | bytes 1179656 | tf_op jit(solution)/shard_map/ppermute | solution.py:317
  75.9 4.6 %collective-permute-start.6 = (bf16[96,2048]{1,0:T(8,128)(2,1)}, bf16[96,2048]{1,0:T(8,128)(2,1)}, u32[]{:S(2)}, u32[]{:S(2)}) collective-permute-start(bf16[96,2048]{1,0:T(8,128)(2,1)} %get-tuple-element.30), channel_id=1, source_target_pairs={{0,3},{1,0},{2,1},{3,2},{4,7},{5,4},{6,5},{7,6},{8,11},{9,8},{10,9... | collective-permute-start | bytes 1179656 | tf_op jit(solution)/shard_map/ppermute | solution.py:317
  80.6 0.5 shard_map.137
  81.1 8.7 %all-to-all-done.2.hidden = bf16[16,64,128]{2,1,0:T(8,128)(2,1)S(1)} async-done(((bf16[16,64,128]{2,1,0:T(8,128)(2,1)}), bf16[16,64,128]{2,1,0:T(8,128)(2,1)S(1)}, u32[]{:S(2)}, u32[]{:S(2)}) %all-to-all-start.2) | async-done | bytes 262176 | tf_op jit(solution)/shard_map/all_to_all | solution.py:294
  89.8 0.3 shard_map.140
  90.2 15.2 %all_to_all.31 = bf16[32,16,512]{2,1,0:T(8,128)(2,1)S(1)} all-to-all(bf16[32,16,512]{2,1,0:T(8,128)(2,1)S(1)} %bitcast.28), channel_id=1, replica_groups=mesh['attn'=8,'zhi'=8,'zlo'=2,'tp'=4] {'attn','tp'}, dimensions={0} | all-to-all | bytes 1048576 | tf_op jit(solution)/shard_map/all_to_all | solution.py:294
  105.4 3.1 %shard_map.141 = bf16[8,2,4,8,512]{4,3,2,1,0:T(8,128)(2,1)S(1)} custom-call(bf16[8,4,16,512]{3,2,1,0:T(8,128)(2,1)S(1)} %bitcast.30, f32[1,2048]{1,0:T(1,128)S(1)} %bitcast.35, bf16[192,2048]{1,0:T(8,128)(2,1)S(1)} %bitcast.24, bf16[192,2048]{1,0:T(8,128)(2,1)S(1)} %bitcast.26, bf16[192,2048]{1,0:T(8,128)(2,1)S(1)} %bitcast.27, ...), custom_call_target="tpu_custom_call" | custom-call | bytes 4194304 | tf_op jit(solution)/shard_map/pallas_call | solution.py:369
  108.5 18.3 %all_to_all.32 = bf16[64,8,512]{2,1,0:T(8,128)(2,1)S(1)} all-to-all(bf16[64,8,512]{2,1,0:T(8,128)(2,1)S(1)} %bitcast.31), channel_id=1, replica_groups=mesh['attn'=8,'zhi'=8,'zlo'=2,'tp'=4] {'attn','zlo','tp'}, dimensions={0} | all-to-all | bytes 1048576 | tf_op jit(solution)/shard_map/all_to_all | solution.py:294
  126.7 0.8 shard_map.142
  127.5 27.4 %all_to_all.33.parts = bf16[32,16,128]{2,1,0:T(8,128)(2,1)S(1)} all-to-all(bf16[32,16,128]{2,1,0:T(8,128)(2,1)S(1)} %shard_map.142), channel_id=1, replica_groups=mesh['attn'=8,'zhi'=8,'zlo'=2,'tp'=4] {'zhi','tp'}, dimensions={0} | all-to-all | bytes 262144 | tf_op jit(solution)/shard_map/all_to_all | solution.py:294
  154.9 0.6 shard_map.143
  (18 shorter events, 0.0 us)
Async XLA Ops:
  0.9 8.1 %collective-permute-start = (bf16[512,128]{1,0:T(8,128)(2,1)S(1)}, bf16[512,128]{1,0:T(8,128)(2,1)S(1)}, u32[]{:S(2)}, u32[]{:S(2)}) collective-permute-start(bf16[512,128]{1,0:T(8,128)(2,1)S(1)} %dynamic-slice_bitcast_fusion), channel_id=1, source_target_pairs={{0,4},{4,0},{1,5},{5,1},{2,6},{6,2},{3,7},{7,3},{8,12},{12,8},{9,1... | collective-permute-start | bytes 393224 | tf_op jit(solution)/shard_map/ppermute | solution.py:323
  9.0 14.5 %copy-start = (bf16[1,2048,192]{1,2,0:T(8,128)(2,1)S(1)}, bf16[1,2048,192]{1,2,0:T(8,128)(2,1)}, u32[]{:S(2)}) copy-start(bf16[1,2048,192]{1,2,0:T(8,128)(2,1)} %param.25) | copy-start | bytes 2359300
  9.0 44.1 %all-to-all-start = ((bf16[16,136,128]{2,1,0:T(8,128)(2,1)}), bf16[16,136,128]{2,1,0:T(8,128)(2,1)S(1)}, u32[]{:S(2)}, u32[]{:S(2)}) async-start(bf16[16,136,128]{2,1,0:T(8,128)(2,1)} %shard_map.136), calls=%async_computation | async-start | bytes 1114112 | tf_op jit(solution)/shard_map/all_to_all | solution.py:294
  23.5 8.0 %copy-start.1 = (bf16[1,2048,192]{1,2,0:T(8,128)(2,1)S(1)}, bf16[1,2048,192]{1,2,0:T(8,128)(2,1)}, u32[]{:S(2)}) copy-start(bf16[1,2048,192]{1,2,0:T(8,128)(2,1)} %param.26) | copy-start | bytes 2359300
  24.5 29.1 %collective-permute-start.5 = (bf16[96,2048]{1,0:T(8,128)(2,1)}, bf16[96,2048]{1,0:T(8,128)(2,1)S(1)}, u32[]{:S(2)}, u32[]{:S(2)}) collective-permute-start(bf16[96,2048]{1,0:T(8,128)(2,1)} %get-tuple-element.31), channel_id=1, source_target_pairs={{0,1},{1,2},{2,3},{3,0},{4,5},{5,6},{6,7},{7,4},{8,9},{9,10},{10,1... | collective-permute-start | bytes 1179656 | tf_op jit(solution)/shard_map/ppermute | solution.py:317
  27.9 25.7 %collective-permute-start.4 = (bf16[96,2048]{1,0:T(8,128)(2,1)}, bf16[96,2048]{1,0:T(8,128)(2,1)}, u32[]{:S(2)}, u32[]{:S(2)}) collective-permute-start(bf16[96,2048]{1,0:T(8,128)(2,1)} %get-tuple-element.32), channel_id=1, source_target_pairs={{0,3},{1,0},{2,1},{3,2},{4,7},{5,4},{6,5},{7,6},{8,11},{9,8},{10,9... | collective-permute-start | bytes 1179656 | tf_op jit(solution)/shard_map/ppermute | solution.py:317
  31.5 21.6 %copy-start.3 = (bf16[2048,128]{1,0:T(8,128)(2,1)S(1)}, bf16[2048,128]{1,0:T(8,128)(2,1)}, u32[]{:S(2)}) copy-start(bf16[2048,128]{1,0:T(8,128)(2,1)} %param.20) | copy-start | bytes 1572868
  32.5 21.1 %collective-permute-start.3 = (bf16[96,2048]{1,0:T(8,128)(2,1)}, bf16[96,2048]{1,0:T(8,128)(2,1)}, u32[]{:S(2)}, u32[]{:S(2)}) collective-permute-start(bf16[96,2048]{1,0:T(8,128)(2,1)} %get-tuple-element.33), channel_id=1, source_target_pairs={{0,1},{1,2},{2,3},{3,0},{4,5},{5,6},{6,7},{7,4},{8,9},{9,10},{10,1... | collective-permute-start | bytes 1179656 | tf_op jit(solution)/shard_map/ppermute | solution.py:317
  34.7 18.9 %collective-permute-start.2 = (bf16[96,2048]{1,0:T(8,128)(2,1)}, bf16[96,2048]{1,0:T(8,128)(2,1)}, u32[]{:S(2)}, u32[]{:S(2)}) collective-permute-start(bf16[96,2048]{1,0:T(8,128)(2,1)} %get-tuple-element.34), channel_id=1, source_target_pairs={{0,3},{1,0},{2,1},{3,2},{4,7},{5,4},{6,5},{7,6},{8,11},{9,8},{10,9... | collective-permute-start | bytes 1179656 | tf_op jit(solution)/shard_map/ppermute | solution.py:317
  39.5 3.2 %collective-permute-start.1 = (bf16[512,128]{1,0:T(8,128)(2,1)S(1)}, bf16[512,128]{1,0:T(8,128)(2,1)S(1)}, u32[]{:S(2)}, u32[]{:S(2)}) collective-permute-start(bf16[512,128]{1,0:T(8,128)(2,1)S(1)} %collective-permute-done.own_lines), channel_id=1, source_target_pairs={{0,64},{64,0},{128,192},{192,128},{256,320},{320,256},{384,448},{4... | collective-permute-start | bytes 393224 | tf_op jit(solution)/shard_map/ppermute | solution.py:349
  53.5 19.0 %copy-start.2 = (bf16[1,192,2048]{2,1,0:T(8,128)(2,1)S(1)}, bf16[1,192,2048]{2,1,0:T(8,128)(2,1)}, u32[]{:S(2)}) copy-start(bf16[1,192,2048]{2,1,0:T(8,128)(2,1)} %param.27) | copy-start | bytes 2359300
  53.6 13.1 %copy-start.4 = (bf16[96,2048]{1,0:T(8,128)(2,1)}, bf16[96,2048]{1,0:T(8,128)(2,1)S(1)}, u32[]{:S(2)}) copy-start(bf16[96,2048]{1,0:T(8,128)(2,1)S(1)} %collective-permute-done.5.gate_c) | copy-start | bytes 1179652
  66.7 23.2 %all-to-all-start.2 = ((bf16[16,64,128]{2,1,0:T(8,128)(2,1)}), bf16[16,64,128]{2,1,0:T(8,128)(2,1)S(1)}, u32[]{:S(2)}, u32[]{:S(2)}) async-start(bf16[16,64,128]{2,1,0:T(8,128)(2,1)} %shard_map.139.spread), calls=%async_computation.2 | async-start | bytes 524288 | tf_op jit(solution)/shard_map/all_to_all | solution.py:294
  73.5 16.6 %collective-permute-start.7 = (bf16[96,2048]{1,0:T(8,128)(2,1)}, bf16[96,2048]{1,0:T(8,128)(2,1)}, u32[]{:S(2)}, u32[]{:S(2)}) collective-permute-start(bf16[96,2048]{1,0:T(8,128)(2,1)} %get-tuple-element.29), channel_id=1, source_target_pairs={{0,1},{1,2},{2,3},{3,0},{4,5},{5,6},{6,7},{7,4},{8,9},{9,10},{10,1... | collective-permute-start | bytes 1179656 | tf_op jit(solution)/shard_map/ppermute | solution.py:317
  75.9 14.2 %collective-permute-start.6 = (bf16[96,2048]{1,0:T(8,128)(2,1)}, bf16[96,2048]{1,0:T(8,128)(2,1)}, u32[]{:S(2)}, u32[]{:S(2)}) collective-permute-start(bf16[96,2048]{1,0:T(8,128)(2,1)} %get-tuple-element.30), channel_id=1, source_target_pairs={{0,3},{1,0},{2,1},{3,2},{4,7},{5,4},{6,5},{7,6},{8,11},{9,8},{10,9... | collective-permute-start | bytes 1179656 | tf_op jit(solution)/shard_map/ppermute | solution.py:317
  90.2 15.2 %copy-start.5 = (bf16[96,2048]{1,0:T(8,128)(2,1)S(1)}, bf16[96,2048]{1,0:T(8,128)(2,1)}, u32[]{:S(2)}) copy-start(bf16[96,2048]{1,0:T(8,128)(2,1)} %copy-done.4) | copy-start | bytes 1179652
  90.2 15.2 %copy-start.6 = (f32[2048]{0:T(1024)S(1)}, f32[2048]{0:T(1024)}, u32[]{:S(2)}) copy-start(f32[2048]{0:T(1024)} %param.22) | copy-start | bytes 24580

commit v8 on v7

--- a/solution.py
+++ b/solution.py
@@ -313,9 +313,9 @@
     z = ("zhi", "zlo")
     own_part = (w_gate[0].T, w_up[0].T, w_down[0])
     ring = {d: [(i, (i + d) % TP) for i in range(TP)] for d in (1, -1)}
-    taken = [
-        (lax.ppermute(w[: FF // 2], "tp", ring[-1]), lax.ppermute(w[FF // 2 :], "tp", ring[1])) for w in own_part
-    ]
+    halves_of = lambda w: (w[: FF // 2], w[FF // 2 :])
+    take = lambda pair: (lax.ppermute(pair[0], "tp", ring[-1]), lax.ppermute(pair[1], "tp", ring[1]))
+    gates, ups = take(halves_of(own_part[0])), take(halves_of(own_part[1]))
     halves = out_weight.reshape(Z_LO, D // Z_LO, LANES)
     quarters = out_weight.reshape(2 * Z_LO, D // Z_LO // 2, LANES)
     core = lax.rem(lax.axis_index("attn"), 2)
@@ -351,7 +351,7 @@
     parts = call(project_kernel, [((Z_LO, TP, BLOCK, LANES), BF16)], [VMEM] * 4, [pltpu.VMEM((2, D // Z_LO // 2, LANES), BF16)])(
         gathered, halves, own_lines, other_lines
     )
-    parts, ups, gates = lax.optimization_barrier((parts, taken[1], taken[0]))
+    parts, ups, gates, down_halves = lax.optimization_barrier((parts, ups, gates, halves_of(own_part[2])))
     parts = exchange(parts.reshape(Z_LO * TP, BLOCK, LANES), ("zlo", "tp"))
     spread = call(reduce_kernel, [((EXPERT, BLOCK, LANES), BF16)], [VMEM])(parts)
     hidden = exchange(spread, z)
@@ -364,7 +364,7 @@
         [VMEM],
     )(gathered)
     outgoing = call(select_kernel, [((ATTN, TP, EXPERT, QUARTER), BF16)], [VMEM, VMEM])(picks, hidden)
-    outgoing, downs = lax.optimization_barrier((outgoing, taken[2]))
+    outgoing, downs = lax.optimization_barrier((outgoing, take(down_halves)))
     incoming = exchange(outgoing.reshape(ATTN * TP, EXPERT, QUARTER), ("attn", "tp"))
     produced = call(
         expert_kernel,

time: 158 us -> 157 us (level)
  blocking collectives: 73.2 us -> 70.5 us
    all_to_all x4, blocking collectives: 73.2 us -> 70.5 us  [exchange(): return lax.all_to_all(x, axes, split_axis=0, concat_axis=0, tiled=True)]
where the time goes in v8:
time: 157 us; the launch traced here: 155 us
  blocking collectives  70.5 us (45%)
  starting transfers between devices  46.2 us (29%)
  waiting for transfers between devices  20.8 us (13%)
  Pallas kernels  11.8 us (8%)
  local copies, waits for them, and re-layouts  5.33 us (3%)
    all_to_all x4, blocking collectives, exchange(): return lax.all_to_all(x, axes, split_axis=0, concat_axis=0, tiled=True)  70.5 us
    all_to_all x2, starting transfers between devices, exchange(): return lax.all_to_all(x, axes, split_axis=0, concat_axis=0, tiled=True)  20.4 us
    all_to_all x2, waiting for transfers between devices, exchange(): return lax.all_to_all(x, axes, split_axis=0, concat_axis=0, tiled=True)  20.2 us
    ppermute x3, starting transfers between devices, shards(): lax.ppermute(pair[0], 'tp', ring[-1])  11.7 us
    ppermute x3, starting transfers between devices, shards(): lax.ppermute(pair[1], 'tp', ring[1])  8.39 us
    pallas_call x1, Pallas kernels, shards(): call(attention_kernel, [((EXPERT, SENT + MORE, LANES), BF16)], [SMEM] + [...  4.25 us
    ppermute x1, starting transfers between devices, shards(): lax.ppermute(lax.dynamic_index_in_dim(quarters, mine, 0, keepdims=False),...  3.83 us
    pallas_call x1, Pallas kernels, shards(): call(expert_kernel, [((ATTN, Z_LO, TP, SERVED, QUARTER), BF16)], [VMEM] *...  3.21 us
  transfers between devices with their start and end apart: 10, of which 3 were waited for; matrix products, arithmetic and copies ran while one was open for 2% of the time, Pallas kernels for 4%

profile of v8, /device:TPU:24, one launch (start us, length us, event | category | flops | bytes accessed | tf_op | source)
XLA Modules:
  0.0 154.8 jit_solution(9589658906860135614)
XLA Ops:
  0.0 0.9 dynamic-slice_bitcast_fusion
  0.9 3.8 %collective-permute-start = (bf16[512,128]{1,0:T(8,128)(2,1)S(1)}, bf16[512,128]{1,0:T(8,128)(2,1)}, u32[]{:S(2)}, u32[]{:S(2)}) collective-permute-start(bf16[512,128]{1,0:T(8,128)(2,1)S(1)} %dynamic-slice_bitcast_fusion), channel_id=1, source_target_pairs={{0,4},{4,0},{1,5},{5,1},{2,6},{6,2},{3,7},{7,3},{8,12},{12,8},{9,1... | collective-permute-start | bytes 393224 | tf_op jit(solution)/shard_map/ppermute | solution.py:323
  4.8 4.3 %shard_map.136 = bf16[16,136,128]{2,1,0:T(8,128)(2,1)} custom-call(s32[16]{0:T(128)} %lengths.1, bf16[16,2048]{1,0:T(8,128)(2,1)} %query_hbm.1, bf16[16,128,128]{2,1,0:T(8,128)(2,1)} %keys_hbm.1, bf16[16,128,128]{2,1,0:T(8,128)(2,1)} %values_hbm.1, bf16[16,128]{1,0:T(8,128)(2,1)} %new_keys_hbm.1, bf16[16,128]{1,0:T(8,128)(2,1)} %new_values_hbm.1, ...), custom_call_target="tpu_custom_call" | custom-call | bytes 16777216 | tf_op jit(solution)/shard_map/pallas_call | solution.py:324
  9.0 0.0 copy-start
  9.0 14.4 %all-to-all-start = ((bf16[16,136,128]{2,1,0:T(8,128)(2,1)}), bf16[16,136,128]{2,1,0:T(8,128)(2,1)S(1)}, u32[]{:S(2)}, u32[]{:S(2)}) async-start(bf16[16,136,128]{2,1,0:T(8,128)(2,1)} %shard_map.136), calls=%async_computation | async-start | bytes 1114112 | tf_op jit(solution)/shard_map/all_to_all | solution.py:294
  23.5 0.9 fusion
  24.4 3.4 %collective-permute-start.5 = (bf16[96,2048]{1,0:T(8,128)(2,1)}, bf16[96,2048]{1,0:T(8,128)(2,1)}, u32[]{:S(2)}, u32[]{:S(2)}) collective-permute-start(bf16[96,2048]{1,0:T(8,128)(2,1)} %get-tuple-element.35), channel_id=1, source_target_pairs={{0,1},{1,2},{2,3},{3,0},{4,5},{5,6},{6,7},{7,4},{8,9},{9,10},{10,1... | collective-permute-start | bytes 1179656 | tf_op jit(solution)/shard_map/ppermute | solution.py:317
  27.8 3.7 %collective-permute-start.4 = (bf16[96,2048]{1,0:T(8,128)(2,1)}, bf16[96,2048]{1,0:T(8,128)(2,1)}, u32[]{:S(2)}, u32[]{:S(2)}) collective-permute-start(bf16[96,2048]{1,0:T(8,128)(2,1)} %get-tuple-element.36), channel_id=1, source_target_pairs={{0,3},{1,0},{2,1},{3,2},{4,7},{5,4},{6,5},{7,6},{8,11},{9,8},{10,9... | collective-permute-start | bytes 1179656 | tf_op jit(solution)/shard_map/ppermute | solution.py:317
  31.5 1.0 fusion.1
  32.5 2.2 %collective-permute-start.3 = (bf16[96,2048]{1,0:T(8,128)(2,1)}, bf16[96,2048]{1,0:T(8,128)(2,1)}, u32[]{:S(2)}, u32[]{:S(2)}) collective-permute-start(bf16[96,2048]{1,0:T(8,128)(2,1)} %get-tuple-element.37), channel_id=1, source_target_pairs={{0,1},{1,2},{2,3},{3,0},{4,5},{5,6},{6,7},{7,4},{8,9},{9,10},{10,1... | collective-permute-start | bytes 1179656 | tf_op jit(solution)/shard_map/ppermute | solution.py:317
  34.7 5.0 %collective-permute-start.2 = (bf16[96,2048]{1,0:T(8,128)(2,1)}, bf16[96,2048]{1,0:T(8,128)(2,1)}, u32[]{:S(2)}, u32[]{:S(2)}) collective-permute-start(bf16[96,2048]{1,0:T(8,128)(2,1)} %get-tuple-element.38), channel_id=1, source_target_pairs={{0,3},{1,0},{2,1},{3,2},{4,7},{5,4},{6,5},{7,6},{8,11},{9,8},{10,9... | collective-permute-start | bytes 1179656 | tf_op jit(solution)/shard_map/ppermute | solution.py:317
  39.7 1.9 %collective-permute-start.1 = (bf16[512,128]{1,0:T(8,128)(2,1)}, bf16[512,128]{1,0:T(8,128)(2,1)S(1)}, u32[]{:S(2)}, u32[]{:S(2)}) collective-permute-start(bf16[512,128]{1,0:T(8,128)(2,1)} %collective-permute-done.own_lines), channel_id=1, source_target_pairs={{0,64},{64,0},{128,192},{192,128},{256,320},{320,256},{384,448},{4... | collective-permute-start | bytes 393224 | tf_op jit(solution)/shard_map/ppermute | solution.py:349
  41.6 0.9 slice_bitcast_fusion
  42.6 0.6 collective-permute-done.1.other_lines
  43.1 0.6 copy-done.4
  43.8 9.3 %all-to-all-done.gathered = bf16[16,136,128]{2,1,0:T(8,128)(2,1)S(1)} async-done(((bf16[16,136,128]{2,1,0:T(8,128)(2,1)}), bf16[16,136,128]{2,1,0:T(8,128)(2,1)S(1)}, u32[]{:S(2)}, u32[]{:S(2)}) %all-to-all-start) | async-done | bytes 557088 | tf_op jit(solution)/shard_map/all_to_all | solution.py:294
  53.1 0.9 copy-done.5
  54.0 1.3 shard_map.138
  55.4 12.2 %all_to_all.30.parts = bf16[8,64,128]{2,1,0:T(8,128)(2,1)S(1)} all-to-all(bf16[8,64,128]{2,1,0:T(8,128)(2,1)S(1)} %bitcast.34), channel_id=1, replica_groups=mesh['attn'=8,'zhi'=8,'zlo'=2,'tp'=4] {'zlo','tp'}, dimensions={0} | all-to-all | bytes 262144 | tf_op jit(solution)/shard_map/all_to_all | solution.py:294
  67.6 0.8 shard_map.139.spread
  68.3 5.9 %all-to-all-start.2 = ((bf16[16,64,128]{2,1,0:T(8,128)(2,1)}), bf16[16,64,128]{2,1,0:T(8,128)(2,1)S(1)}, u32[]{:S(2)}, u32[]{:S(2)}) async-start(bf16[16,64,128]{2,1,0:T(8,128)(2,1)} %shard_map.139.spread), calls=%async_computation.2 | async-start | bytes 524288 | tf_op jit(solution)/shard_map/all_to_all | solution.py:294
  74.3 3.0 %collective-permute-start.6 = (bf16[96,2048]{1,0:T(8,128)(2,1)}, bf16[96,2048]{1,0:T(8,128)(2,1)}, u32[]{:S(2)}, u32[]{:S(2)}) collective-permute-start(bf16[96,2048]{1,0:T(8,128)(2,1)} %get-tuple-element.23), channel_id=1, source_target_pairs={{0,3},{1,0},{2,1},{3,2},{4,7},{5,4},{6,5},{7,6},{8,11},{9,8},{10,9... | collective-permute-start | bytes 1179656 | tf_op jit(solution)/shard_map/ppermute | solution.py:317
  77.3 2.8 %collective-permute-start.7 = (bf16[96,2048]{1,0:T(8,128)(2,1)}, bf16[96,2048]{1,0:T(8,128)(2,1)}, u32[]{:S(2)}, u32[]{:S(2)}) collective-permute-start(bf16[96,2048]{1,0:T(8,128)(2,1)} %get-tuple-element.24), channel_id=1, source_target_pairs={{0,1},{1,2},{2,3},{3,0},{4,5},{5,6},{6,7},{7,4},{8,9},{9,10},{10,1... | collective-permute-start | bytes 1179656 | tf_op jit(solution)/shard_map/ppermute | solution.py:317
  80.1 0.5 shard_map.137
  80.6 10.9 %all-to-all-done.2.hidden = bf16[16,64,128]{2,1,0:T(8,128)(2,1)S(1)} async-done(((bf16[16,64,128]{2,1,0:T(8,128)(2,1)}), bf16[16,64,128]{2,1,0:T(8,128)(2,1)S(1)}, u32[]{:S(2)}, u32[]{:S(2)}) %all-to-all-start.2) | async-done | bytes 262176 | tf_op jit(solution)/shard_map/all_to_all | solution.py:294
  91.5 0.3 shard_map.140
  91.8 15.0 %all_to_all.31 = bf16[32,16,512]{2,1,0:T(8,128)(2,1)S(1)} all-to-all(bf16[32,16,512]{2,1,0:T(8,128)(2,1)S(1)} %bitcast.28), channel_id=1, replica_groups=mesh['attn'=8,'zhi'=8,'zlo'=2,'tp'=4] {'attn','tp'}, dimensions={0} | all-to-all | bytes 1048576 | tf_op jit(solution)/shard_map/all_to_all | solution.py:294
  106.9 3.2 %shard_map.141 = bf16[8,2,4,8,512]{4,3,2,1,0:T(8,128)(2,1)S(1)} custom-call(bf16[8,4,16,512]{3,2,1,0:T(8,128)(2,1)S(1)} %bitcast.30, f32[1,2048]{1,0:T(1,128)S(1)} %bitcast.35, bf16[192,2048]{1,0:T(8,128)(2,1)S(1)} %bitcast.24, bf16[192,2048]{1,0:T(8,128)(2,1)S(1)} %bitcast.26, bf16[192,2048]{1,0:T(8,128)(2,1)S(1)} %bitcast.27, ...), custom_call_target="tpu_custom_call" | custom-call | bytes 4194304 | tf_op jit(solution)/shard_map/pallas_call | solution.py:369
  110.1 18.3 %all_to_all.32 = bf16[64,8,512]{2,1,0:T(8,128)(2,1)S(1)} all-to-all(bf16[64,8,512]{2,1,0:T(8,128)(2,1)S(1)} %bitcast.31), channel_id=1, replica_groups=mesh['attn'=8,'zhi'=8,'zlo'=2,'tp'=4] {'attn','zlo','tp'}, dimensions={0} | all-to-all | bytes 1048576 | tf_op jit(solution)/shard_map/all_to_all | solution.py:294
  128.4 0.8 shard_map.142
  129.2 25.0 %all_to_all.33.parts = bf16[32,16,128]{2,1,0:T(8,128)(2,1)S(1)} all-to-all(bf16[32,16,128]{2,1,0:T(8,128)(2,1)S(1)} %shard_map.142), channel_id=1, replica_groups=mesh['attn'=8,'zhi'=8,'zlo'=2,'tp'=4] {'zhi','tp'}, dimensions={0} | all-to-all | bytes 262144 | tf_op jit(solution)/shard_map/all_to_all | solution.py:294
  154.2 0.6 shard_map.143
  (18 shorter events, 0.0 us)
Async XLA Ops:
  0.9 8.1 %collective-permute-start = (bf16[512,128]{1,0:T(8,128)(2,1)S(1)}, bf16[512,128]{1,0:T(8,128)(2,1)}, u32[]{:S(2)}, u32[]{:S(2)}) collective-permute-start(bf16[512,128]{1,0:T(8,128)(2,1)S(1)} %dynamic-slice_bitcast_fusion), channel_id=1, source_target_pairs={{0,4},{4,0},{1,5},{5,1},{2,6},{6,2},{3,7},{7,3},{8,12},{12,8},{9,1... | collective-permute-start | bytes 393224 | tf_op jit(solution)/shard_map/ppermute | solution.py:323
  9.0 14.5 %copy-start = (bf16[1,2048,192]{1,2,0:T(8,128)(2,1)S(1)}, bf16[1,2048,192]{1,2,0:T(8,128)(2,1)}, u32[]{:S(2)}) copy-start(bf16[1,2048,192]{1,2,0:T(8,128)(2,1)} %param.25) | copy-start | bytes 2359300
  9.0 44.1 %all-to-all-start = ((bf16[16,136,128]{2,1,0:T(8,128)(2,1)}), bf16[16,136,128]{2,1,0:T(8,128)(2,1)S(1)}, u32[]{:S(2)}, u32[]{:S(2)}) async-start(bf16[16,136,128]{2,1,0:T(8,128)(2,1)} %shard_map.136), calls=%async_computation | async-start | bytes 1114112 | tf_op jit(solution)/shard_map/all_to_all | solution.py:294
  23.5 8.0 %copy-start.1 = (bf16[1,2048,192]{1,2,0:T(8,128)(2,1)S(1)}, bf16[1,2048,192]{1,2,0:T(8,128)(2,1)}, u32[]{:S(2)}) copy-start(bf16[1,2048,192]{1,2,0:T(8,128)(2,1)} %param.26) | copy-start | bytes 2359300
  24.4 30.9 %collective-permute-start.5 = (bf16[96,2048]{1,0:T(8,128)(2,1)}, bf16[96,2048]{1,0:T(8,128)(2,1)}, u32[]{:S(2)}, u32[]{:S(2)}) collective-permute-start(bf16[96,2048]{1,0:T(8,128)(2,1)} %get-tuple-element.35), channel_id=1, source_target_pairs={{0,1},{1,2},{2,3},{3,0},{4,5},{5,6},{6,7},{7,4},{8,9},{9,10},{10,1... | collective-permute-start | bytes 1179656 | tf_op jit(solution)/shard_map/ppermute | solution.py:317
  27.8 27.5 %collective-permute-start.4 = (bf16[96,2048]{1,0:T(8,128)(2,1)}, bf16[96,2048]{1,0:T(8,128)(2,1)}, u32[]{:S(2)}, u32[]{:S(2)}) collective-permute-start(bf16[96,2048]{1,0:T(8,128)(2,1)} %get-tuple-element.36), channel_id=1, source_target_pairs={{0,3},{1,0},{2,1},{3,2},{4,7},{5,4},{6,5},{7,6},{8,11},{9,8},{10,9... | collective-permute-start | bytes 1179656 | tf_op jit(solution)/shard_map/ppermute | solution.py:317
  31.5 10.1 %copy-start.2 = (bf16[1,192,2048]{2,1,0:T(8,128)(2,1)S(1)}, bf16[1,192,2048]{2,1,0:T(8,128)(2,1)}, u32[]{:S(2)}) copy-start(bf16[1,192,2048]{2,1,0:T(8,128)(2,1)} %param.27) | copy-start | bytes 2359300
  32.5 22.9 %collective-permute-start.3 = (bf16[96,2048]{1,0:T(8,128)(2,1)}, bf16[96,2048]{1,0:T(8,128)(2,1)}, u32[]{:S(2)}, u32[]{:S(2)}) collective-permute-start(bf16[96,2048]{1,0:T(8,128)(2,1)} %get-tuple-element.37), channel_id=1, source_target_pairs={{0,1},{1,2},{2,3},{3,0},{4,5},{5,6},{6,7},{7,4},{8,9},{9,10},{10,1... | collective-permute-start | bytes 1179656 | tf_op jit(solution)/shard_map/ppermute | solution.py:317
  34.7 18.4 %copy-start.3 = (bf16[2048,128]{1,0:T(8,128)(2,1)S(1)}, bf16[2048,128]{1,0:T(8,128)(2,1)}, u32[]{:S(2)}) copy-start(bf16[2048,128]{1,0:T(8,128)(2,1)} %param.20) | copy-start | bytes 1572868
  34.7 20.7 %collective-permute-start.2 = (bf16[96,2048]{1,0:T(8,128)(2,1)}, bf16[96,2048]{1,0:T(8,128)(2,1)}, u32[]{:S(2)}, u32[]{:S(2)}) collective-permute-start(bf16[96,2048]{1,0:T(8,128)(2,1)} %get-tuple-element.38), channel_id=1, source_target_pairs={{0,3},{1,0},{2,1},{3,2},{4,7},{5,4},{6,5},{7,6},{8,11},{9,8},{10,9... | collective-permute-start | bytes 1179656 | tf_op jit(solution)/shard_map/ppermute | solution.py:317
  39.7 3.5 %collective-permute-start.1 = (bf16[512,128]{1,0:T(8,128)(2,1)}, bf16[512,128]{1,0:T(8,128)(2,1)S(1)}, u32[]{:S(2)}, u32[]{:S(2)}) collective-permute-start(bf16[512,128]{1,0:T(8,128)(2,1)} %collective-permute-done.own_lines), channel_id=1, source_target_pairs={{0,64},{64,0},{128,192},{192,128},{256,320},{320,256},{384,448},{4... | collective-permute-start | bytes 393224 | tf_op jit(solution)/shard_map/ppermute | solution.py:349
  43.1 0.6 copy-start.4
  53.1 0.9 copy-start.5
  68.3 23.1 %all-to-all-start.2 = ((bf16[16,64,128]{2,1,0:T(8,128)(2,1)}), bf16[16,64,128]{2,1,0:T(8,128)(2,1)S(1)}, u32[]{:S(2)}, u32[]{:S(2)}) async-start(bf16[16,64,128]{2,1,0:T(8,128)(2,1)} %shard_map.139.spread), calls=%async_computation.2 | async-start | bytes 524288 | tf_op jit(solution)/shard_map/all_to_all | solution.py:294
  74.3 17.5 %collective-permute-start.6 = (bf16[96,2048]{1,0:T(8,128)(2,1)}, bf16[96,2048]{1,0:T(8,128)(2,1)}, u32[]{:S(2)}, u32[]{:S(2)}) collective-permute-start(bf16[96,2048]{1,0:T(8,128)(2,1)} %get-tuple-element.23), channel_id=1, source_target_pairs={{0,3},{1,0},{2,1},{3,2},{4,7},{5,4},{6,5},{7,6},{8,11},{9,8},{10,9... | collective-permute-start | bytes 1179656 | tf_op jit(solution)/shard_map/ppermute | solution.py:317
  77.3 14.5 %collective-permute-start.7 = (bf16[96,2048]{1,0:T(8,128)(2,1)}, bf16[96,2048]{1,0:T(8,128)(2,1)}, u32[]{:S(2)}, u32[]{:S(2)}) collective-permute-start(bf16[96,2048]{1,0:T(8,128)(2,1)} %get-tuple-element.24), channel_id=1, source_target_pairs={{0,1},{1,2},{2,3},{3,0},{4,5},{5,6},{6,7},{7,4},{8,9},{9,10},{10,1... | collective-permute-start | bytes 1179656 | tf_op jit(solution)/shard_map/ppermute | solution.py:317
  91.8 15.1 %copy-start.6 = (f32[2048]{0:T(1024)S(1)}, f32[2048]{0:T(1024)}, u32[]{:S(2)}) copy-start(f32[2048]{0:T(1024)} %param.22) | copy-start | bytes 24580
